TPU v7x, 32 devices: a whole 2x2x4 slice. The times are simulated.
32 devices in a mesh: batch: 8 (over z, y), expert: 4 (over x, core).
Axes of the slice: x: 2, y: 2, z: 4, core: 2. Of those that a mesh axis runs over, the one named last changes fastest.
Arguments:
- tokens: bfloat16 [2, 16384, 512], P(None, ('batch', 'expert')), may hold values from -6 to 6
- routes: int32 [2, 16384, 3], P(None, ('batch', 'expert')), may hold values from 0 to 11, all different within a row; in each aligned block of 512 rows (0 to 511, 512 to 1023, ..., all dimensions but the last counted through in order) at most 256 rows name the same one
- lengths: int32 [2, 8, 8], P(None, 'batch'), may hold values from 1 to 1537, 2048 in all within a row
- gain_one: bfloat16 [512], replicated, may hold values from 0.5 to 1.5
- shift_one: bfloat16 [512], replicated, may hold values from -1 to 1
- router: bfloat16 [512, 12], replicated, may hold values from -0.1875 to 0.1875
- key_value: bfloat16 [512, 128], replicated, may hold values from -0.25 to 0.25
- w_query: bfloat16 [12, 512, 64], P('expert'), may hold values from -0.25 to 0.25
- w_out: bfloat16 [12, 64, 512], P('expert'), may hold values from -4 to 4
- gain_two: bfloat16 [512], replicated, may hold values from 0.5 to 1.5
- shift_two: bfloat16 [512], replicated, may hold values from -1 to 1
- w_up: bfloat16 [512, 2048], replicated, may hold values from -0.25 to 0.25
- up_bias: bfloat16 [2048], replicated, may hold values from -1 to 1
- w_down: bfloat16 [2048, 512], replicated, may hold values from -0.125 to 0.125
- down_bias: bfloat16 [512], replicated, may hold values from -1 to 1
- cotangent: bfloat16 [2, 16384, 512], P(None, ('batch', 'expert')), may hold values from -6 to 6
Outputs:
- block_out: bfloat16 [2, 16384, 512], P(None, ('batch', 'expert'))
- input_grad: float32 [2, 16384, 512], P(None, ('batch', 'expert'))
- grad_gain_one: float32 [512], replicated
- grad_shift_one: float32 [512], replicated
- grad_router: float32 [512, 12], replicated
- grad_key_value: float32 [512, 128], replicated
- grad_w_query: float32 [12, 512, 64], P('expert')
- grad_w_out: float32 [12, 64, 512], P('expert')
- grad_gain_two: float32 [512], replicated
- grad_shift_two: float32 [512], replicated
- grad_up: float32 [512, 2048], replicated
- grad_up_bias: float32 [2048], replicated
- grad_down: float32 [2048, 512], replicated
- grad_down_bias: float32 [512], replicated
Inputs may be any that keep to these rules, and one draw needn't show every extreme that they name: `routes`: each token names 3 different experts. In each aligned block of 512 rows (the tokens of one device in one micro-batch) no expert is named by more than 256 rows, a bound that some block reaches. Each row gives the lengths of the sequences of one group in order; they sum to 2048, and the longest is exactly 1537.
All inputs are finite; a program needn't handle non-finite values.
Results may differ from a plain program's by a relative error of at most 0.011.
Values may be sent and summed in bfloat16 or wider, within the bound.
No kernel may reach another device: no remote copies, remote signals or barrier semaphores. Data moves between devices by JAX's collectives and lax.ppermute only.
A program may use at most 192 MiB of HBM per device.

v0:
```python
import jax
import jax.numpy as jnp
from jax import lax
from jax.sharding import PartitionSpec as P

epsilon = 1e-05
highest = lax.Precision.HIGHEST


def layer_norm(values, gain_vector, shift_vector):
    centred = values - jnp.mean(values, axis=-1, keepdims=True)
    spread = jnp.mean(centred * centred, axis=-1, keepdims=True)
    return centred * lax.rsqrt(spread + epsilon) * gain_vector + shift_vector


def gelu_tanh(values):
    return jax.nn.gelu(values, approximate=True)


def soft_gates(chosen):
    row_peak = jnp.max(chosen, axis=-1, keepdims=True)
    powers = jnp.exp(chosen - row_peak)
    return powers / jnp.sum(powers, axis=-1, keepdims=True)


def segment_of(places, seq_ends):
    return jnp.sum((places[:, None] >= seq_ends[None, :]).astype(jnp.int32), axis=1)


def mask_scores(query_block, place_block, key_rows, key_seg, seq_ends):
    raw_scores = (
        jnp.einsum("qh,kh->qk", query_block, key_rows, preferred_element_type=jnp.float32) * 0.125
    )
    key_places = jnp.arange(key_rows.shape[0], dtype=jnp.int32)
    query_seg = segment_of(place_block, seq_ends)
    allowed = (query_seg[:, None] == key_seg[None, :]) & (
        key_places[None, :] <= place_block[:, None]
    )
    return jnp.where(allowed, raw_scores, -1e30)


def block_size():
    return 512


def attend_rows(queries, places, key_value_rows, key_seg, seq_ends):
    total_rows, head_size = queries.shape
    block_rows = block_size()
    key_rows = key_value_rows[:, :head_size]
    value_rows = key_value_rows[:, head_size:]

    def one_block(block_pair):
        query_block, place_block = block_pair
        masked = mask_scores(query_block, place_block, key_rows, key_seg, seq_ends)
        row_peak = jnp.max(masked, axis=1, keepdims=True)
        powers = jnp.exp(masked - row_peak)
        row_total = jnp.sum(powers, axis=1, keepdims=True)
        weights_soft = (powers / row_total).astype(jnp.bfloat16)
        result = jnp.dot(weights_soft, value_rows, preferred_element_type=jnp.float32)
        return (result, (row_peak + jnp.log(row_total))[:, 0])

    outputs, log_totals = lax.map(
        one_block, (queries.reshape(-1, block_rows, head_size), places.reshape(-1, block_rows))
    )
    return (outputs.reshape(total_rows, head_size), log_totals.reshape(total_rows))


def attend_back(queries, places, log_totals, grad_heads, key_value_rows, key_seg, seq_ends):
    total_rows, head_size = queries.shape
    block_rows = block_size()
    key_rows = key_value_rows[:, :head_size]
    value_rows = key_value_rows[:, head_size:]

    def one_block(carried, block_items):
        query_block, place_block, log_block, grad_block = block_items
        masked = mask_scores(query_block, place_block, key_rows, key_seg, seq_ends)
        weights_soft = jnp.exp(masked - log_block[:, None])
        grad_soft = jnp.einsum(
            "qh,kh->qk", grad_block, value_rows, preferred_element_type=jnp.float32
        )
        inner_sum = jnp.sum(weights_soft * grad_soft, axis=1, keepdims=True)
        grad_scores = (weights_soft * (grad_soft - inner_sum)).astype(jnp.bfloat16)
        grad_query = jnp.dot(grad_scores, key_rows, preferred_element_type=jnp.float32) * 0.125
        grad_keys = (
            jnp.einsum("qk,qh->kh", grad_scores, query_block, preferred_element_type=jnp.float32)
            * 0.125
        )
        grad_values = jnp.einsum(
            "qk,qh->kh",
            weights_soft.astype(jnp.bfloat16),
            grad_block,
            preferred_element_type=jnp.float32,
        )
        return (carried + jnp.concatenate([grad_keys, grad_values], axis=1), grad_query)

    zero_grads = jnp.zeros(key_value_rows.shape, jnp.float32)
    grad_kv, grad_queries = lax.scan(
        one_block,
        zero_grads,
        (
            queries.reshape(-1, block_rows, head_size),
            places.reshape(-1, block_rows),
            log_totals.reshape(-1, block_rows),
            grad_heads.reshape(-1, block_rows, head_size),
        ),
    )
    return (grad_queries.reshape(total_rows, head_size), grad_kv)


def experts_forward(
    row_data, place_data, query_weights, out_weights, key_value_rows, key_seg, seq_ends
):
    expert_count, per_expert, model_width = row_data.shape
    head_size = query_weights.shape[2]
    queries = jnp.einsum(
        "erd,edh->erh", row_data, query_weights, preferred_element_type=jnp.float32
    )
    queries = queries.astype(jnp.bfloat16).reshape(expert_count * per_expert, head_size)
    outputs, log_totals = attend_rows(
        queries, place_data.reshape(-1), key_value_rows, key_seg, seq_ends
    )
    head_out = outputs.astype(jnp.bfloat16).reshape(expert_count, per_expert, head_size)
    projected = jnp.einsum(
        "erh,ehd->erd", head_out, out_weights, preferred_element_type=jnp.float32
    ).astype(jnp.bfloat16)
    return (projected, (queries, head_out, log_totals))


def experts_back(
    row_data,
    place_data,
    query_weights,
    out_weights,
    key_value_rows,
    key_seg,
    seq_ends,
    kept_state,
    grad_rows,
):
    queries, head_out, log_totals = kept_state
    expert_count, per_expert, model_width = row_data.shape
    head_size = query_weights.shape[2]
    grad_heads = jnp.einsum(
        "erd,ehd->erh", grad_rows, out_weights, preferred_element_type=jnp.float32
    ).astype(jnp.bfloat16)
    grad_w_out = jnp.einsum("erh,erd->ehd", head_out, grad_rows, preferred_element_type=jnp.float32)
    grad_queries, grad_kv = attend_back(
        queries,
        place_data.reshape(-1),
        log_totals,
        grad_heads.reshape(-1, head_size),
        key_value_rows,
        key_seg,
        seq_ends,
    )
    grad_queries = grad_queries.astype(jnp.bfloat16).reshape(expert_count, per_expert, head_size)
    grad_w_query = jnp.einsum(
        "erd,erh->edh", row_data, grad_queries, preferred_element_type=jnp.float32
    )
    grad_inputs = jnp.einsum(
        "erh,edh->erd", grad_queries, query_weights, preferred_element_type=jnp.float32
    ).astype(jnp.bfloat16)
    return (grad_inputs, grad_w_query, grad_w_out, grad_kv)


def shards(
    tokens,
    routes,
    lengths,
    gain_one,
    shift_one,
    router,
    key_value,
    w_query,
    w_out,
    gain_two,
    shift_two,
    w_up,
    up_bias,
    w_down,
    down_bias,
    cotangent,
):
    groups = lax.axis_size("expert")
    member = lax.axis_index("expert")
    micro_count, tok_count, model_width = tokens.shape
    top_count = routes.shape[2]
    local_experts = w_query.shape[0]
    experts_all = local_experts * groups
    capacity = 2 * tok_count * top_count // experts_all
    slot_count = experts_all * capacity
    gain_one_f = gain_one.astype(jnp.float32)
    shift_one_f = shift_one.astype(jnp.float32)
    gain_two_f = gain_two.astype(jnp.float32)
    shift_two_f = shift_two.astype(jnp.float32)
    router_f = router.astype(jnp.float32)
    up_bias_f = up_bias.astype(jnp.float32)
    down_bias_f = down_bias.astype(jnp.float32)
    expert_ids = jnp.arange(experts_all, dtype=jnp.int32)
    own_places = member * tok_count + jnp.arange(tok_count, dtype=jnp.int32)
    group_places = jnp.arange(tok_count * groups, dtype=jnp.int32)
    query_weights, out_weights = (w_query, w_out)
    grad_gain_one = jnp.zeros(gain_one.shape, jnp.float32)
    grad_shift_one = jnp.zeros(shift_one.shape, jnp.float32)
    grad_router = jnp.zeros(router.shape, jnp.float32)
    grad_key_value = jnp.zeros(key_value.shape, jnp.float32)
    grad_w_query = jnp.zeros(query_weights.shape, jnp.float32)
    grad_w_out = jnp.zeros(out_weights.shape, jnp.float32)
    grad_gain_two = jnp.zeros(gain_two.shape, jnp.float32)
    grad_shift_two = jnp.zeros(shift_two.shape, jnp.float32)
    grad_up = jnp.zeros(w_up.shape, jnp.float32)
    grad_up_bias = jnp.zeros(up_bias.shape, jnp.float32)
    grad_down = jnp.zeros(w_down.shape, jnp.float32)
    grad_down_bias = jnp.zeros(down_bias.shape, jnp.float32)
    block_outs = []
    input_grads = []
    for micro_step in range(micro_count):
        own_tokens = tokens[micro_step].astype(jnp.float32)
        routes_now = routes[micro_step]
        seq_ends = jnp.cumsum(lengths[micro_step, 0])
        key_seg = segment_of(group_places, seq_ends)
        normed_b = layer_norm(own_tokens, gain_one_f, shift_one_f).astype(jnp.bfloat16)
        logits = jnp.dot(normed_b, router, preferred_element_type=jnp.float32)
        picked = routes_now[:, :, None] == expert_ids[None, None, :]
        chosen = jnp.sum(jnp.where(picked, logits[:, None, :], 0.0), axis=2)
        gate_weights = soft_gates(chosen)
        kv_local = jnp.dot(normed_b, key_value, preferred_element_type=jnp.float32).astype(
            jnp.bfloat16
        )
        kv_group = lax.all_gather(kv_local, "expert", axis=0, tiled=True)
        load_count = jnp.sum(picked.astype(jnp.int32), axis=1)
        before = jnp.cumsum(load_count, axis=0) - load_count
        slot_ids = jnp.sum(jnp.where(picked, before[:, None, :], 0), axis=2)
        flat_slots = (routes_now * capacity + slot_ids).reshape(-1)
        send_rows = (
            jnp.zeros((slot_count, model_width), jnp.bfloat16)
            .at[flat_slots]
            .set(jnp.repeat(normed_b, top_count, axis=0))
        )
        send_places = (
            jnp.zeros((slot_count,), jnp.int32)
            .at[flat_slots]
            .set(jnp.repeat(own_places, top_count))
        )
        arrived, arrived_places = (
            lax.all_to_all(
                send_rows.reshape(groups, local_experts, capacity, model_width),
                "expert",
                split_axis=0,
                concat_axis=2,
                tiled=True,
            ),
            lax.all_to_all(
                send_places.reshape(groups, local_experts, capacity),
                "expert",
                split_axis=0,
                concat_axis=2,
                tiled=True,
            ),
        )
        row_data = arrived.reshape(local_experts, groups * capacity, model_width)
        place_data = arrived_places.reshape(local_experts, groups * capacity)
        projected, kept_state = experts_forward(
            row_data, place_data, query_weights, out_weights, kv_group, key_seg, seq_ends
        )
        returned = lax.all_to_all(
            projected.reshape(1, local_experts, groups * capacity, model_width),
            "expert",
            split_axis=2,
            concat_axis=0,
            tiled=True,
        ).reshape(slot_count, model_width)
        route_out = (
            returned[flat_slots].reshape(tok_count, top_count, model_width).astype(jnp.float32)
        )
        mixed_sum = jnp.sum(gate_weights[:, :, None] * route_out, axis=1)
        hidden = own_tokens + mixed_sum
        normed_two = layer_norm(hidden, gain_two_f, shift_two_f).astype(jnp.bfloat16)
        upward = jnp.dot(normed_two, w_up, preferred_element_type=jnp.float32) + up_bias_f
        active = gelu_tanh(upward).astype(jnp.bfloat16)
        block_value = (
            hidden + jnp.dot(active, w_down, preferred_element_type=jnp.float32) + down_bias_f
        )
        block_outs.append(block_value.astype(jnp.bfloat16))
        cotan_now = cotangent[micro_step]
        cotan_f = cotan_now.astype(jnp.float32)
        grad_down_bias = grad_down_bias + jnp.sum(cotan_f, axis=0)
        grad_down = grad_down + jnp.einsum(
            "tf,td->fd", active, cotan_now, preferred_element_type=jnp.float32
        )
        grad_active = jnp.einsum("td,fd->tf", cotan_now, w_down, preferred_element_type=jnp.float32)
        unused, gelu_pull = jax.vjp(gelu_tanh, upward)
        grad_upward = gelu_pull(grad_active)[0].astype(jnp.bfloat16)
        grad_up_bias = grad_up_bias + jnp.sum(grad_upward.astype(jnp.float32), axis=0)
        grad_up = grad_up + jnp.einsum(
            "td,tf->df", normed_two, grad_upward, preferred_element_type=jnp.float32
        )
        grad_normed_two = jnp.einsum(
            "tf,df->td", grad_upward, w_up, preferred_element_type=jnp.float32
        )
        unused, second_pull = jax.vjp(layer_norm, hidden, gain_two_f, shift_two_f)
        grad_hidden, part_gain, part_shift = second_pull(grad_normed_two)
        grad_gain_two = grad_gain_two + part_gain
        grad_shift_two = grad_shift_two + part_shift
        grad_hidden = grad_hidden + cotan_f
        grad_gates = jnp.sum(grad_hidden[:, None, :] * route_out, axis=2)
        grad_chosen = gate_weights * (
            grad_gates - jnp.sum(gate_weights * grad_gates, axis=1, keepdims=True)
        )
        grad_logits = jnp.sum(jnp.where(picked, grad_chosen[:, :, None], 0.0), axis=1)
        grad_router = grad_router + jnp.einsum(
            "td,te->de", normed_b.astype(jnp.float32), grad_logits, precision=highest
        )
        grad_normed = jnp.einsum("te,de->td", grad_logits, router_f, precision=highest)
        grad_route = (gate_weights[:, :, None] * grad_hidden[:, None, :]).astype(jnp.bfloat16)
        grad_send = (
            jnp.zeros((slot_count, model_width), jnp.bfloat16)
            .at[flat_slots]
            .set(grad_route.reshape(tok_count * top_count, model_width))
        )
        grad_arrived = lax.all_to_all(
            grad_send.reshape(groups, local_experts, capacity, model_width),
            "expert",
            split_axis=0,
            concat_axis=2,
            tiled=True,
        )
        grad_inputs, part_query, part_out, grad_kv = experts_back(
            row_data,
            place_data,
            query_weights,
            out_weights,
            kv_group,
            key_seg,
            seq_ends,
            kept_state,
            grad_arrived.reshape(local_experts, groups * capacity, model_width),
        )
        grad_returned = lax.all_to_all(
            grad_inputs.reshape(1, local_experts, groups * capacity, model_width),
            "expert",
            split_axis=2,
            concat_axis=0,
            tiled=True,
        ).reshape(slot_count, model_width)
        grad_w_query = grad_w_query + part_query
        grad_w_out = grad_w_out + part_out
        grad_from_routes = (
            grad_returned[flat_slots].reshape(tok_count, top_count, model_width).astype(jnp.float32)
        )
        grad_normed = grad_normed + jnp.sum(grad_from_routes, axis=1)
        grad_kv_own = lax.psum_scatter(grad_kv, "expert", scatter_dimension=0, tiled=True).astype(
            jnp.bfloat16
        )
        grad_key_value = grad_key_value + jnp.einsum(
            "td,tc->dc", normed_b, grad_kv_own, preferred_element_type=jnp.float32
        )
        grad_normed = grad_normed + jnp.einsum(
            "tc,dc->td", grad_kv_own, key_value, preferred_element_type=jnp.float32
        )
        unused, first_pull = jax.vjp(layer_norm, own_tokens, gain_one_f, shift_one_f)
        grad_tokens, part_gain, part_shift = first_pull(grad_normed)
        grad_gain_one = grad_gain_one + part_gain
        grad_shift_one = grad_shift_one + part_shift
        input_grads.append(grad_tokens + grad_hidden)
    grad_w_query, grad_w_out = lax.psum((grad_w_query, grad_w_out), "batch")
    (
        grad_gain_one,
        grad_shift_one,
        grad_router,
        grad_key_value,
        grad_gain_two,
        grad_shift_two,
        grad_up,
        grad_up_bias,
        grad_down,
        grad_down_bias,
    ) = lax.psum(
        (
            grad_gain_one,
            grad_shift_one,
            grad_router,
            grad_key_value,
            grad_gain_two,
            grad_shift_two,
            grad_up,
            grad_up_bias,
            grad_down,
            grad_down_bias,
        ),
        ("batch", "expert"),
    )
    return (
        jnp.stack(block_outs),
        jnp.stack(input_grads),
        grad_gain_one,
        grad_shift_one,
        grad_router,
        grad_key_value,
        grad_w_query,
        grad_w_out,
        grad_gain_two,
        grad_shift_two,
        grad_up,
        grad_up_bias,
        grad_down,
        grad_down_bias,
    )


def solution(mesh):
    in_specs = (
        P(None, ("batch", "expert"), None),
        P(None, ("batch", "expert"), None),
        P(None, "batch", None),
        P(),
        P(),
        P(),
        P(),
        P("expert", None, None),
        P("expert", None, None),
        P(),
        P(),
        P(),
        P(),
        P(),
        P(),
        P(None, ("batch", "expert"), None),
    )
    out_specs = (
        P(None, ("batch", "expert"), None),
        P(None, ("batch", "expert"), None),
        P(),
        P(),
        P(),
        P(),
        P("expert", None, None),
        P("expert", None, None),
        P(),
        P(),
        P(),
        P(),
        P(),
        P(),
    )
    return jax.shard_map(shards, mesh=mesh, in_specs=in_specs, out_specs=out_specs, check_vma=False)
```

profile of v0, /device:TPU:0, one launch (start us, length us, event | category | flops | bytes accessed | tf_op | source)
XLA Modules:
  0.0 919.7 jit_solution(9918071275392244885)
XLA Ops:
  11.8 6.2 scatter_custom_fusion.2
  27.4 6.2 scatter_custom_fusion
  41.4 5.0 reshape.763
  46.4 9.9 %scatter_custom_fusion.1 = bf16[3072,512]{1,0:T(8,128)(2,1)} fusion(s32[1536]{0:T(1024)S(1)} %fusion.142, bf16[1536,512]{1,0:T(8,128)(2,1)} %reshape.763, bf16[]{:T(256)} %constant.133.clone.1), kind=kCustom, calls=%fused_computation.143 | custom fusion | bytes 3146240 | tf_op jit(solution)/shard_map/scatter | solution.py:238
  56.3 4.9 all-to-all-start.1
  64.5 5.0 reshape.779
  69.5 9.9 %scatter_custom_fusion.3 = bf16[3072,512]{1,0:T(8,128)(2,1)} fusion(s32[1536]{0:T(1024)S(1)} %fusion.143, bf16[1536,512]{1,0:T(8,128)(2,1)} %reshape.779, bf16[]{:T(256)} %constant.133.clone.1), kind=kCustom, calls=%fused_computation.141 | custom fusion | bytes 3146240 | tf_op jit(solution)/shard_map/scatter | solution.py:238
  79.4 18.8 %all-to-all-done.1 = bf16[4,3,256,512]{3,2,1,0:T(8,128)(2,1)} async-done(((bf16[4,3,256,512]{3,2,1,0:T(8,128)(2,1)}), bf16[4,3,256,512]{3,2,1,0:T(8,128)(2,1)}, u32[]{:S(2)}, u32[]{:S(2)}) %all-to-all-start.1) | async-done | bytes 3145760 | tf_op jit(solution)/shard_map/all_to_all | solution.py:246
  104.4 39.0 %all_gather.7 = bf16[2048,128]{1,0:T(8,128)(2,1)S(1)} all-gather(bf16[512,128]{1,0:T(8,128)(2,1)S(1)} %convolution_convert_fusion.4), channel_id=1, replica_groups=mesh['batch'=8,'expert'=4] {'expert'}, dimensions={0}, use_global_device_ids=true | all-gather | bytes 655360 | tf_op jit(solution)/shard_map/all_gather | solution.py:230
  144.8 7.3 all_gather.6
  170.8 30.1 %while.51 = (s32[]{:T(128)}, bf16[6,512,64]{1,2,0:T(8,128)(2,1)}, f32[6,512]{1,0:T(8,128)S(1)}, s32[6,512]{1,0:T(8,128)S(1)}, s32[8]{0:T(128)S(1)}, /*index=5*/s...) while((s32[]{:T(128)}, bf16[6,512,64]{1,2,0:T(8,128)(2,1)}, ...), condition=%wide.region_38.39_spmd, body=%wide.region_34.38_spmd.sunk | while | flops 279981056 | bytes 14721217 | solution.py:62
  207.3 4.7 copy.298
  212.0 5.3 all-to-all-start.5
  218.1 30.1 %while.50 = (s32[]{:T(128)}, bf16[6,512,64]{1,2,0:T(8,128)(2,1)}, f32[6,512]{1,0:T(8,128)S(1)}, s32[6,512]{1,0:T(8,128)S(1)}, s32[8]{0:T(128)S(1)}, /*index=5*/s...) while((s32[]{:T(128)}, bf16[6,512,64]{1,2,0:T(8,128)(2,1)}, ...), condition=%wide.region_17.18_spmd, body=%wide.region_13.17_spmd.sunk | while | flops 279981056 | bytes 14721217 | solution.py:62
  254.7 4.7 copy.284
  259.4 6.1 all-to-all-done.5
  265.5 5.1 all-to-all-start.2
  282.9 7.8 gather_fusion.1
  290.7 5.5 reshape.716
  296.2 5.7 multiply_reduce_fusion.4
  301.9 17.0 %all-to-all-done.2 = bf16[1,3,1024,512]{3,1,0,2:T(4,128)(2,1)} async-done(((bf16[1,3,1024,512]{3,1,0,2:T(4,128)(2,1)}), bf16[1,3,1024,512]{3,1,0,2:T(4,128)(2,1)}, u32[]{:S(2)}, u32[]{:S(2)}) %all-to-all-start.2) | async-done | bytes 3145760 | tf_op jit(solution)/shard_map/all_to_all | solution.py:266
  323.5 7.8 gather_fusion
  331.3 5.5 reshape.715
  336.8 4.9 multiply_reduce_fusion.5
  347.3 4.8 convert_reduce_fusion.5
  375.0 5.9 mul.525
  381.0 10.9 %scatter_custom_fusion.4 = bf16[3072,512]{1,0:T(8,128)(2,1)} fusion(s32[1536]{0:T(1024)S(1)} %fusion.142, f32[1536,512]{1,0:T(8,128)} %mul.525, f32[1536]{0:T(1024)S(1)} %div.149, bf16[]{:T(256)} %constant.133.clone.1), kind=kCustom, calls=%fused_computation.131 | custom fusion | flops 1572864 | bytes 6299650 | tf_op jit(solution)/shard_map/scatter | solution.py:319
  391.8 4.8 all-to-all-start.6
  399.4 5.9 mul.553
  405.3 10.7 %scatter_custom_fusion.5 = bf16[3072,512]{1,0:T(8,128)(2,1)} fusion(s32[1536]{0:T(1024)S(1)} %fusion.143, f32[1536,512]{1,0:T(8,128)} %mul.553, f32[1536]{0:T(1024)S(1)} %div.156, bf16[]{:T(256)} %constant.133.clone.1), kind=kCustom, calls=%fused_computation.132 | custom fusion | flops 1572864 | bytes 6299650 | tf_op jit(solution)/shard_map/scatter | solution.py:319
  447.3 68.4 %while.52 = (s32[]{:T(128)}, f32[2048,128]{0,1:T(8,128)S(1)}, bf16[6,512,64]{1,2,0:T(8,128)(2,1)}, s32[6,512]{1,0:T(8,128)S(1)}, s32[8]{0:T(128)}, /*index=5*/s3...) while((s32[]{:T(128)}, f32[2048,128]{0,1:T(8,128)S(1)}, ...), condition=%wide.region_51.52_spmd.clone, body=%wide.region_48.51_spmd.clone.sunk | while | flops 684633088 | bytes 38467840 | solution.py:97
  519.2 4.7 copy.309
  524.0 4.9 all-to-all-start.7
  537.5 69.4 %while.53 = (s32[]{:T(128)}, f32[2048,128]{0,1:T(8,128)S(1)}, bf16[6,512,64]{1,2,0:T(8,128)(2,1)}, s32[6,512]{1,0:T(8,128)}, s32[8]{0:T(128)S(1)}, /*index=5*/s3...) while((s32[]{:T(128)}, f32[2048,128]{0,1:T(8,128)S(1)}, ...), condition=%wide.region_65.66_spmd.clone, body=%wide.region_62.65_spmd.clone.sunk | while | flops 684633088 | bytes 38435044 | solution.py:97
  608.0 5.0 fusion.93
  614.6 4.7 copy.320
  623.6 5.0 all-to-all-start.9
  648.8 4.7 copy.310
  653.5 8.0 gather_fusion.2
  661.5 5.5 reshape.717
  667.0 12.1 %all-to-all-done.9 = bf16[1,3,1024,512]{3,1,0,2:T(4,128)(2,1)} async-done(((bf16[1,3,1024,512]{3,1,0,2:T(4,128)(2,1)}), bf16[1,3,1024,512]{3,1,0,2:T(4,128)(2,1)}, u32[]{:S(2)}, u32[]{:S(2)}) %all-to-all-start.9) | async-done | bytes 3145760 | tf_op jit(solution)/shard_map/all_to_all | solution.py:339
  683.8 7.8 gather_fusion.3
  691.5 5.5 reshape.718
  697.0 5.7 reduce_sum.553
  702.7 5.7 reduce_sum.567
  714.9 42.6 %all-reduce = (f32[512]{0:T(512)}, f32[512]{0:T(512)}, f32[512,12]{0,1:T(8,128)}, f32[512]{0:T(512)}, f32[512]{0:T(512)}, /*index=5*/f32[2048]{0:T(1024)}, f32[512]{0:T(512)}) all-reduce(f32[512]{0:T(512)S(1)} %add.360, f32[512]{0:T(512)S(1)} %add.361, ...), channel_id=1, replica_groups=mesh['batch'=8,'expert'=4] {'batch','expert'}, use_global_device_ids=true, to_apply=%region_72.73 | all-reduce | flops 10752 | bytes 86016 | tf_op jit(solution)/shard_map/psum | solution.py:378
  761.9 137.9 %all-reduce.6.cloned.1.call-done = (f32[512,128]{1,0:T(8,128)}, f32[512,2048]{1,0:T(8,128)}, f32[2048,512]{1,0:T(8,128)}) async-done(((f32[512,128]{1,0:T(8,128)}, f32[512,2048]{1,0:T(8,128)}, f32[2048,512]{1,0:T(8,128)}), (f32[512,128]{1,0:T(8,128)}, f32[512,2048]{1,0:T(8,128)}, f32[2048,512]{1,0:T(8,128)})) %all-reduce.6.cloned.1.call-update) | async-done | bytes 8650768 | tf_op jit(solution)/shard_map/psum | solution.py:378
  905.0 4.8 copy.410
  (719 shorter events, 400.4 us)
Async XLA Ops:
  8.0 338.6 %copy-start = (bf16[2048,512]{1,0:T(8,128)(2,1)S(1)}, bf16[2048,512]{1,0:T(8,128)(2,1)}, u32[]{:S(2)}) copy-start(bf16[2048,512]{1,0:T(8,128)(2,1)} %param.37) | copy-start | bytes 6291460
  8.0 16.2 %copy-start.1 = (bf16[2,512,512]{2,1,0:T(8,128)(2,1)S(1)}, bf16[2,512,512]{2,1,0:T(8,128)(2,1)}, u32[]{:S(2)}) copy-start(bf16[2,512,512]{2,1,0:T(8,128)(2,1)} %param.24) | copy-start | bytes 3145732
  8.0 19.3 %copy-start.123 = (bf16[512]{0:T(512)(128)(2,1)S(1)}, bf16[512]{0:T(512)(128)(2,1)}, u32[]{:S(2)}) copy-start(bf16[512]{0:T(512)(128)(2,1)} %param.27) | copy-start | bytes 3076
  8.0 19.3 %copy-start.124 = (bf16[512]{0:T(512)(128)(2,1)S(1)}, bf16[512]{0:T(512)(128)(2,1)}, u32[]{:S(2)}) copy-start(bf16[512]{0:T(512)(128)(2,1)} %param.28) | copy-start | bytes 3076
  9.0 263.6 %copy-start.66 = (s32[512,3]{0,1:T(4,128)}, s32[512,3]{0,1:T(4,128)S(1)}, u32[]{:S(2)}) copy-start(s32[512,3]{0,1:T(4,128)S(1)} %get-tuple-element.708) | copy-start | bytes 18436
  18.6 15.6 %all-to-all-start.3 = ((s32[4,3,256]{2,1,0:T(4,128)}), s32[4,3,256]{2,1,0:T(4,128)S(1)}, u32[]{:S(2)}, u32[]{:S(2)}) async-start(s32[4,3,256]{2,1,0:T(4,128)} %reshape.699), calls=%async_computation.3 | async-start | bytes 32768 | tf_op jit(solution)/shard_map/all_to_all | solution.py:253
  24.2 22.2 %copy-start.75 = (f32[512]{0:T(512)}, f32[512]{0:T(512)S(1)}, u32[]{:S(2)}) copy-start(f32[512]{0:T(512)S(1)} %get-tuple-element.709) | copy-start | bytes 6148
  24.2 22.1 %copy-start.78 = (f32[512]{0:T(512)}, f32[512]{0:T(512)S(1)}, u32[]{:S(2)}) copy-start(f32[512]{0:T(512)S(1)} %get-tuple-element.710) | copy-start | bytes 6148
  24.8 21.6 %copy-start.92 = (f32[512]{0:T(512)}, f32[512]{0:T(512)S(1)}, u32[]{:S(2)}) copy-start(f32[512]{0:T(512)S(1)} %fusion.148) | copy-start | bytes 6148
  24.8 21.6 %copy-start.95 = (f32[512]{0:T(512)}, f32[512]{0:T(512)S(1)}, u32[]{:S(2)}) copy-start(f32[512]{0:T(512)S(1)} %fusion.150) | copy-start | bytes 6148
  27.3 19.1 %copy-start.85 = (f32[512]{0:T(512)}, f32[512]{0:T(512)S(1)}, u32[]{:S(2)}) copy-start(f32[512]{0:T(512)S(1)} %convert_element_type.223) | copy-start | bytes 6148
  34.2 22.2 %all-to-all-start = ((s32[4,3,256]{2,1,0:T(4,128)}), s32[4,3,256]{2,1,0:T(4,128)S(1)}, u32[]{:S(2)}, u32[]{:S(2)}) async-start(s32[4,3,256]{2,1,0:T(4,128)} %reshape.689), calls=%async_computation | async-start | bytes 32768 | tf_op jit(solution)/shard_map/all_to_all | solution.py:253
  46.4 14.8 %copy-start.128 = (s32[2,1,8]{2,1,0:T(1,128)S(1)}, s32[2,1,8]{2,1,0:T(1,128)}, u32[]{:S(2)}) copy-start(s32[2,1,8]{2,1,0:T(1,128)} %param.26) | copy-start | bytes 196
  56.3 41.9 %all-to-all-start.1 = ((bf16[4,3,256,512]{3,2,1,0:T(8,128)(2,1)}), bf16[4,3,256,512]{3,2,1,0:T(8,128)(2,1)}, u32[]{:S(2)}, u32[]{:S(2)}) async-start(bf16[4,3,256,512]{3,2,1,0:T(8,128)(2,1)} %bitcast.397), calls=%async_computation.1 | async-start | bytes 6291456 | tf_op jit(solution)/shard_map/all_to_all | solution.py:246
  69.5 33.5 %copy-start.51 = (bf16[512,128]{1,0:T(8,128)(2,1)S(1)}, bf16[512,128]{1,0:T(8,128)(2,1)}, u32[]{:S(2)}) copy-start(bf16[512,128]{1,0:T(8,128)(2,1)} %param.30) | copy-start | bytes 393220
  98.2 64.0 %all-to-all-start.4 = ((bf16[4,3,256,512]{3,2,1,0:T(8,128)(2,1)}), bf16[4,3,256,512]{3,2,1,0:T(8,128)(2,1)}, u32[]{:S(2)}, u32[]{:S(2)}) async-start(bf16[4,3,256,512]{3,2,1,0:T(8,128)(2,1)} %bitcast.395), calls=%async_computation.4 | async-start | bytes 6291456 | tf_op jit(solution)/shard_map/all_to_all | solution.py:246
  170.8 34.4 %copy-start.46 = (bf16[3,64,512]{2,1,0:T(8,128)(2,1)S(1)}, bf16[3,64,512]{2,1,0:T(8,128)(2,1)}, u32[]{:S(2)}) copy-start(bf16[3,64,512]{2,1,0:T(8,128)(2,1)} %param.32) | copy-start | bytes 589828
  212.0 53.5 %all-to-all-start.5 = ((bf16[1,3,1024,512]{3,1,0,2:T(4,128)(2,1)}), bf16[1,3,1024,512]{3,1,0,2:T(4,128)(2,1)}, u32[]{:S(2)}, u32[]{:S(2)}) async-start(bf16[1,3,1024,512]{3,1,0,2:T(4,128)(2,1)} %copy.298), calls=%async_computation.5 | async-start | bytes 8388608 | tf_op jit(solution)/shard_map/all_to_all | solution.py:266
  259.4 11.3 %copy-start.125 = (bf16[512]{0:T(512)(128)(2,1)S(1)}, bf16[512]{0:T(512)(128)(2,1)}, u32[]{:S(2)}) copy-start(bf16[512]{0:T(512)(128)(2,1)} %param.33) | copy-start | bytes 3076
  259.4 11.3 %copy-start.126 = (bf16[512]{0:T(512)(128)(2,1)S(1)}, bf16[512]{0:T(512)(128)(2,1)}, u32[]{:S(2)}) copy-start(bf16[512]{0:T(512)(128)(2,1)} %param.34) | copy-start | bytes 3076
  259.4 11.3 %copy-start.127 = (bf16[512]{0:T(512)(128)(2,1)S(1)}, bf16[512]{0:T(512)(128)(2,1)}, u32[]{:S(2)}) copy-start(bf16[512]{0:T(512)(128)(2,1)} %param.38) | copy-start | bytes 3076
  259.4 11.9 %copy-start.116 = (bf16[2048]{0:T(1024)(128)(2,1)S(1)}, bf16[2048]{0:T(1024)(128)(2,1)}, u32[]{:S(2)}) copy-start(bf16[2048]{0:T(1024)(128)(2,1)} %param.36) | copy-start | bytes 12292
  259.4 11.9 %copy-start.64 = (bf16[512,12]{0,1:T(8,128)(2,1)S(1)}, bf16[512,12]{0,1:T(8,128)(2,1)}, u32[]{:S(2)}) copy-start(bf16[512,12]{0,1:T(8,128)(2,1)} %param.29) | copy-start | bytes 36868
  265.5 53.3 %all-to-all-start.2 = ((bf16[1,3,1024,512]{3,1,0,2:T(4,128)(2,1)}), bf16[1,3,1024,512]{3,1,0,2:T(4,128)(2,1)}, u32[]{:S(2)}, u32[]{:S(2)}) async-start(bf16[1,3,1024,512]{3,1,0,2:T(4,128)(2,1)} %copy.284), calls=%async_computation.2 | async-start | bytes 8388608 | tf_op jit(solution)/shard_map/all_to_all | solution.py:266
  271.3 154.3 %copy-start.109 = (f32[2048]{0:T(1024)}, f32[2048]{0:T(1024)S(1)}, u32[]{:S(2)}) copy-start(f32[2048]{0:T(1024)S(1)} %convert_element_type.238) | copy-start | bytes 24580
  278.2 12.5 %copy-start.70 = (s32[2048]{0:T(1024)}, s32[2048]{0:T(1024)S(1)}, u32[]{:S(2)}) copy-start(s32[2048]{0:T(1024)S(1)} %pad_clamp_fusion) | copy-start | bytes 24580
  278.2 45.3 %copy-start.72 = (s32[2048]{0:T(1024)}, s32[2048]{0:T(1024)S(1)}, u32[]{:S(2)}) copy-start(s32[2048]{0:T(1024)S(1)} %pad_clamp_fusion.1) | copy-start | bytes 24580
  342.0 18.0 %copy-start.15 = (f32[512,512]{1,0:T(8,128)}, f32[512,512]{1,0:T(8,128)S(1)}, u32[]{:S(2)}) copy-start(f32[512,512]{1,0:T(8,128)S(1)} %get-tuple-element.683) | copy-start | bytes 3145732
  342.0 18.0 %copy-start.18 = (f32[512,512]{1,0:T(8,128)}, f32[512,512]{1,0:T(8,128)S(1)}, u32[]{:S(2)}) copy-start(f32[512,512]{1,0:T(8,128)S(1)} %get-tuple-element.665) | copy-start | bytes 3145732
  391.8 41.8 %all-to-all-start.6 = ((bf16[4,3,256,512]{3,2,1,0:T(8,128)(2,1)}), bf16[4,3,256,512]{3,2,1,0:T(8,128)(2,1)}, u32[]{:S(2)}, u32[]{:S(2)}) async-start(bf16[4,3,256,512]{3,2,1,0:T(8,128)(2,1)} %bitcast.396), calls=%async_computation.6 | async-start | bytes 6291456 | tf_op jit(solution)/shard_map/all_to_all | solution.py:321
  405.3 11.3 %copy-start.19 = (f32[512,512]{1,0:T(8,128)S(1)}, f32[512,512]{1,0:T(8,128)}, u32[]{:S(2)}) copy-start(f32[512,512]{1,0:T(8,128)} %copy-done.18) | copy-start | bytes 3145732
  433.6 90.3 %all-to-all-start.8 = ((bf16[4,3,256,512]{3,2,1,0:T(8,128)(2,1)}), bf16[4,3,256,512]{3,2,1,0:T(8,128)(2,1)}, u32[]{:S(2)}, u32[]{:S(2)}) async-start(bf16[4,3,256,512]{3,2,1,0:T(8,128)(2,1)} %bitcast.394), calls=%async_computation.9 | async-start | bytes 6291456 | tf_op jit(solution)/shard_map/all_to_all | solution.py:321
  438.3 195.5 %reduce-scatter.3.cloned.1.call-start = ((), (), s32[]{:S(2)}) async-start(), calls=%async_computation.12 | async-start | bytes 1310720 | tf_op jit(solution)/shard_map/reduce_scatter | solution.py:352
  447.3 70.9 %copy-start.48 = (bf16[3,512,64]{1,2,0:T(8,128)(2,1)S(1)}, bf16[3,512,64]{1,2,0:T(8,128)(2,1)}, u32[]{:S(2)}) copy-start(bf16[3,512,64]{1,2,0:T(8,128)(2,1)} %param.31) | copy-start | bytes 589828
  524.0 99.7 %all-to-all-start.7 = ((bf16[1,3,1024,512]{3,1,0,2:T(4,128)(2,1)}), bf16[1,3,1024,512]{3,1,0,2:T(4,128)(2,1)}, u32[]{:S(2)}, u32[]{:S(2)}) async-start(bf16[1,3,1024,512]{3,1,0,2:T(4,128)(2,1)} %copy.309), calls=%async_computation.7 | async-start | bytes 8388608 | tf_op jit(solution)/shard_map/all_to_all | solution.py:339
  528.9 108.4 %reduce-scatter.5.cloned.1.call-start = ((), (), s32[]{:S(2)}) async-start(), calls=%async_computation.13 | async-start | bytes 1310720 | tf_op jit(solution)/shard_map/reduce_scatter | solution.py:352
  537.5 70.4 %copy-start.110 = (f32[2048]{0:T(1024)S(1)}, f32[2048]{0:T(1024)}, u32[]{:S(2)}) copy-start(f32[2048]{0:T(1024)} %copy-done.109) | copy-start | bytes 24580
  537.5 70.4 %copy-start.121 = (f32[512]{0:T(512)S(1)}, f32[512]{0:T(512)}, u32[]{:S(2)}) copy-start(f32[512]{0:T(512)} %convert_element_type.240) | copy-start | bytes 6148
  623.6 55.5 %all-to-all-start.9 = ((bf16[1,3,1024,512]{3,1,0,2:T(4,128)(2,1)}), bf16[1,3,1024,512]{3,1,0,2:T(4,128)(2,1)}, u32[]{:S(2)}, u32[]{:S(2)}) async-start(bf16[1,3,1024,512]{3,1,0,2:T(4,128)(2,1)} %copy.320), calls=%async_computation.10 | async-start | bytes 8388608 | tf_op jit(solution)/shard_map/all_to_all | solution.py:339
  628.7 133.2 %all-reduce.8.cloned.1.call-start = ((), (), s32[]{:S(2)}) async-start(), calls=%async_computation.15 | async-start | bytes 1572864 | tf_op jit(solution)/shard_map/psum | solution.py:366
  632.3 267.5 %all-reduce.6.cloned.1.call-start = ((), (), s32[]{:S(2)}) async-start(), calls=%async_computation.14 | async-start | bytes 17301504 | tf_op jit(solution)/shard_map/psum | solution.py:378
  666.9 16.8 %copy-start.71 = (s32[2048]{0:T(1024)S(1)}, s32[2048]{0:T(1024)}, u32[]{:S(2)}) copy-start(s32[2048]{0:T(1024)} %copy-done.70) | copy-start | bytes 24580
  697.0 11.4 %copy-start.65 = (bf16[512,12]{0,1:T(8,128)(2,1)S(1)}, bf16[512,12]{0,1:T(8,128)(2,1)}, u32[]{:S(2)}) copy-start(bf16[512,12]{0,1:T(8,128)(2,1)} %param.29) | copy-start | bytes 36868
  712.8 44.7 %copy-start.77 = (f32[512]{0:T(512)S(1)}, f32[512]{0:T(512)}, u32[]{:S(2)}) copy-start(f32[512]{0:T(512)} %copy-done.75) | copy-start | bytes 6148
  712.8 44.7 %copy-start.80 = (f32[512]{0:T(512)S(1)}, f32[512]{0:T(512)}, u32[]{:S(2)}) copy-start(f32[512]{0:T(512)} %copy-done.78) | copy-start | bytes 6148
  712.8 44.7 %copy-start.87 = (f32[512]{0:T(512)S(1)}, f32[512]{0:T(512)}, u32[]{:S(2)}) copy-start(f32[512]{0:T(512)} %copy-done.85) | copy-start | bytes 6148
  712.8 44.7 %copy-start.94 = (f32[512]{0:T(512)S(1)}, f32[512]{0:T(512)}, u32[]{:S(2)}) copy-start(f32[512]{0:T(512)} %copy-done.92) | copy-start | bytes 6148
  712.8 44.7 %copy-start.97 = (f32[512]{0:T(512)S(1)}, f32[512]{0:T(512)}, u32[]{:S(2)}) copy-start(f32[512]{0:T(512)} %copy-done.95) | copy-start | bytes 6148
  (120 other events, 488.3 us)
Sparse Core Ops, SparseCore 0:
  516.7 32.8 reduce-scatter.2
  608.1 29.2 reduce-scatter.4
Sparse Core Ops, SparseCore 1:
  633.2 76.3 all-reduce.7
  717.3 182.5 all-reduce.5
where the time goes:
time: 933 us; the launch traced here: 920 us
  local copies, waits for them, and re-layouts  242 us (26%)
  matrix products  230 us (25%)
  waiting for transfers between devices  198 us (21%)
  other arithmetic  93.7 us (10%)
  blocking collectives  88.9 us (10%)
  starting transfers between devices  47.4 us (5%)
  between operations  17.8 us (2%)
    psum x1, waiting for transfers between devices, shards(): lax.psum((grad_gain_one, grad_shift_one, grad_router, grad_key_value, gra...  138 us
    dot_general x24, matrix products, mask_scores(): jnp.einsum('qh,kh->qk', query_block, key_rows, preferred_element_type=jnp...  65.2 us
    all_gather x2, blocking collectives, shards(): kv_group = lax.all_gather(kv_local, 'expert', axis=0, tiled=True)  46.3 us
    psum x1, blocking collectives, shards(): lax.psum((grad_gain_one, grad_shift_one, grad_router, grad_key_value, gra...  42.6 us
    unnamed x259, local copies, waits for them, and re-layouts  32.4 us
    all_to_all x2, waiting for transfers between devices, shards(): lax.all_to_all(projected.reshape(1, local_experts, groups * capacity, mod...  23.1 us
    dot_general x12, matrix products, one_block(): jnp.einsum('qh,kh->qk', grad_block, value_rows, preferred_element_type=jn...  21.8 us
    scatter x2, other arithmetic, shards(): grad_send = jnp.zeros((slot_count, model_width), jnp.bfloat16).at[flat_sl...  21.5 us
  transfers between devices with their start and end apart: 14, of which 7 were waited for; matrix products, arithmetic and copies ran while one was open for 45% of the time, Pallas kernels for 0%

commit v1 on v0

v1 whole, which is shorter than its diff:
```python
import functools

import jax
import jax.numpy as jnp
from jax import lax
from jax.experimental import pallas as pl
from jax.experimental.pallas import tpu as pltpu
from jax.sharding import PartitionSpec as P

epsilon = 1e-05
b16 = jnp.bfloat16
f32 = jnp.float32
LOW = -1e30
LIMIT = 56 * 1024 * 1024


def dot(left, right, over=((1,), (0,))):
    return lax.dot_general(left, right, (over, ((), ())), preferred_element_type=f32)


def log2(size):
    return size.bit_length() - 1


def flip(values, axis, bit):
    size = lax.axis_size(axis)
    return lax.ppermute(values, axis, [(i, i ^ (1 << bit)) for i in range(size)])


def add(left, right):
    return (left.astype(f32) + right.astype(f32)).astype(b16)


def normalize(values):
    centred = values - jnp.mean(values, axis=-1, keepdims=True)
    spread = lax.rsqrt(jnp.mean(centred * centred, axis=-1, keepdims=True) + epsilon)
    return centred * spread, spread


def norm_back(grad, unit, spread):
    inner = jnp.mean(grad * unit, axis=-1, keepdims=True)
    return spread * (grad - jnp.mean(grad, axis=-1, keepdims=True) - unit * inner)


def first_kernel(tokens, routes, gain, shift, router, key_value, normed, kv, gates):
    unit, _ = normalize(tokens[0].astype(f32))
    rows = (unit * gain[...].astype(f32) + shift[...].astype(f32)).astype(b16)
    normed[0] = rows
    kv[0] = dot(rows, key_value[...]).astype(b16)
    logits = dot(router[...], rows, ((1,), (1,)))
    ids = lax.broadcasted_iota(jnp.int32, logits.shape, 0)
    top = routes.shape[1]
    chosen = [
        jnp.sum(jnp.where(ids == routes[0, k : k + 1, :], logits, 0.0), axis=0, keepdims=True)
        for k in range(top)
    ]
    peak = functools.reduce(jnp.maximum, chosen)
    powers = [jnp.exp(c - peak) for c in chosen]
    total = sum(powers)
    for k in range(top):
        gates[0, k : k + 1, :] = powers[k] / total


def bounds(lens, micro, first, count):
    place = first + lax.broadcasted_iota(jnp.int32, (1, count), 1)
    run = jnp.int32(0)
    low = jnp.int32(0)
    start = jnp.zeros((1, count), jnp.int32)
    for j in range(lens.shape[1]):
        run = run + lens[micro, j]
        start = jnp.where(place >= run, run, start)
        low = jnp.where(first >= run, run, low)
    return place, start, low


def spread_rows(pieces, ids, expert):
    out = jnp.zeros_like(pieces[0])
    for piece, row in zip(pieces, ids):
        out = jnp.where(row == expert, piece, out)
    return out


def gather_rows(table, ids, experts, head):
    out = jnp.zeros((head, table.shape[1]), f32)
    for i, expert in enumerate(experts):
        out = jnp.where(ids == expert, table[i * head : (i + 1) * head], out)
    return out


def expert_ids(meta, groups, local):
    base = 4 + groups
    return [meta[base + s] * local + l for s in range(groups) for l in range(local)]


def transpose_kv(kv, kvt, groups, tok):
    for s in range(groups):
        kvt[:, s * tok : (s + 1) * tok] = kv[s, 0].T


def masked(scores, key_base, place, start):
    keys = key_base + lax.broadcasted_iota(jnp.int32, scores.shape, 0)
    return jnp.where((keys <= place) & (keys >= start), scores, LOW)


def forward_kernel(
    dims, meta, lens, normed, tokens, routes, gates, kv, wq, wo, gain, shift,
    hidden, second, qt, ot, lse, mixt, kvt, acc,
):
    groups, tok, head, tile, block, top, local = dims
    micro = pl.program_id(0)
    me = meta[0]
    experts = expert_ids(meta, groups, local)
    transpose_kv(kv, kvt, groups, tok)
    table = dot(wq[...], normed[0], ((1,), (1,)))
    for i in range(tok // tile):
        cols = slice(i * tile, (i + 1) * tile)
        ids = [routes[0, k : k + 1, cols] for k in range(top)]
        heads = [gather_rows(table[:, cols], row, experts, head) for row in ids]
        query = jnp.concatenate(heads, axis=1).astype(b16) * jnp.asarray(0.125, b16)
        qt[0, i] = query
        padded = jnp.concatenate([query, jnp.zeros_like(query)], axis=0)
        first = me * tok + i * tile
        place, start, low = bounds(lens, micro, first, tile)
        place = jnp.concatenate([place] * top, axis=1)
        start = jnp.concatenate([start] * top, axis=1)
        acc[...] = jnp.zeros_like(acc)

        def one_block(index, carry):
            peak, total = carry
            chunk = (index * block) // tok
            row = pl.multiple_of(index * block - chunk * tok, block)
            slot = meta[4 + chunk]
            column = pl.multiple_of(slot * tok + row, block)
            scores = dot(kv[slot, 0, pl.ds(row, block), :], padded)
            scores = masked(scores, index * block, place, start)
            new_peak = jnp.maximum(peak, jnp.max(scores, axis=0, keepdims=True))
            scale = jnp.exp(peak - new_peak)
            powers = jnp.exp(scores - new_peak)
            total = total * scale + jnp.sum(powers, axis=0, keepdims=True)
            acc[...] = acc[...] * scale + dot(
                kvt[head:, pl.ds(column, block)], powers.astype(b16)
            )
            return new_peak, total

        width = top * tile
        peak, total = lax.fori_loop(
            low // block,
            (first + tile - 1) // block + 1,
            one_block,
            (jnp.full((1, width), LOW, f32), jnp.zeros((1, width), f32)),
        )
        out = acc[...] / total
        ot[0, i] = out
        lse[0, i] = peak + jnp.log(total)
        rounded = out.astype(b16).astype(f32)
        pieces = [
            rounded[:, k * tile : (k + 1) * tile] * gates[0, k : k + 1, cols] for k in range(top)
        ]
        for e, expert in enumerate(experts):
            mixt[0, e * head : (e + 1) * head, cols] = spread_rows(pieces, ids, expert).astype(b16)
        mixed = dot(mixt[0, :, cols], wo[...], ((0,), (0,)))
        rows = tokens[0, cols, :].astype(f32) + mixed
        hidden[0, cols, :] = rows
        unit, _ = normalize(rows)
        second[0, cols, :] = (unit * gain[...].astype(f32) + shift[...].astype(f32)).astype(b16)


def backward_kernel(
    dims, meta, lens, normed, gh, routes, gates, kv, qt, ot, lse, mixt, wqr, wo,
    part, dkv, wbuf, router_rows, kvt, dkv_acc, dq, gq, wq_acc, wo_acc,
):
    groups, tok, head, tile, block, top, local = dims
    micro = pl.program_id(0)
    me = meta[0]
    experts = expert_ids(meta, groups, local)
    every = len(experts) * head
    pad = gq.shape[0] - every
    transpose_kv(kv, kvt, groups, tok)
    dkv_acc[...] = jnp.zeros_like(dkv_acc)

    @pl.when(micro == 0)
    def _():
        wq_acc[...] = jnp.zeros_like(wq_acc)
        wo_acc[...] = jnp.zeros_like(wo_acc)

    grad_rows = gh[0].astype(b16)
    table = dot(wo[...], grad_rows, ((1,), (1,)))
    wo_acc[...] += dot(mixt[0], grad_rows)
    for i in range(tok // tile):
        cols = slice(i * tile, (i + 1) * tile)
        ids = [routes[0, k : k + 1, cols] for k in range(top)]
        back = [gather_rows(table[:, cols], row, experts, head) for row in ids]
        weights = [gates[0, k : k + 1, cols] for k in range(top)]
        out = ot[0, i]
        outs = [out[:, k * tile : (k + 1) * tile] for k in range(top)]
        grad_gates = [
            jnp.sum(b * o.astype(b16).astype(f32), axis=0, keepdims=True)
            for b, o in zip(back, outs)
        ]
        inner = sum(w * g for w, g in zip(weights, grad_gates))
        chosen = [w * (g - inner) for w, g in zip(weights, grad_gates)]
        names = lax.broadcasted_iota(jnp.int32, (pad, tile), 0)
        gq[every:, cols] = spread_rows(
            [jnp.broadcast_to(c, (pad, tile)) for c in chosen], ids, names
        ).astype(b16)
        grad = jnp.concatenate([w * b for w, b in zip(weights, back)], axis=1).astype(b16)
        delta = jnp.sum(grad.astype(f32) * out, axis=0, keepdims=True)
        query = qt[0, i]
        padded = jnp.concatenate([query, jnp.zeros_like(query)], axis=0)
        grad_pad = jnp.concatenate([jnp.zeros_like(grad), grad], axis=0)
        level = lse[0, i]
        first = me * tok + i * tile
        place, start, low = bounds(lens, micro, first, tile)
        place = jnp.concatenate([place] * top, axis=1)
        start = jnp.concatenate([start] * top, axis=1)
        dq[...] = jnp.zeros_like(dq)

        def one_block(index, carry):
            chunk = (index * block) // tok
            row = pl.multiple_of(index * block - chunk * tok, block)
            slot = meta[4 + chunk]
            column = pl.multiple_of(slot * tok + row, block)
            keys = kv[slot, 0, pl.ds(row, block), :]
            scores = masked(dot(keys, padded), index * block, place, start)
            soft = jnp.exp(scores - level)
            grad_scores = (soft * (dot(keys, grad_pad) - delta)).astype(b16)
            dkv_acc[pl.ds(column, block), :] += dot(grad_scores, padded, ((1,), (1,))) + dot(
                soft.astype(b16), grad_pad, ((1,), (1,))
            )
            dq[...] += dot(kvt[:head, pl.ds(column, block)], grad_scores)
            return carry

        lax.fori_loop(low // block, (first + tile - 1) // block + 1, one_block, 0)
        grad_query = dq[...] * 0.125
        pieces = [grad_query[:, k * tile : (k + 1) * tile] for k in range(top)]
        for e, expert in enumerate(experts):
            gq[e * head : (e + 1) * head, cols] = spread_rows(pieces, ids, expert).astype(b16)
    part[0] = dot(gq[...], wqr[...], ((0,), (0,)))
    wq_acc[...] += dot(gq[...], normed[0])
    for s in range(groups):
        dkv[s, 0] = dkv_acc[s * tok : (s + 1) * tok, :].astype(b16)

    @pl.when(micro == pl.num_programs(0) - 1)
    def _():
        size = local * head
        for s in range(groups):
            wbuf[s, :size] = wq_acc[s * size : (s + 1) * size, :].astype(b16)
            wbuf[s, size:] = wo_acc[s * size : (s + 1) * size, :].astype(b16)
        router_rows[...] = wq_acc[every:, :]


def ffn_kernel(
    dims, meta, hidden, second, cotan, w_up, up_bias, w_down, down_bias, gain,
    block_out, gh, own_a, own_b, snd_a, snd_b, up_row, rows,
    acc, grad_acc, act_s, gu_s,
):
    chunk, sub = dims
    step = pl.program_id(0)
    total, width = hidden.shape
    tile = w_up.shape[1]
    half = width // 2

    @pl.when(step == 0)
    def _():
        acc[...] = jnp.zeros_like(acc)
        grad_acc[...] = jnp.zeros_like(grad_acc)

    bias = up_bias[...].astype(f32)
    up_sum = jnp.zeros((1, tile), f32)
    c0 = 0.7978845608028654
    c1 = c0 * 0.044715
    for i in range(total // sub):
        at = slice(i * sub, (i + 1) * sub)
        upward = dot(second[at, :], w_up[...]) + bias
        grad = dot(cotan[at, :], w_down[...], ((1,), (1,)))
        square = upward * upward
        curve = jnp.tanh(upward * (c0 + c1 * square))
        lift = 0.5 + 0.5 * curve
        value = upward * lift
        slope = lift + value * (1.0 - curve) * (c0 + (3.0 * c1) * square)
        active = value.astype(b16)
        grad_up = (grad * slope).astype(b16)
        act_s[at, :] = active
        gu_s[at, :] = grad_up
        up_sum = up_sum + jnp.sum(grad_up.astype(f32), axis=0, keepdims=True)
        acc[at, :] += dot(active, w_down[...])
        grad_acc[at, :] += dot(grad_up, w_up[...], ((1,), (1,)))
    up_row[...] = up_sum
    grad_down = dot(act_s[...], cotan[...], ((0,), (0,))).astype(b16)
    grad_up_t = dot(gu_s[...], second[...], ((0,), (0,))).astype(b16)
    per = tile // chunk

    def place(values, left, right):
        for target, low, lanes in ((left, meta[2], slice(0, half)), (right, meta[3], slice(half, width))):
            for i in range(per):
                at = pl.multiple_of((i ^ (low & (per - 1))) * chunk, chunk)
                target[pl.ds(at, chunk), :] = values[i * chunk : (i + 1) * chunk, lanes]

    @pl.when(meta[1] == 0)
    def _():
        place(grad_down, own_a, own_b)
        place(grad_up_t, snd_a, snd_b)

    @pl.when(meta[1] != 0)
    def _():
        place(grad_up_t, own_a, own_b)
        place(grad_down, snd_a, snd_b)

    @pl.when(step == pl.num_programs(0) - 1)
    def _():
        gain_row = gain[...].astype(f32)
        sums = [jnp.zeros((1, width), f32) for _ in range(3)]
        for i in range(total // sub):
            at = slice(i * sub, (i + 1) * sub)
            rows_now = hidden[at, :]
            cot = cotan[at, :].astype(f32)
            block_out[at, :] = (rows_now + acc[at, :] + down_bias[...].astype(f32)).astype(b16)
            unit, spread = normalize(rows_now)
            grad = grad_acc[at, :]
            gh[at, :] = cot + norm_back(grad * gain_row, unit, spread)
            for j, piece in enumerate((cot, grad * unit, grad)):
                sums[j] = sums[j] + jnp.sum(piece, axis=0, keepdims=True)
        rows[...] = jnp.zeros_like(rows)
        for j in range(3):
            rows[j : j + 1, :] = sums[j]


def last_kernel(
    tokens, normed, part, kv_own, kv_got, gh, gain, key_value, up_row, rows, router_rows,
    input_grad, bundle, acc, sums,
):
    micro = pl.program_id(0)
    width = tokens.shape[2]

    @pl.when(micro == 0)
    def _():
        acc[...] = jnp.zeros_like(acc)
        sums[...] = jnp.zeros_like(sums)

    grad_kv = (kv_own[0, 0].astype(f32) + kv_got[0, 0].astype(f32)).astype(b16)
    acc[...] += dot(grad_kv, normed[0], ((0,), (0,)))
    grad = part[0] + dot(grad_kv, key_value[...], ((1,), (1,)))
    unit, spread = normalize(tokens[0].astype(f32))
    input_grad[0] = gh[0] + norm_back(grad * gain[...].astype(f32), unit, spread)
    sums[0:1, :] += jnp.sum(grad * unit, axis=0, keepdims=True)
    sums[1:2, :] += jnp.sum(grad, axis=0, keepdims=True)

    @pl.when(micro == pl.num_programs(0) - 1)
    def _():
        at = acc.shape[0]
        pad = router_rows.shape[0]
        bundle[:at, :] = acc[...].astype(b16)
        bundle[at : at + pad, :] = router_rows[...].astype(b16)
        count = up_row.shape[1] // width
        pieces = [up_row[:, i * width : (i + 1) * width] for i in range(count)]
        pieces += [rows[0:3, :], sums[0:2, :]]
        left = bundle.shape[0] - at - pad - count - 5
        pieces.append(jnp.zeros((left, width), f32))
        bundle[at + pad :, :] = jnp.concatenate(pieces, axis=0).astype(b16)


def order_kernel(chunk, meta, own_a, own_b, got_a, got_b, down, up):
    tile, half = own_a.shape
    per = tile // chunk

    def sorted_rows(left, right):
        parts = []
        for ref, low in ((left, meta[2]), (right, meta[3])):
            blocks = []
            for i in range(per):
                at = pl.multiple_of((i ^ (low & (per - 1))) * chunk, chunk)
                blocks.append(ref[pl.ds(at, chunk), :])
            parts.append(blocks[0] if per == 1 else jnp.concatenate(blocks, axis=0))
        return jnp.concatenate(parts, axis=1).astype(f32)

    own = sorted_rows(own_a, own_b)
    got = sorted_rows(got_a, got_b)

    @pl.when(meta[1] == 0)
    def _():
        down[...] = own
        up[...] = got.T

    @pl.when(meta[1] != 0)
    def _():
        down[...] = got
        up[...] = own.T


def shards(
    tokens, routes, lengths, gain_one, shift_one, router, key_value, w_query, w_out,
    gain_two, shift_two, w_up, up_bias, w_down, down_bias, cotangent,
):
    groups = lax.axis_size("expert")
    batch = lax.axis_size("batch")
    me = lax.axis_index("expert")
    mine = lax.axis_index("batch")
    micros, tok, width = tokens.shape
    top = routes.shape[2]
    local, _, head = w_query.shape
    experts = local * groups
    every = experts * head
    hidden_units = w_up.shape[1]
    group_bits, batch_bits = log2(groups), log2(batch)
    chips = groups * batch // 2
    chip_bits = log2(chips)
    chunk = hidden_units // chips
    tile, block = min(256, tok), min(256, tok)
    tiles = tok // tile
    span = top * tile
    pad = -(-experts // 16) * 16
    both = 2 * head

    x_bits = [("expert", bit) for bit in range(1, group_bits)]
    b_bits = [("batch", bit) for bit in range(batch_bits)]
    order_a = x_bits + b_bits
    order_b = b_bits[:1] + x_bits + b_bits[1:]
    shared = len(b_bits) - 1

    def place_of(order):
        total = jnp.int32(0)
        for i, (axis, bit) in enumerate(order):
            index = me if axis == "expert" else mine
            total = total | (((index >> bit) & 1) << (len(order) - 1 - i))
        return total

    high = group_bits - 1
    offsets = jnp.arange(groups, dtype=jnp.int32)
    away = offsets ^ me
    slots = (away >> 1) | ((away & 1) << high)
    devices = (((offsets << 1) & (groups - 1)) | (offsets >> high)) ^ me
    meta = jnp.concatenate(
        [jnp.stack([me, me & 1, place_of(order_a), place_of(order_b)]).astype(jnp.int32), slots, devices]
    )
    lens = lengths.reshape(micros, lengths.shape[2])

    def row(vector):
        return vector.reshape(1, -1)

    def gather(values):
        for axis, bit in x_bits + [("expert", 0)]:
            values = jnp.concatenate([values, flip(values, axis, bit)], axis=0)
        return values

    own_weights = jnp.concatenate(
        [w_query.transpose(0, 2, 1).reshape(local * head, width), w_out.reshape(local * head, width)]
    )
    all_weights = gather(own_weights[None])
    size = local * head
    wq = all_weights[:, :size].reshape(every, width)
    wo = all_weights[:, size:].reshape(every, width)
    router_t = jnp.zeros((pad, width), b16).at[:experts].set(router.T)
    routes_t = routes.transpose(0, 2, 1)

    def full(shape):
        return pl.BlockSpec(shape, lambda *a: (0,) * len(shape))

    def micro_block(*shape):
        return pl.BlockSpec((1, *shape), lambda m, *a: (m,) + (0,) * len(shape))

    def params():
        return pltpu.CompilerParams(vmem_limit_bytes=LIMIT)

    normed, kv, gates = pl.pallas_call(
        first_kernel,
        grid=(micros,),
        in_specs=[
            micro_block(tok, width), micro_block(top, tok), full((1, width)), full((1, width)),
            full((pad, width)), full((width, both)),
        ],
        out_specs=[micro_block(tok, width), micro_block(tok, both), micro_block(8, tok)],
        out_shape=[
            jax.ShapeDtypeStruct((micros, tok, width), b16),
            jax.ShapeDtypeStruct((micros, tok, both), b16),
            jax.ShapeDtypeStruct((micros, 8, tok), f32),
        ],
        compiler_params=params(),
    )(tokens, routes_t, row(gain_one), row(shift_one), router_t, key_value)

    kv_all = gather(kv[None])
    dims = (groups, tok, head, tile, block, top, local)
    kv_spec = pl.BlockSpec((groups, 1, tok, both), lambda m, *a: (0, m, 0, 0))
    state_specs = [
        micro_block(tiles, head, span), micro_block(tiles, head, span), micro_block(tiles, 1, span),
        micro_block(every, tok),
    ]
    hidden, second, qt, ot, lse, mixt = pl.pallas_call(
        functools.partial(forward_kernel, dims),
        grid_spec=pltpu.PrefetchScalarGridSpec(
            num_scalar_prefetch=2,
            grid=(micros,),
            in_specs=[
                micro_block(tok, width), micro_block(tok, width), micro_block(top, tok),
                micro_block(8, tok), kv_spec, full((every, width)), full((every, width)),
                full((1, width)), full((1, width)),
            ],
            out_specs=[micro_block(tok, width), micro_block(tok, width)] + state_specs,
            scratch_shapes=[
                pltpu.VMEM((both, groups * tok), b16),
                pltpu.VMEM((head, span), f32),
            ],
        ),
        out_shape=[
            jax.ShapeDtypeStruct((micros, tok, width), f32),
            jax.ShapeDtypeStruct((micros, tok, width), b16),
            jax.ShapeDtypeStruct((micros, tiles, head, span), b16),
            jax.ShapeDtypeStruct((micros, tiles, head, span), f32),
            jax.ShapeDtypeStruct((micros, tiles, 1, span), f32),
            jax.ShapeDtypeStruct((micros, every, tok), b16),
        ],
        compiler_params=params(),
    )(meta, lens, normed, tokens, routes_t, gates, kv_all, wq, wo, row(gain_two), row(shift_two))

    total = micros * tok
    f_tile = 256
    low_bits = log2(f_tile // chunk)
    grad_a = pl.BlockSpec((f_tile, width // 2), lambda j, meta: (j ^ (meta[2] >> low_bits), 0))
    grad_b = pl.BlockSpec((f_tile, width // 2), lambda j, meta: (j ^ (meta[3] >> low_bits), 0))
    grad_shape = jax.ShapeDtypeStruct((hidden_units, width // 2), b16)
    block_out, gh, own_a, own_b, snd_a, snd_b, up_row, ffn_rows = pl.pallas_call(
        functools.partial(ffn_kernel, (chunk, 256)),
        grid_spec=pltpu.PrefetchScalarGridSpec(
            num_scalar_prefetch=1,
            grid=(hidden_units // f_tile,),
            in_specs=[
                full((total, width)), full((total, width)), full((total, width)),
                pl.BlockSpec((width, f_tile), lambda j, meta: (0, j)),
                pl.BlockSpec((1, f_tile), lambda j, meta: (0, j)),
                pl.BlockSpec((f_tile, width), lambda j, meta: (j, 0)),
                full((1, width)), full((1, width)),
            ],
            out_specs=[
                full((total, width)), full((total, width)), grad_a, grad_b, grad_a, grad_b,
                pl.BlockSpec((1, f_tile), lambda j, meta: (0, j)), full((8, width)),
            ],
            scratch_shapes=[
                pltpu.VMEM((total, width), f32),
                pltpu.VMEM((total, width), f32),
                pltpu.VMEM((total, f_tile), b16),
                pltpu.VMEM((total, f_tile), b16),
            ],
        ),
        out_shape=[
            jax.ShapeDtypeStruct((total, width), b16),
            jax.ShapeDtypeStruct((total, width), f32),
            grad_shape, grad_shape, grad_shape, grad_shape,
            jax.ShapeDtypeStruct((1, hidden_units), f32),
            jax.ShapeDtypeStruct((8, width), f32),
        ],
        compiler_params=params(),
    )(
        meta, hidden.reshape(total, width), second.reshape(total, width),
        cotangent.reshape(total, width), w_up, row(up_bias), w_down, row(down_bias), row(gain_two),
    )
    gh = gh.reshape(micros, tok, width)

    keep_a, keep_b = own_a, own_b
    got_a, got_b = flip(snd_a, "expert", 0), flip(snd_b, "expert", 0)
    ways_a, ways_b = order_a[: len(order_a) - shared], order_b[: len(order_b) - shared]

    def halve(keep, got, way):
        count = keep.shape[0] // 2
        sent = add(keep[count:], got[count:])
        return add(keep[:count], got[:count]), flip(sent, *way)

    for way_a, way_b in zip(ways_a, ways_b):
        keep_a, got_a = halve(keep_a, got_a, way_a)
        keep_b, got_b = halve(keep_b, got_b, way_b)
    keep = jnp.concatenate([keep_a, keep_b], axis=1)
    got = jnp.concatenate([got_a, got_b], axis=1)
    for way in order_a[len(order_a) - shared :]:
        keep, got = halve(keep, got, way)
    whole = add(keep, got)
    for way in order_a[len(order_a) - shared :][::-1]:
        whole = jnp.concatenate([whole, flip(whole, *way)], axis=0)
    whole_a, whole_b = whole[:, : width // 2], whole[:, width // 2 :]
    for way_a, way_b in list(zip(ways_a, ways_b))[::-1]:
        whole_a = jnp.concatenate([whole_a, flip(whole_a, *way_a)], axis=0)
        whole_b = jnp.concatenate([whole_b, flip(whole_b, *way_b)], axis=0)
    other_a, other_b = flip(whole_a, "expert", 0), flip(whole_b, "expert", 0)

    wqr = jnp.concatenate([wq, router_t], axis=0)
    part, dkv, wbuf, router_rows = pl.pallas_call(
        functools.partial(backward_kernel, dims),
        grid_spec=pltpu.PrefetchScalarGridSpec(
            num_scalar_prefetch=2,
            grid=(micros,),
            in_specs=[
                micro_block(tok, width), micro_block(tok, width), micro_block(top, tok),
                micro_block(8, tok), kv_spec,
            ] + state_specs + [full((every + pad, width)), full((every, width))],
            out_specs=[
                micro_block(tok, width), kv_spec, full((groups, 2 * size, width)), full((pad, width)),
            ],
            scratch_shapes=[
                pltpu.VMEM((both, groups * tok), b16),
                pltpu.VMEM((groups * tok, both), f32),
                pltpu.VMEM((head, span), f32),
                pltpu.VMEM((every + pad, tok), b16),
                pltpu.VMEM((every + pad, width), f32),
                pltpu.VMEM((every, width), f32),
            ],
        ),
        out_shape=[
            jax.ShapeDtypeStruct((micros, tok, width), f32),
            jax.ShapeDtypeStruct((groups, micros, tok, both), b16),
            jax.ShapeDtypeStruct((groups, 2 * size, width), b16),
            jax.ShapeDtypeStruct((pad, width), f32),
        ],
        compiler_params=params(),
    )(meta, lens, normed, gh, routes_t, gates, kv_all, qt, ot, lse, mixt, wqr, wo)

    def scatter(values):
        count = groups // 2
        keep, sent = values[:count], values[count:]
        for i, way in enumerate([("expert", 0)] + x_bits[::-1]):
            got = flip(sent, *way)
            if count > 1:
                sent = add(keep[count // 2 :], got[count // 2 :])
                keep, got = keep[: count // 2], got[: count // 2]
                if i < len(x_bits):
                    keep = add(keep, got)
            count //= 2
        return keep, got

    kv_own, kv_got = scatter(dkv)
    rows_all = both + pad + 16
    input_grad, bundle = pl.pallas_call(
        last_kernel,
        grid=(micros,),
        in_specs=[
            micro_block(tok, width), micro_block(tok, width), micro_block(tok, width),
            pl.BlockSpec((1, 1, tok, both), lambda m: (0, m, 0, 0)),
            pl.BlockSpec((1, 1, tok, both), lambda m: (0, m, 0, 0)),
            micro_block(tok, width), full((1, width)), full((width, both)),
            full((1, hidden_units)), full((8, width)), full((pad, width)),
        ],
        out_specs=[micro_block(tok, width), full((rows_all, width))],
        out_shape=[
            jax.ShapeDtypeStruct((micros, tok, width), f32),
            jax.ShapeDtypeStruct((rows_all, width), b16),
        ],
        scratch_shapes=[pltpu.VMEM((both, width), f32), pltpu.VMEM((8, width), f32)],
        compiler_params=params(),
    )(tokens, normed, part, kv_own, kv_got, gh, row(gain_one), key_value, up_row, ffn_rows, router_rows)

    w_own, w_got = scatter(wbuf)
    w_sum = add(w_own, w_got)[0]
    for way in [("expert", 0)] + x_bits:
        bundle = add(bundle, flip(bundle, *way))
    tail = jnp.concatenate([w_sum, bundle], axis=0)
    for way in b_bits:
        tail = add(tail, flip(tail, *way))

    grad_down, grad_up = pl.pallas_call(
        functools.partial(order_kernel, chunk),
        grid_spec=pltpu.PrefetchScalarGridSpec(
            num_scalar_prefetch=1,
            grid=(hidden_units // f_tile,),
            in_specs=[grad_a, grad_b, grad_a, grad_b],
            out_specs=[
                pl.BlockSpec((f_tile, width), lambda j, meta: (j, 0)),
                pl.BlockSpec((width, f_tile), lambda j, meta: (0, j)),
            ],
        ),
        out_shape=[
            jax.ShapeDtypeStruct((hidden_units, width), f32),
            jax.ShapeDtypeStruct((width, hidden_units), f32),
        ],
        compiler_params=params(),
    )(meta, whole_a, whole_b, other_a, other_b)

    tail = tail.astype(f32)
    grad_wq = tail[:size].reshape(local, head, width).transpose(0, 2, 1)
    grad_wo = tail[size : 2 * size].reshape(local, head, width)
    at = 2 * size
    grad_key_value = tail[at : at + both].T
    grad_router = tail[at + both : at + both + experts].T
    at = at + both + pad
    count = hidden_units // width
    grad_up_bias = tail[at : at + count].reshape(hidden_units)
    at = at + count
    return (
        block_out.reshape(micros, tok, width),
        input_grad,
        tail[at + 3],
        tail[at + 4],
        grad_router,
        grad_key_value,
        grad_wq,
        grad_wo,
        tail[at + 1],
        tail[at + 2],
        grad_up,
        grad_up_bias,
        grad_down,
        tail[at],
    )


def solution(mesh):
    split = P(None, ("batch", "expert"), None)
    own = P("expert", None, None)
    in_specs = (
        split, split, P(None, "batch", None), P(), P(), P(), P(), own, own, P(), P(), P(), P(), P(),
        P(), split,
    )
    out_specs = (split, split, P(), P(), P(), P(), own, own, P(), P(), P(), P(), P(), P())
    return jax.shard_map(shards, mesh=mesh, in_specs=in_specs, out_specs=out_specs, check_vma=False)
```

time: 933 us -> 242 us (0.26); the launches traced: 920 us -> 240 us
  matrix products: 230 us -> 0 us
  local copies, waits for them, and re-layouts: 242 us -> 15.2 us
  waiting for transfers between devices: 198 us -> 80.3 us
  blocking collectives: 88.9 us -> 0 us
  other arithmetic: 93.7 us -> 8.33 us
  Pallas kernels: 0 us -> 71.4 us
  between operations: 17.8 us -> 1.04 us
  starting transfers between devices: 47.4 us -> 63.2 us
    dot_general x120 -> x0, matrix products: 230 us -> none  [the longest x24 65.2 us: mask_scores(): jnp.einsum('qh,kh->qk', query_block, key_rows, preferred_element_type=jnp...]
    psum x2 -> x0, waiting for transfers between devices: 138 us -> none  [the longest x1 138 us: shards(): lax.psum((grad_gain_one, grad_shift_one, grad_router, grad_key_value, gra...]
    ppermute x0 -> x29, waiting for transfers between devices: none -> 80.3 us  [flip(): return lax.ppermute(values, axis, [(i, i ^ 1 << bit) for i in range(size)])]
    pallas_call x0 -> x6, Pallas kernels: none -> 71.4 us  [the longest x1 27.9 us: shards(): pl.pallas_call(functools.partial(ffn_kernel, (chunk, 256)), grid_spec=plt...]
    ppermute x0 -> x29, starting transfers between devices: none -> 63.2 us  [flip(): return lax.ppermute(values, axis, [(i, i ^ 1 << bit) for i in range(size)])]
    all_to_all x10 -> x0, waiting for transfers between devices: 57.4 us -> none  [the longest x2 23.1 us: shards(): lax.all_to_all(projected.reshape(1, local_experts, groups * capacity, mod...]
    reduce_sum x64 -> x0, other arithmetic: 49.4 us -> none  [the longest x2 11.4 us: shards(): grad_normed = grad_normed + jnp.sum(grad_from_routes, axis=1)]
    all_to_all x10 -> x0, starting transfers between devices: 46.8 us -> none  [the longest x2 10.4 us: shards(): lax.all_to_all(projected.reshape(1, local_experts, groups * capacity, mod...]
  transfers between devices with their start and end apart: 14 -> 29, of which waited for: 7 -> 15; matrix products, arithmetic and copies ran while one was open for 45% -> 8% of each run, Pallas kernels for 0% -> 10%
where the time goes in v1:
time: 242 us; the launch traced here: 240 us
  waiting for transfers between devices  80.3 us (33%)
  Pallas kernels  71.4 us (30%)
  starting transfers between devices  63.2 us (26%)
  local copies, waits for them, and re-layouts  15.2 us (6%)
  other arithmetic  8.33 us (3%)
    ppermute x29, waiting for transfers between devices, flip(): return lax.ppermute(values, axis, [(i, i ^ 1 << bit) for i in range(size)])  80.3 us
    ppermute x29, starting transfers between devices, flip(): return lax.ppermute(values, axis, [(i, i ^ 1 << bit) for i in range(size)])  63.2 us
    pallas_call x1, Pallas kernels, shards(): pl.pallas_call(functools.partial(ffn_kernel, (chunk, 256)), grid_spec=plt...  27.9 us
    pallas_call x1, Pallas kernels, shards(): pl.pallas_call(functools.partial(backward_kernel, dims), grid_spec=pltpu....  14.9 us
    pallas_call x1, Pallas kernels, shards(): pl.pallas_call(functools.partial(forward_kernel, dims), grid_spec=pltpu.P...  11.4 us
    pallas_call x1, Pallas kernels, shards(): pl.pallas_call(functools.partial(order_kernel, chunk), grid_spec=pltpu.Pr...  8.87 us
    pallas_call x1, Pallas kernels, shards(): pl.pallas_call(last_kernel, grid=(micros,), in_specs=[micro_block(tok, wi...  5.01 us
    reshape x6, local copies, waits for them, and re-layouts, row(): return vector.reshape(1, -1)  4.86 us
  transfers between devices with their start and end apart: 29, of which 15 were waited for; matrix products, arithmetic and copies ran while one was open for 8% of the time, Pallas kernels for 10%

profile of v1, /device:TPU:0, one launch (start us, length us, event | category | flops | bytes accessed | tf_op | source)
XLA Modules:
  0.0 239.6 jit_solution(16650881440523093346)
XLA Ops:
  0.6 1.0 maximum_bitcast_fusion
  1.7 3.0 %collective-permute-start.2 = (bf16[1,384,512]{2,1,0:T(8,128)(2,1)S(1)}, bf16[1,384,512]{2,1,0:T(8,128)(2,1)S(1)}, u32[]{:S(2)}, u32[]{:S(2)}) collective-permute-start(bf16[1,384,512]{2,1,0:T(8,128)(2,1)S(1)} %maximum_bitcast_fusion), channel_id=1, source_target_pairs={{0,2},{1,3},{2,0},{3,1},{4,6},{5,7},{6,4},{7,5},{8,10},{9,11},{10,... | collective-permute-start | bytes 1179656 | tf_op jit(solution)/shard_map/ppermute | solution.py:27
  4.7 1.3 reshape.114.gain
  6.0 1.3 reshape.115.shift
  7.2 1.3 copy.34
  8.5 1.3 scatter.4.router
  9.9 3.3 %shard_map.263 = (bf16[2,512,512]{2,1,0:T(8,128)(2,1)}, bf16[2,512,128]{2,1,0:T(8,128)(2,1)}, f32[2,8,512]{2,1,0:T(8,128)}) custom-call(bf16[2,512,512]{2,1,0:T(8,128)(2,1)} %tokens.5, s32[2,3,512]{2,1,0:T(4,128)} %bitcast.55, bf16[1,512]{1,0:T(2,128)(2,1)} %reshape.114.gain, bf16[1,512]{1,0:T(2,128)(2,1)} %reshape.115.shift, ...), custom_call_target="tpu_custom_call" | custom-call | tf_op jit(solution)/shard_map/pallas_call | solution.py:464
  14.0 7.3 %collective-permute-done = bf16[1,2,512,128]{3,2,1,0:T(8,128)(2,1)S(1)} collective-permute-done((bf16[1,2,512,128]{3,2,1,0:T(8,128)(2,1)}, bf16[1,2,512,128]{3,2,1,0:T(8,128)(2,1)S(1)}, u32[]{:S(2)}, u32[]{:S(2)}) %collective-permute-start) | collective-permute-done | bytes 262176 | tf_op jit(solution)/shard_map/ppermute | solution.py:27
  24.4 2.1 pad_maximum_fusion.1.kv
  26.7 1.4 fusion.6
  28.1 11.4 %shard_map.264 = (f32[2,512,512]{2,1,0:T(8,128)}, bf16[2,512,512]{2,1,0:T(8,128)(2,1)}, bf16[2,2,64,768]{3,2,1,0:T(8,128)(2,1)}, f32[2,2,64,768]{3,2,1,0:T(8,128...) custom-call(s32[12]{0:T(128)} %concatenate.55.meta, s32[2,8]{1,0:T(2,128)} %bitcast.62, ...), custom_call_target="tpu_custom_call" | custom-call | tf_op jit(solution)/shard_map/pallas_call | solution.py:487
  39.5 27.9 %shard_map.265 = (bf16[1024,512]{1,0:T(8,128)(2,1)}, f32[1024,512]{1,0:T(8,128)}, bf16[2048,256]{1,0:T(8,128)(2,1)}, bf16[2048,256]{1,0:T(8,128)(2,1)}, bf16[204...) custom-call(s32[12]{0:T(128)} %concatenate.55.meta, ...), custom_call_target="tpu_custom_call" | custom-call | tf_op jit(solution)/shard_map/pallas_call | solution.py:520
  67.4 3.7 %collective-permute-start.13 = (bf16[2048,256]{1,0:T(8,128)(2,1)}, bf16[2048,256]{1,0:T(8,128)(2,1)S(1)}, u32[]{:S(2)}, u32[]{:S(2)}) collective-permute-start(bf16[2048,256]{1,0:T(8,128)(2,1)} %get-tuple-element.71), channel_id=1, source_target_pairs={{0,1},{1,0},{2,3},{3,2},{4,5},{5,4},{6,7},{7,6},{8,9},{9,8},{10,11... | collective-permute-start | bytes 3145736 | tf_op jit(solution)/shard_map/ppermute | solution.py:27
  71.2 0.9 pad_maximum_fusion.4.wqr
  72.1 14.9 %shard_map.266 = (f32[2,512,512]{2,1,0:T(8,128)}, bf16[4,2,512,128]{3,2,1,0:T(8,128)(2,1)}, bf16[4,384,512]{2,1,0:T(8,128)(2,1)}, f32[16,512]{1,0:T(8,128)}) custom-call(s32[12]{0:T(128)} %concatenate.55.meta, s32[2,8]{1,0:T(2,128)} %bitcast.63, bf16[2,512,512]{2,1,0:T(8,128)(2,1)} %get-tuple-element.51.normed, f32[2,512,512]{2,1,0:T(8,128)} %bitcast.41, ...), custom_call_target="tpu_custom_call" | custom-call | tf_op jit(solution)/shard_map/pallas_call | solution.py:583
  87.1 1.2 slice.169
  88.3 3.9 %collective-permute-start.4 = (bf16[2,2,512,128]{3,2,1,0:T(8,128)(2,1)S(1)}, bf16[2,2,512,128]{3,2,1,0:T(8,128)(2,1)S(1)}, u32[]{:S(2)}, u32[]{:S(2)}) collective-permute-start(bf16[2,2,512,128]{3,2,1,0:T(8,128)(2,1)S(1)} %slice.169), channel_id=1, source_target_pairs={{0,1},{1,0},{2,3},{3,2},{4,5},{5,4},{6,7},{7,6},{8,9},{9,8},{10,11... | collective-permute-start | bytes 1572872 | tf_op jit(solution)/shard_map/ppermute | solution.py:27
  92.2 1.4 collective-permute-done.4
  93.7 1.9 add_convert_fusion.16
  95.5 11.9 %collective-permute-start.5 = (bf16[1,2,512,128]{3,2,1,0:T(8,128)(2,1)S(1)}, bf16[1,2,512,128]{3,2,1,0:T(8,128)(2,1)S(1)}, u32[]{:S(2)}, u32[]{:S(2)}) collective-permute-start(bf16[1,2,512,128]{3,2,1,0:T(8,128)(2,1)S(1)} %get-tuple-element.94), channel_id=1, source_target_pairs={{0,2},{1,3},{2,0},{3,1},{4,6},{5,7},{6,4},{7,5},{8,10},{9,11},{10,... | collective-permute-start | bytes 786440 | tf_op jit(solution)/shard_map/ppermute | solution.py:27
  107.6 6.6 %collective-permute-done.5.kv_got = bf16[1,2,512,128]{3,2,1,0:T(8,128)(2,1)S(1)} collective-permute-done((bf16[1,2,512,128]{3,2,1,0:T(8,128)(2,1)S(1)}, bf16[1,2,512,128]{3,2,1,0:T(8,128)(2,1)S(1)}, u32[]{:S(2)}, u32[]{:S(2)}) %collective-permute-start.5) | collective-permute-done | bytes 262176 | tf_op jit(solution)/shard_map/ppermute | solution.py:27
  115.0 5.0 %shard_map.267 = (f32[2,512,512]{2,1,0:T(8,128)}, bf16[160,512]{1,0:T(8,128)(2,1)}) custom-call(bf16[2,512,512]{2,1,0:T(8,128)(2,1)} %tokens.5, bf16[2,512,512]{2,1,0:T(8,128)(2,1)} %get-tuple-element.51.normed, f32[2,512,512]{2,1,0:T(8,128)} %get-tuple-element.62.part, bf16[1,2,512,128]{3,2,1,0:T(8,128)(2,1)} %get-tuple-element.95.kv_own, ...), custom_call_target="tpu_custom_call" | custom-call | tf_op jit(solution)/shard_map/pallas_call | solution.py:628
  120.3 1.8 collective-permute-start.14
  122.4 6.5 %collective-permute-start.16 = (bf16[1024,256]{1,0:T(8,128)(2,1)S(1)}, bf16[1024,256]{1,0:T(8,128)(2,1)S(1)}, u32[]{:S(2)}, u32[]{:S(2)}) collective-permute-start(bf16[1024,256]{1,0:T(8,128)(2,1)S(1)} %get-tuple-element.91), channel_id=1, source_target_pairs={{0,4},{4,0},{8,12},{12,8},{16,20},{20,16},{24,28},{28,24},{1,5},{5... | collective-permute-start | bytes 1572872 | tf_op jit(solution)/shard_map/ppermute | solution.py:27
  129.0 0.9 collective-permute-start.7
  130.0 1.2 collective-permute-start.9
  131.2 3.9 %collective-permute-done.14 = bf16[1024,256]{1,0:T(8,128)(2,1)S(1)} collective-permute-done((bf16[1024,256]{1,0:T(8,128)(2,1)S(1)}, bf16[1024,256]{1,0:T(8,128)(2,1)S(1)}, u32[]{:S(2)}, u32[]{:S(2)}) %collective-permute-start.14) | collective-permute-done | bytes 524320 | tf_op jit(solution)/shard_map/ppermute | solution.py:27
  135.3 6.5 %collective-permute-start.17 = (bf16[512,256]{1,0:T(8,128)(2,1)S(1)}, bf16[512,256]{1,0:T(8,128)(2,1)S(1)}, u32[]{:S(2)}, u32[]{:S(2)}) collective-permute-start(bf16[512,256]{1,0:T(8,128)(2,1)S(1)} %get-tuple-element.108), channel_id=1, source_target_pairs={{0,4},{4,0},{8,12},{12,8},{16,20},{20,16},{24,28},{28,24},{1,5},{5... | collective-permute-start | bytes 786440 | tf_op jit(solution)/shard_map/ppermute | solution.py:27
  141.9 1.8 collective-permute-start.18
  143.7 3.3 %collective-permute-done.9 = bf16[160,512]{1,0:T(8,128)(2,1)S(1)} collective-permute-done((bf16[160,512]{1,0:T(8,128)(2,1)S(1)}, bf16[160,512]{1,0:T(8,128)(2,1)S(1)}, u32[]{:S(2)}, u32[]{:S(2)}) %collective-permute-start.9) | collective-permute-done | bytes 163872 | tf_op jit(solution)/shard_map/ppermute | solution.py:27
  147.5 4.7 %collective-permute-done.18 = bf16[512,256]{1,0:T(8,128)(2,1)S(1)} collective-permute-done((bf16[512,256]{1,0:T(8,128)(2,1)S(1)}, bf16[512,256]{1,0:T(8,128)(2,1)S(1)}, u32[]{:S(2)}, u32[]{:S(2)}) %collective-permute-start.18) | collective-permute-done | bytes 262176 | tf_op jit(solution)/shard_map/ppermute | solution.py:27
  152.4 1.9 collective-permute-start.19
  154.5 6.0 %collective-permute-done.19 = bf16[256,512]{1,0:T(8,128)(2,1)S(1)} collective-permute-done((bf16[256,512]{1,0:T(8,128)(2,1)S(1)}, bf16[256,512]{1,0:T(8,128)(2,1)S(1)}, u32[]{:S(2)}, u32[]{:S(2)}) %collective-permute-start.19) | collective-permute-done | bytes 262176 | tf_op jit(solution)/shard_map/ppermute | solution.py:27
  160.5 7.5 %collective-permute-start.20 = (bf16[128,512]{1,0:T(8,128)(2,1)S(1)}, bf16[128,512]{1,0:T(8,128)(2,1)S(1)}, u32[]{:S(2)}, u32[]{:S(2)}) collective-permute-start(bf16[128,512]{1,0:T(8,128)(2,1)S(1)} %add_convert_fusion.21), channel_id=1, source_target_pairs={{0,16},{4,20},{8,24},{12,28},{16,0},{20,4},{24,8},{28,12},{1,17},{... | collective-permute-start | bytes 393224 | tf_op jit(solution)/shard_map/ppermute | solution.py:27
  168.0 1.6 collective-permute-start.10
  169.6 3.6 %collective-permute-done.20 = bf16[128,512]{1,0:T(8,128)(2,1)S(1)} collective-permute-done((bf16[128,512]{1,0:T(8,128)(2,1)S(1)}, bf16[128,512]{1,0:T(8,128)(2,1)S(1)}, u32[]{:S(2)}, u32[]{:S(2)}) %collective-permute-start.20) | collective-permute-done | bytes 131104 | tf_op jit(solution)/shard_map/ppermute | solution.py:27
  174.1 7.4 %collective-permute-done.21 = bf16[128,512]{1,0:T(8,128)(2,1)S(1)} collective-permute-done((bf16[128,512]{1,0:T(8,128)(2,1)S(1)}, bf16[128,512]{1,0:T(8,128)(2,1)S(1)}, u32[]{:S(2)}, u32[]{:S(2)}) %collective-permute-start.21) | collective-permute-done | bytes 131104 | tf_op jit(solution)/shard_map/ppermute | solution.py:27
  181.7 2.1 collective-permute-start.11
  183.8 7.0 %collective-permute-done.22 = bf16[256,512]{1,0:T(8,128)(2,1)S(1)} collective-permute-done((bf16[256,512]{1,0:T(8,128)(2,1)S(1)}, bf16[256,512]{1,0:T(8,128)(2,1)S(1)}, u32[]{:S(2)}, u32[]{:S(2)}) %collective-permute-start.22) | collective-permute-done | bytes 262176 | tf_op jit(solution)/shard_map/ppermute | solution.py:27
  190.9 1.7 collective-permute-start.23
  192.5 8.0 %collective-permute-done.11 = bf16[544,512]{1,0:T(8,128)(2,1)S(1)} collective-permute-done((bf16[544,512]{1,0:T(8,128)(2,1)S(1)}, bf16[544,512]{1,0:T(8,128)(2,1)S(1)}, u32[]{:S(2)}, u32[]{:S(2)}) %collective-permute-start.11) | collective-permute-done | bytes 557088 | tf_op jit(solution)/shard_map/ppermute | solution.py:27
  200.6 1.8 collective-permute-start.12
  202.4 1.7 collective-permute-start.25
  204.6 7.1 %collective-permute-done.25 = bf16[512,256]{1,0:T(8,128)(2,1)S(1)} collective-permute-done((bf16[512,256]{1,0:T(8,128)(2,1)S(1)}, bf16[512,256]{1,0:T(8,128)(2,1)S(1)}, u32[]{:S(2)}, u32[]{:S(2)}) %collective-permute-start.25) | collective-permute-done | bytes 262176 | tf_op jit(solution)/shard_map/ppermute | solution.py:27
  211.7 1.4 collective-permute-start.26
  213.1 13.0 %collective-permute-done.12 = bf16[544,512]{1,0:T(8,128)(2,1)S(1)} collective-permute-done((bf16[544,512]{1,0:T(8,128)(2,1)S(1)}, bf16[544,512]{1,0:T(8,128)(2,1)S(1)}, u32[]{:S(2)}, u32[]{:S(2)}) %collective-permute-start.12) | collective-permute-done | bytes 557088 | tf_op jit(solution)/shard_map/ppermute | solution.py:27
  229.8 0.9 fusion.8
  230.7 8.9 %shard_map.268 = (f32[2048,512]{1,0:T(8,128)}, f32[512,2048]{1,0:T(8,128)}) custom-call(s32[12]{0:T(128)} %concatenate.55.meta, bf16[2048,256]{1,0:T(8,128)(2,1)} %copy-done.1, bf16[2048,256]{1,0:T(8,128)(2,1)} %copy-done.2, bf16[2048,256]{1,0:T(8,128)(2,1)} %collective-permute-done.27.got_a, bf16[2048,256]{1,0:T(8,128)(2,1)} %collective-permute-done.28.got_b), custom_call_target="tpu_custom_call" | custom-call | tf_op jit(solution)/shard_map/pallas_call | solution.py:655
  (97 shorter events, 12.2 us)
Async XLA Ops:
  1.7 12.1 %collective-permute-start.2 = (bf16[1,384,512]{2,1,0:T(8,128)(2,1)S(1)}, bf16[1,384,512]{2,1,0:T(8,128)(2,1)S(1)}, u32[]{:S(2)}, u32[]{:S(2)}) collective-permute-start(bf16[1,384,512]{2,1,0:T(8,128)(2,1)S(1)} %maximum_bitcast_fusion), channel_id=1, source_target_pairs={{0,2},{1,3},{2,0},{3,1},{4,6},{5,7},{6,4},{7,5},{8,10},{9,11},{10,... | collective-permute-start | bytes 1179656 | tf_op jit(solution)/shard_map/ppermute | solution.py:27
  13.2 8.1 %copy-start.6 = (bf16[2,512,128]{2,1,0:T(8,128)(2,1)S(1)}, bf16[2,512,128]{2,1,0:T(8,128)(2,1)}, u32[]{:S(2)}) copy-start(bf16[2,512,128]{2,1,0:T(8,128)(2,1)} %get-tuple-element.53) | copy-start | bytes 786436
  13.2 8.2 %copy-start.11 = (bf16[512]{0:T(512)(128)(2,1)S(1)}, bf16[512]{0:T(512)(128)(2,1)}, u32[]{:S(2)}) copy-start(bf16[512]{0:T(512)(128)(2,1)} %param.27) | copy-start | bytes 3076
  13.2 8.8 %copy-start.12 = (bf16[512]{0:T(512)(128)(2,1)S(1)}, bf16[512]{0:T(512)(128)(2,1)}, u32[]{:S(2)}) copy-start(bf16[512]{0:T(512)(128)(2,1)} %param.28) | copy-start | bytes 3076
  13.2 9.4 %copy-start.13 = (bf16[512]{0:T(512)(128)(2,1)S(1)}, bf16[512]{0:T(512)(128)(2,1)}, u32[]{:S(2)}) copy-start(bf16[512]{0:T(512)(128)(2,1)} %param.32) | copy-start | bytes 3076
  13.2 10.0 %copy-start.10 = (bf16[2048]{0:T(1024)(128)(2,1)S(1)}, bf16[2048]{0:T(1024)(128)(2,1)}, u32[]{:S(2)}) copy-start(bf16[2048]{0:T(1024)(128)(2,1)} %param.30) | copy-start | bytes 12292
  13.2 8.0 %collective-permute-start = (bf16[1,2,512,128]{3,2,1,0:T(8,128)(2,1)}, bf16[1,2,512,128]{3,2,1,0:T(8,128)(2,1)S(1)}, u32[]{:S(2)}, u32[]{:S(2)}) collective-permute-start(bf16[1,2,512,128]{3,2,1,0:T(8,128)(2,1)} %bitcast.50), channel_id=1, source_target_pairs={{0,2},{1,3},{2,0},{3,1},{4,6},{5,7},{6,4},{7,5},{8,10},{9,11},{10,... | collective-permute-start | bytes 786440 | tf_op jit(solution)/shard_map/ppermute | solution.py:27
  13.9 12.6 %collective-permute-start.3 = (bf16[2,384,512]{2,1,0:T(8,128)(2,1)S(1)}, bf16[2,384,512]{2,1,0:T(8,128)(2,1)S(1)}, u32[]{:S(2)}, u32[]{:S(2)}) collective-permute-start(bf16[2,384,512]{2,1,0:T(8,128)(2,1)S(1)} %pad_maximum_fusion.5), channel_id=1, source_target_pairs={{0,1},{1,0},{2,3},{3,2},{4,5},{5,4},{6,7},{7,6},{8,9},{9,8},{10,11... | collective-permute-start | bytes 2359304 | tf_op jit(solution)/shard_map/ppermute | solution.py:27
  21.3 3.1 %collective-permute-start.1 = (bf16[2,2,512,128]{3,2,1,0:T(8,128)(2,1)S(1)}, bf16[2,2,512,128]{3,2,1,0:T(8,128)(2,1)}, u32[]{:S(2)}, u32[]{:S(2)}) collective-permute-start(bf16[2,2,512,128]{3,2,1,0:T(8,128)(2,1)S(1)} %pad_maximum_fusion.7), channel_id=1, source_target_pairs={{0,1},{1,0},{2,3},{3,2},{4,5},{5,4},{6,7},{7,6},{8,9},{9,8},{10,11... | collective-permute-start | bytes 1572872 | tf_op jit(solution)/shard_map/ppermute | solution.py:27
  39.5 31.7 %copy-start = (bf16[4,192,512]{2,1,0:T(8,128)(2,1)S(1)}, bf16[4,192,512]{2,1,0:T(8,128)(2,1)}, u32[]{:S(2)}) copy-start(bf16[4,192,512]{2,1,0:T(8,128)(2,1)} %get-tuple-element.97) | copy-start | bytes 2359300
  39.5 31.7 %copy-start.9 = (bf16[16,512]{1,0:T(8,128)(2,1)S(1)}, bf16[16,512]{1,0:T(8,128)(2,1)}, u32[]{:S(2)}) copy-start(bf16[16,512]{1,0:T(8,128)(2,1)} %scatter.4.router) | copy-start | bytes 49156
  67.4 52.6 %collective-permute-start.13 = (bf16[2048,256]{1,0:T(8,128)(2,1)}, bf16[2048,256]{1,0:T(8,128)(2,1)S(1)}, u32[]{:S(2)}, u32[]{:S(2)}) collective-permute-start(bf16[2048,256]{1,0:T(8,128)(2,1)} %get-tuple-element.71), channel_id=1, source_target_pairs={{0,1},{1,0},{2,3},{3,2},{4,5},{5,4},{6,7},{7,6},{8,9},{9,8},{10,11... | collective-permute-start | bytes 3145736 | tf_op jit(solution)/shard_map/ppermute | solution.py:27
  72.1 20.0 %copy-start.14 = (bf16[2048,256]{1,0:T(8,128)(2,1)S(1)}, bf16[2048,256]{1,0:T(8,128)(2,1)}, u32[]{:S(2)}) copy-start(bf16[2048,256]{1,0:T(8,128)(2,1)} %get-tuple-element.73) | copy-start | bytes 3145732
  87.0 20.4 %copy-start.3 = (bf16[4,384,512]{2,1,0:T(8,128)(2,1)S(1)}, bf16[4,384,512]{2,1,0:T(8,128)(2,1)}, u32[]{:S(2)}) copy-start(bf16[4,384,512]{2,1,0:T(8,128)(2,1)} %get-tuple-element.68) | copy-start | bytes 4718596
  88.3 5.4 %collective-permute-start.4 = (bf16[2,2,512,128]{3,2,1,0:T(8,128)(2,1)S(1)}, bf16[2,2,512,128]{3,2,1,0:T(8,128)(2,1)S(1)}, u32[]{:S(2)}, u32[]{:S(2)}) collective-permute-start(bf16[2,2,512,128]{3,2,1,0:T(8,128)(2,1)S(1)} %slice.169), channel_id=1, source_target_pairs={{0,1},{1,0},{2,3},{3,2},{4,5},{5,4},{6,7},{7,6},{8,9},{9,8},{10,11... | collective-permute-start | bytes 1572872 | tf_op jit(solution)/shard_map/ppermute | solution.py:27
  92.1 30.0 %collective-permute-start.15 = (bf16[2048,256]{1,0:T(8,128)(2,1)S(1)}, bf16[2048,256]{1,0:T(8,128)(2,1)S(1)}, u32[]{:S(2)}, u32[]{:S(2)}) collective-permute-start(bf16[2048,256]{1,0:T(8,128)(2,1)S(1)} %copy-done.14), channel_id=1, source_target_pairs={{0,1},{1,0},{2,3},{3,2},{4,5},{5,4},{6,7},{7,6},{8,9},{9,8},{10,11... | collective-permute-start | bytes 3145736 | tf_op jit(solution)/shard_map/ppermute | solution.py:27
  95.5 18.7 %collective-permute-start.5 = (bf16[1,2,512,128]{3,2,1,0:T(8,128)(2,1)S(1)}, bf16[1,2,512,128]{3,2,1,0:T(8,128)(2,1)S(1)}, u32[]{:S(2)}, u32[]{:S(2)}) collective-permute-start(bf16[1,2,512,128]{3,2,1,0:T(8,128)(2,1)S(1)} %get-tuple-element.94), channel_id=1, source_target_pairs={{0,2},{1,3},{2,0},{3,1},{4,6},{5,7},{6,4},{7,5},{8,10},{9,11},{10,... | collective-permute-start | bytes 786440 | tf_op jit(solution)/shard_map/ppermute | solution.py:27
  107.5 21.5 %collective-permute-start.6 = (bf16[2,384,512]{2,1,0:T(8,128)(2,1)S(1)}, bf16[2,384,512]{2,1,0:T(8,128)(2,1)S(1)}, u32[]{:S(2)}, u32[]{:S(2)}) collective-permute-start(bf16[2,384,512]{2,1,0:T(8,128)(2,1)S(1)} %slice.174), channel_id=1, source_target_pairs={{0,1},{1,0},{2,3},{3,2},{4,5},{5,4},{6,7},{7,6},{8,9},{9,8},{10,11... | collective-permute-start | bytes 2359304 | tf_op jit(solution)/shard_map/ppermute | solution.py:27
  114.3 0.7 copy-start.7
  115.0 5.1 %copy-start.5 = (bf16[2048,256]{1,0:T(8,128)(2,1)S(1)}, bf16[2048,256]{1,0:T(8,128)(2,1)}, u32[]{:S(2)}) copy-start(bf16[2048,256]{1,0:T(8,128)(2,1)} %get-tuple-element.70) | copy-start | bytes 3145732
  120.0 10.0 %collective-permute-start.8 = (bf16[160,512]{1,0:T(8,128)(2,1)}, bf16[160,512]{1,0:T(8,128)(2,1)S(1)}, u32[]{:S(2)}, u32[]{:S(2)}) collective-permute-start(bf16[160,512]{1,0:T(8,128)(2,1)} %get-tuple-element.69), channel_id=1, source_target_pairs={{0,1},{1,0},{2,3},{3,2},{4,5},{5,4},{6,7},{7,6},{8,9},{9,8},{10,11... | collective-permute-start | bytes 491528 | tf_op jit(solution)/shard_map/ppermute | solution.py:27
  120.1 2.1 copy-start.4
  120.3 14.8 %collective-permute-start.14 = (bf16[1024,256]{1,0:T(8,128)(2,1)S(1)}, bf16[1024,256]{1,0:T(8,128)(2,1)S(1)}, u32[]{:S(2)}, u32[]{:S(2)}) collective-permute-start(bf16[1024,256]{1,0:T(8,128)(2,1)S(1)} %get-tuple-element.93), channel_id=1, source_target_pairs={{0,2},{1,3},{2,0},{3,1},{4,6},{5,7},{6,4},{7,5},{8,10},{9,11},{10,... | collective-permute-start | bytes 1572872 | tf_op jit(solution)/shard_map/ppermute | solution.py:27
  122.2 7.8 %copy-start.8 = (bf16[160,512]{1,0:T(8,128)(2,1)S(1)}, bf16[160,512]{1,0:T(8,128)(2,1)}, u32[]{:S(2)}) copy-start(bf16[160,512]{1,0:T(8,128)(2,1)} %get-tuple-element.69) | copy-start | bytes 491524
  122.4 19.3 %collective-permute-start.16 = (bf16[1024,256]{1,0:T(8,128)(2,1)S(1)}, bf16[1024,256]{1,0:T(8,128)(2,1)S(1)}, u32[]{:S(2)}, u32[]{:S(2)}) collective-permute-start(bf16[1024,256]{1,0:T(8,128)(2,1)S(1)} %get-tuple-element.91), channel_id=1, source_target_pairs={{0,4},{4,0},{8,12},{12,8},{16,20},{20,16},{24,28},{28,24},{1,5},{5... | collective-permute-start | bytes 1572872 | tf_op jit(solution)/shard_map/ppermute | solution.py:27
  129.0 25.3 %collective-permute-start.7 = (bf16[1,384,512]{2,1,0:T(8,128)(2,1)S(1)}, bf16[1,384,512]{2,1,0:T(8,128)(2,1)S(1)}, u32[]{:S(2)}, u32[]{:S(2)}) collective-permute-start(bf16[1,384,512]{2,1,0:T(8,128)(2,1)S(1)} %add_convert_fusion.8), channel_id=1, source_target_pairs={{0,2},{1,3},{2,0},{3,1},{4,6},{5,7},{6,4},{7,5},{8,10},{9,11},{10,... | collective-permute-start | bytes 1179656 | tf_op jit(solution)/shard_map/ppermute | solution.py:27
  130.0 17.0 %collective-permute-start.9 = (bf16[160,512]{1,0:T(8,128)(2,1)S(1)}, bf16[160,512]{1,0:T(8,128)(2,1)S(1)}, u32[]{:S(2)}, u32[]{:S(2)}) collective-permute-start(bf16[160,512]{1,0:T(8,128)(2,1)S(1)} %add_convert_fusion.19), channel_id=1, source_target_pairs={{0,2},{1,3},{2,0},{3,1},{4,6},{5,7},{6,4},{7,5},{8,10},{9,11},{10,... | collective-permute-start | bytes 491528 | tf_op jit(solution)/shard_map/ppermute | solution.py:27
  135.3 12.2 %collective-permute-start.17 = (bf16[512,256]{1,0:T(8,128)(2,1)S(1)}, bf16[512,256]{1,0:T(8,128)(2,1)S(1)}, u32[]{:S(2)}, u32[]{:S(2)}) collective-permute-start(bf16[512,256]{1,0:T(8,128)(2,1)S(1)} %get-tuple-element.108), channel_id=1, source_target_pairs={{0,4},{4,0},{8,12},{12,8},{16,20},{20,16},{24,28},{28,24},{1,5},{5... | collective-permute-start | bytes 786440 | tf_op jit(solution)/shard_map/ppermute | solution.py:27
  141.9 10.3 %collective-permute-start.18 = (bf16[512,256]{1,0:T(8,128)(2,1)S(1)}, bf16[512,256]{1,0:T(8,128)(2,1)S(1)}, u32[]{:S(2)}, u32[]{:S(2)}) collective-permute-start(bf16[512,256]{1,0:T(8,128)(2,1)S(1)} %get-tuple-element.110), channel_id=1, source_target_pairs={{0,2},{1,3},{2,0},{3,1},{4,6},{5,7},{6,4},{7,5},{8,10},{9,11},{10,... | collective-permute-start | bytes 786440 | tf_op jit(solution)/shard_map/ppermute | solution.py:27
  152.4 8.0 %collective-permute-start.19 = (bf16[256,512]{1,0:T(8,128)(2,1)S(1)}, bf16[256,512]{1,0:T(8,128)(2,1)S(1)}, u32[]{:S(2)}, u32[]{:S(2)}) collective-permute-start(bf16[256,512]{1,0:T(8,128)(2,1)S(1)} %get-tuple-element.106), channel_id=1, source_target_pairs={{0,8},{4,12},{8,0},{12,4},{16,24},{20,28},{24,16},{28,20},{1,9},{5... | collective-permute-start | bytes 786440 | tf_op jit(solution)/shard_map/ppermute | solution.py:27
  160.5 12.7 %collective-permute-start.20 = (bf16[128,512]{1,0:T(8,128)(2,1)S(1)}, bf16[128,512]{1,0:T(8,128)(2,1)S(1)}, u32[]{:S(2)}, u32[]{:S(2)}) collective-permute-start(bf16[128,512]{1,0:T(8,128)(2,1)S(1)} %add_convert_fusion.21), channel_id=1, source_target_pairs={{0,16},{4,20},{8,24},{12,28},{16,0},{20,4},{24,8},{28,12},{1,17},{... | collective-permute-start | bytes 393224 | tf_op jit(solution)/shard_map/ppermute | solution.py:27
  168.0 13.5 %collective-permute-start.10 = (bf16[544,512]{1,0:T(8,128)(2,1)S(1)}, bf16[544,512]{1,0:T(8,128)(2,1)S(1)}, u32[]{:S(2)}, u32[]{:S(2)}) collective-permute-start(bf16[544,512]{1,0:T(8,128)(2,1)S(1)} %pad_maximum_fusion.6), channel_id=1, source_target_pairs={{0,4},{4,0},{8,12},{12,8},{16,20},{20,16},{24,28},{28,24},{1,5},{5... | collective-permute-start | bytes 1671176 | tf_op jit(solution)/shard_map/ppermute | solution.py:27
  173.3 8.1 %collective-permute-start.21 = (bf16[128,512]{1,0:T(8,128)(2,1)S(1)}, bf16[128,512]{1,0:T(8,128)(2,1)S(1)}, u32[]{:S(2)}, u32[]{:S(2)}) collective-permute-start(bf16[128,512]{1,0:T(8,128)(2,1)S(1)} %add_convert_fusion.20), channel_id=1, source_target_pairs={{0,16},{4,20},{8,24},{12,28},{16,0},{20,4},{24,8},{28,12},{1,17},{... | collective-permute-start | bytes 393224 | tf_op jit(solution)/shard_map/ppermute | solution.py:27
  181.5 9.3 %collective-permute-start.22 = (bf16[256,512]{1,0:T(8,128)(2,1)S(1)}, bf16[256,512]{1,0:T(8,128)(2,1)S(1)}, u32[]{:S(2)}, u32[]{:S(2)}) collective-permute-start(bf16[256,512]{1,0:T(8,128)(2,1)S(1)} %pad_maximum_fusion.12), channel_id=1, source_target_pairs={{0,8},{4,12},{8,0},{12,4},{16,24},{20,28},{24,16},{28,20},{1,9},{5... | collective-permute-start | bytes 786440 | tf_op jit(solution)/shard_map/ppermute | solution.py:27
  181.7 18.8 %collective-permute-start.11 = (bf16[544,512]{1,0:T(8,128)(2,1)S(1)}, bf16[544,512]{1,0:T(8,128)(2,1)S(1)}, u32[]{:S(2)}, u32[]{:S(2)}) collective-permute-start(bf16[544,512]{1,0:T(8,128)(2,1)S(1)} %add_convert_fusion.2), channel_id=1, source_target_pairs={{0,8},{4,12},{8,0},{12,4},{16,24},{20,28},{24,16},{28,20},{1,9},{5... | collective-permute-start | bytes 1671176 | tf_op jit(solution)/shard_map/ppermute | solution.py:27
  190.9 13.3 %collective-permute-start.23 = (bf16[512,256]{1,0:T(8,128)(2,1)S(1)}, bf16[512,256]{1,0:T(8,128)(2,1)S(1)}, u32[]{:S(2)}, u32[]{:S(2)}) collective-permute-start(bf16[512,256]{1,0:T(8,128)(2,1)S(1)} %get-tuple-element.112), channel_id=1, source_target_pairs={{0,4},{4,0},{8,12},{12,8},{16,20},{20,16},{24,28},{28,24},{1,5},{5... | collective-permute-start | bytes 786440 | tf_op jit(solution)/shard_map/ppermute | solution.py:27
  200.6 25.4 %collective-permute-start.12 = (bf16[544,512]{1,0:T(8,128)(2,1)S(1)}, bf16[544,512]{1,0:T(8,128)(2,1)S(1)}, u32[]{:S(2)}, u32[]{:S(2)}) collective-permute-start(bf16[544,512]{1,0:T(8,128)(2,1)S(1)} %add_convert_fusion.1), channel_id=1, source_target_pairs={{0,16},{4,20},{8,24},{12,28},{16,0},{20,4},{24,8},{28,12},{1,17},{... | collective-permute-start | bytes 1671176 | tf_op jit(solution)/shard_map/ppermute | solution.py:27
  202.4 9.2 %collective-permute-start.25 = (bf16[512,256]{1,0:T(8,128)(2,1)S(1)}, bf16[512,256]{1,0:T(8,128)(2,1)S(1)}, u32[]{:S(2)}, u32[]{:S(2)}) collective-permute-start(bf16[512,256]{1,0:T(8,128)(2,1)S(1)} %get-tuple-element.111), channel_id=1, source_target_pairs={{0,2},{1,3},{2,0},{3,1},{4,6},{5,7},{6,4},{7,5},{8,10},{9,11},{10,... | collective-permute-start | bytes 786440 | tf_op jit(solution)/shard_map/ppermute | solution.py:27
  204.2 22.0 %collective-permute-start.24 = (bf16[1024,256]{1,0:T(8,128)(2,1)S(1)}, bf16[1024,256]{1,0:T(8,128)(2,1)S(1)}, u32[]{:S(2)}, u32[]{:S(2)}) collective-permute-start(bf16[1024,256]{1,0:T(8,128)(2,1)S(1)} %pad_maximum_fusion.9), channel_id=1, source_target_pairs={{0,2},{1,3},{2,0},{3,1},{4,6},{5,7},{6,4},{7,5},{8,10},{9,11},{10,... | collective-permute-start | bytes 1572872 | tf_op jit(solution)/shard_map/ppermute | solution.py:27
  211.7 14.7 %collective-permute-start.26 = (bf16[1024,256]{1,0:T(8,128)(2,1)S(1)}, bf16[1024,256]{1,0:T(8,128)(2,1)S(1)}, u32[]{:S(2)}, u32[]{:S(2)}) collective-permute-start(bf16[1024,256]{1,0:T(8,128)(2,1)S(1)} %pad_maximum_fusion.10), channel_id=1, source_target_pairs={{0,4},{4,0},{8,12},{12,8},{16,20},{20,16},{24,28},{28,24},{1,5},{5... | collective-permute-start | bytes 1572872 | tf_op jit(solution)/shard_map/ppermute | solution.py:27
  226.3 2.2 copy-start.1
  226.3 4.3 %collective-permute-start.27 = (bf16[2048,256]{1,0:T(8,128)(2,1)S(1)}, bf16[2048,256]{1,0:T(8,128)(2,1)}, u32[]{:S(2)}, u32[]{:S(2)}) collective-permute-start(bf16[2048,256]{1,0:T(8,128)(2,1)S(1)} %pad_maximum_fusion.2.own_a), channel_id=1, source_target_pairs={{0,1},{1,0},{2,3},{3,2},{4,5},{5,4},{6,7},{7,6},{8,9},{9,8},{10,11... | collective-permute-start | bytes 3145736 | tf_op jit(solution)/shard_map/ppermute | solution.py:27
  226.5 4.2 %copy-start.2 = (bf16[2048,256]{1,0:T(8,128)(2,1)}, bf16[2048,256]{1,0:T(8,128)(2,1)S(1)}, u32[]{:S(2)}) copy-start(bf16[2048,256]{1,0:T(8,128)(2,1)S(1)} %pad_maximum_fusion.3.own_b) | copy-start | bytes 3145732
  226.5 4.2 %collective-permute-start.28 = (bf16[2048,256]{1,0:T(8,128)(2,1)S(1)}, bf16[2048,256]{1,0:T(8,128)(2,1)}, u32[]{:S(2)}, u32[]{:S(2)}) collective-permute-start(bf16[2048,256]{1,0:T(8,128)(2,1)S(1)} %pad_maximum_fusion.3.own_b), channel_id=1, source_target_pairs={{0,1},{1,0},{2,3},{3,2},{4,5},{5,4},{6,7},{7,6},{8,9},{9,8},{10,11... | collective-permute-start | bytes 3145736 | tf_op jit(solution)/shard_map/ppermute | solution.py:27

commit v2 on v1

v2 whole, which is shorter than its diff:
```python
import functools

import jax
import jax.numpy as jnp
from jax import lax
from jax.experimental import pallas as pl
from jax.experimental.pallas import tpu as pltpu
from jax.sharding import PartitionSpec as P

epsilon = 1e-05
b16 = jnp.bfloat16
f32 = jnp.float32
LOW = -1e30
MIB = 1024 * 1024


def dot(left, right, over=((1,), (0,))):
    return lax.dot_general(left, right, (over, ((), ())), preferred_element_type=f32)


def log2(size):
    return size.bit_length() - 1


def flip(values, axis, bit):
    size = lax.axis_size(axis)
    return lax.ppermute(values, axis, [(i, i ^ (1 << bit)) for i in range(size)])


def hop(values, ways, groups, batch):
    pairs = []
    for b in range(batch):
        for e in range(groups):
            axis, bit = ways[e & 1]
            to_b, to_e = (b, e ^ (1 << bit)) if axis == "expert" else (b ^ (1 << bit), e)
            pairs.append((b * groups + e, to_b * groups + to_e))
    return lax.ppermute(values, ("batch", "expert"), pairs)


def add(left, right):
    return (left.astype(f32) + right.astype(f32)).astype(b16)


def normalize(values):
    centred = values - jnp.mean(values, axis=-1, keepdims=True)
    spread = lax.rsqrt(jnp.mean(centred * centred, axis=-1, keepdims=True) + epsilon)
    return centred * spread, spread


def norm_back(grad, unit, spread):
    inner = jnp.mean(grad * unit, axis=-1, keepdims=True)
    return spread * (grad - jnp.mean(grad, axis=-1, keepdims=True) - unit * inner)


def first_kernel(micro, tokens, routes, vectors, router, key_value, normed, kv, gates):
    unit, _ = normalize(tokens[micro].astype(f32))
    rows = (unit * vectors[0:1, :] + vectors[1:2, :]).astype(b16)
    normed[...] = rows
    kv[...] = dot(rows, key_value[...]).astype(b16)
    logits = dot(router[...], rows, ((1,), (1,)))
    ids = lax.broadcasted_iota(jnp.int32, logits.shape, 0)
    top = routes.shape[1]
    chosen = [
        jnp.sum(jnp.where(ids == routes[micro, k : k + 1, :], logits, 0.0), axis=0, keepdims=True)
        for k in range(top)
    ]
    peak = functools.reduce(jnp.maximum, chosen)
    powers = [jnp.exp(c - peak) for c in chosen]
    total = sum(powers)
    for k in range(top):
        gates[k : k + 1, :] = powers[k] / total


def bounds(lens, micro, first, count):
    place = first + lax.broadcasted_iota(jnp.int32, (1, count), 1)
    run = jnp.int32(0)
    low = jnp.int32(0)
    high = jnp.int32(0)
    start = jnp.zeros((1, count), jnp.int32)
    for j in range(lens.shape[1]):
        run = run + lens[micro, j]
        start = jnp.where(place >= run, run, start)
        low = jnp.where(first >= run, run, low)
        high = jnp.where(first + count - 1 >= run, run, high)
    return place, start, low, high


def key_loops(body, carry, first, tile, low, high, block):
    begin = low // block
    full_end = first // block
    full_begin = jnp.minimum((high + block - 1) // block, full_end)
    end = (first + tile - 1) // block + 1
    carry = lax.fori_loop(begin, full_begin, functools.partial(body, True), carry)
    carry = lax.fori_loop(full_begin, full_end, functools.partial(body, False), carry)
    return lax.fori_loop(full_end, end, functools.partial(body, True), carry)


def spread_rows(pieces, ids, expert):
    out = jnp.zeros_like(pieces[0])
    for piece, row in zip(pieces, ids):
        out = jnp.where(row == expert, piece, out)
    return out


def gather_rows(table, ids, experts, head):
    out = jnp.zeros((head, table[0].shape[1]), f32)
    for piece, expert in zip(table, experts):
        out = jnp.where(ids == expert, piece, out)
    return out


def expert_ids(meta, groups, local):
    base = 4 + groups
    return [meta[base + s] * local + l for s in range(groups) for l in range(local)]


def head_table(weights, rows, local, head):
    out = []
    for piece in weights:
        whole = dot(piece[...], rows, ((1,), (1,)))
        out += [whole[l * head : (l + 1) * head] for l in range(local)]
    return out


def masked(scores, key_base, place, start):
    keys = key_base + lax.broadcasted_iota(jnp.int32, scores.shape, 0)
    return jnp.where((keys <= place) & (keys >= start), scores, LOW)


def forward_kernel(dims, micro, *refs):
    groups, tok, head, tile, block, top, local = dims
    meta, lens, normed, routes, gates = refs[:5]
    pieces_kv = refs[5 : 5 + groups]
    weights = refs[5 + groups : 5 + 2 * groups]
    kv, kvt, qt, ot, lse, mixt, acc = refs[5 + 2 * groups :]
    me = meta[0]
    experts = expert_ids(meta, groups, local)
    for s, piece in enumerate(pieces_kv):
        kv[s * tok : (s + 1) * tok, :] = piece[...]
        kvt[:, s * tok : (s + 1) * tok] = piece[...].T
    table = head_table(weights, normed[...], local, head)
    for i in range(tok // tile):
        cols = slice(i * tile, (i + 1) * tile)
        ids = [routes[micro, k : k + 1, cols] for k in range(top)]
        part = [t[:, cols] for t in table]
        heads = [gather_rows(part, row, experts, head) for row in ids]
        query = jnp.concatenate(heads, axis=1).astype(b16) * jnp.asarray(0.125, b16)
        qt[i] = query
        padded = jnp.concatenate([query, jnp.zeros_like(query)], axis=0)
        first = me * tok + i * tile
        place, start, low, high = bounds(lens, micro, first, tile)
        place = jnp.concatenate([place] * top, axis=1)
        start = jnp.concatenate([start] * top, axis=1)
        acc[...] = jnp.zeros_like(acc)

        def one_block(edge, index, carry):
            peak, total = carry
            chunk = (index * block) // tok
            row = index * block - chunk * tok
            at = pl.multiple_of(meta[4 + chunk] * tok + row, block)
            scores = dot(kv[pl.ds(at, block), :], padded)
            if edge:
                scores = masked(scores, index * block, place, start)
            new_peak = jnp.maximum(peak, jnp.max(scores, axis=0, keepdims=True))
            scale = jnp.exp(peak - new_peak)
            powers = jnp.exp(scores - new_peak)
            total = total * scale + jnp.sum(powers, axis=0, keepdims=True)
            acc[...] = acc[...] * scale + dot(kvt[head:, pl.ds(at, block)], powers.astype(b16))
            return new_peak, total

        width = top * tile
        none = (jnp.full((1, width), LOW, f32), jnp.zeros((1, width), f32))
        peak, total = key_loops(one_block, none, first, tile, low, high, block)
        out = acc[...] / total
        ot[i] = out
        lse[i] = peak + jnp.log(total)
        rounded = out.astype(b16).astype(f32)
        pieces = [
            rounded[:, k * tile : (k + 1) * tile] * gates[k : k + 1, cols] for k in range(top)
        ]
        for e, expert in enumerate(experts):
            mixt[e * head : (e + 1) * head, cols] = spread_rows(pieces, ids, expert).astype(b16)


def backward_kernel(dims, micro, *refs):
    groups, tok, head, tile, block, top, local = dims
    meta, lens, gh, routes, gates, kv, kvt, qt, ot, lse, router = refs[:11]
    wq = refs[11 : 11 + groups]
    wo = refs[11 + groups : 11 + 2 * groups]
    part, keep, sent, gq, dkv, dq = refs[11 + 2 * groups :]
    me = meta[0]
    experts = expert_ids(meta, groups, local)
    every = len(experts) * head
    pad = gq.shape[0] - every
    dkv[...] = jnp.zeros_like(dkv)
    table = head_table(wo, gh[micro * tok : (micro + 1) * tok, :].astype(b16), local, head)
    for i in range(tok // tile):
        cols = slice(i * tile, (i + 1) * tile)
        ids = [routes[micro, k : k + 1, cols] for k in range(top)]
        cut = [t[:, cols] for t in table]
        back = [gather_rows(cut, row, experts, head) for row in ids]
        weights = [gates[k : k + 1, cols] for k in range(top)]
        out = ot[i]
        outs = [out[:, k * tile : (k + 1) * tile] for k in range(top)]
        grad_gates = [
            jnp.sum(b * o.astype(b16).astype(f32), axis=0, keepdims=True)
            for b, o in zip(back, outs)
        ]
        inner = sum(w * g for w, g in zip(weights, grad_gates))
        chosen = [w * (g - inner) for w, g in zip(weights, grad_gates)]
        names = lax.broadcasted_iota(jnp.int32, (pad, tile), 0)
        gq[every:, cols] = spread_rows(
            [jnp.broadcast_to(c, (pad, tile)) for c in chosen], ids, names
        ).astype(b16)
        grad = jnp.concatenate([w * b for w, b in zip(weights, back)], axis=1).astype(b16)
        delta = jnp.sum(grad.astype(f32) * out, axis=0, keepdims=True)
        query = qt[i]
        padded = jnp.concatenate([query, jnp.zeros_like(query)], axis=0)
        grad_pad = jnp.concatenate([jnp.zeros_like(grad), grad], axis=0)
        level = lse[i]
        first = me * tok + i * tile
        place, start, low, high = bounds(lens, micro, first, tile)
        place = jnp.concatenate([place] * top, axis=1)
        start = jnp.concatenate([start] * top, axis=1)
        dq[...] = jnp.zeros_like(dq)

        def one_block(edge, index, carry):
            chunk = (index * block) // tok
            row = index * block - chunk * tok
            at = pl.multiple_of(meta[4 + chunk] * tok + row, block)
            keys = kv[pl.ds(at, block), :]
            scores = dot(keys, padded)
            if edge:
                scores = masked(scores, index * block, place, start)
            soft = jnp.exp(scores - level)
            grad_scores = (soft * (dot(keys, grad_pad) - delta)).astype(b16)
            dkv[pl.ds(at, block), :] += dot(grad_scores, padded, ((1,), (1,))) + dot(
                soft.astype(b16), grad_pad, ((1,), (1,))
            )
            dq[...] += dot(kvt[:head, pl.ds(at, block)], grad_scores)
            return carry

        key_loops(one_block, 0, first, tile, low, high, block)
        grad_query = dq[...] * 0.125
        pieces = [grad_query[:, k * tile : (k + 1) * tile] for k in range(top)]
        for e, expert in enumerate(experts):
            gq[e * head : (e + 1) * head, cols] = spread_rows(pieces, ids, expert).astype(b16)
    half = groups // 2
    for s in range(half):
        keep[s] = dkv[s * tok : (s + 1) * tok, :].astype(b16)
        sent[s] = dkv[(half + s) * tok : (half + s + 1) * tok, :].astype(b16)
    size = local * head
    total = dot(gq[every : every + router.shape[0], :], router[...], ((0,), (0,)))
    for s in range(groups):
        total = total + dot(gq[s * size : (s + 1) * size, :], wq[s][...], ((0,), (0,)))
    part[...] = total


def weights_kernel(dims, rows, *refs):
    groups, size, tok, micros = dims
    table, gh = refs[:2]
    gq = refs[2 : 2 + micros]
    normed = refs[2 + micros : 2 + 2 * micros]
    mixt = refs[2 + 2 * micros : 2 + 3 * micros]
    own, sent, router_rows = refs[2 + 3 * micros :]
    every = groups * size
    router_rows[...] = sum(dot(g[every:, :], n[...]) for g, n in zip(gq, normed))
    grads = [gh[m * tok : (m + 1) * tok, :].astype(b16) for m in range(micros)]
    for s in range(groups):
        at = slice(s * size, (s + 1) * size)
        wq = sum(dot(g[at, :], n[...]) for g, n in zip(gq, normed)).astype(b16)
        wo = sum(dot(m[at, :], g) for m, g in zip(mixt, grads)).astype(b16)
        target = own if s < groups // 2 else sent
        for k in range(2 * size // rows):
            to = pl.multiple_of(table[s, k] * rows, 16)
            source = wq if k * rows < size else wo
            begin = k * rows % size
            target[pl.ds(to, rows), :] = source[begin : begin + rows, :]


def ffn_kernel(dims, *refs):
    chunk, tile, sub, micros, groups = dims
    meta, tokens, cotan, vectors, w_up, up_bias, w_down = refs[:7]
    mixt = refs[7 : 7 + micros]
    wo = refs[7 + micros : 7 + micros + groups]
    block_out, gh, own, sent, up_row, rows = refs[7 + micros + groups : 13 + micros + groups]
    hidden, second, acc, grad_acc, act_s, gu_s = refs[13 + micros + groups :]
    total, width = hidden.shape
    tok = tokens.shape[1]
    size = wo[0].shape[0]
    for m in range(micros):
        at = slice(m * tok, (m + 1) * tok)
        mixed = dot(mixt[m][:size, :], wo[0][...], ((0,), (0,)))
        for s in range(1, groups):
            mixed = mixed + dot(mixt[m][s * size : (s + 1) * size, :], wo[s][...], ((0,), (0,)))
        values = tokens[m].astype(f32) + mixed
        hidden[at, :] = values
        unit, _ = normalize(values)
        second[at, :] = (unit * vectors[2:3, :] + vectors[3:4, :]).astype(b16)
    acc[...] = jnp.zeros_like(acc)
    grad_acc[...] = jnp.zeros_like(grad_acc)
    c0 = 0.7978845608028654
    c1 = c0 * 0.044715
    per = tile // chunk

    def one_tile(step, carry):
        base = pl.multiple_of(step * tile, tile)
        span = pl.ds(base, tile)
        bias = up_bias[:, span]
        up_sum = jnp.zeros((1, tile), f32)
        for i in range(total // sub):
            at = slice(i * sub, (i + 1) * sub)
            upward = dot(second[at, :], w_up[:, span]) + bias
            grad = dot(cotan[at, :], w_down[span, :], ((1,), (1,)))
            square = upward * upward
            curve = jnp.tanh(upward * (c0 + c1 * square))
            lift = 0.5 + 0.5 * curve
            value = upward * lift
            slope = lift + value * (1.0 - curve) * (c0 + (3.0 * c1) * square)
            active = value.astype(b16)
            grad_up = (grad * slope).astype(b16)
            act_s[at, :] = active
            gu_s[at, :] = grad_up
            up_sum = up_sum + jnp.sum(grad_up.astype(f32), axis=0, keepdims=True)
            acc[at, :] += dot(active, w_down[span, :])
            grad_acc[at, :] += dot(grad_up, w_up[:, span], ((1,), (1,)))
        up_row[:, span] = up_sum
        grad_down = dot(act_s[...], cotan[...], ((0,), (0,))).astype(b16)
        grad_up_t = dot(gu_s[...], second[...], ((0,), (0,))).astype(b16)

        def place(values, target, low):
            for i in range(per):
                at = pl.multiple_of(((step * per + i) ^ low) * chunk, chunk)
                target[pl.ds(at, chunk), :] = values[i * chunk : (i + 1) * chunk, :]

        @pl.when(meta[1] == 0)
        def _():
            place(grad_down, own, meta[2])
            place(grad_up_t, sent, meta[3])

        @pl.when(meta[1] != 0)
        def _():
            place(grad_up_t, own, meta[2])
            place(grad_down, sent, meta[3])

        return carry

    lax.fori_loop(0, w_up.shape[1] // tile, one_tile, 0)
    sums = [jnp.zeros((1, width), f32) for _ in range(3)]
    for i in range(total // sub):
        at = slice(i * sub, (i + 1) * sub)
        rows_now = hidden[at, :]
        cot = cotan[at, :].astype(f32)
        block_out[at, :] = (rows_now + acc[at, :] + vectors[4:5, :]).astype(b16)
        unit, spread = normalize(rows_now)
        grad = grad_acc[at, :]
        gh[at, :] = cot + norm_back(grad * vectors[2:3, :], unit, spread)
        for j, piece in enumerate((cot, grad * unit, grad)):
            sums[j] = sums[j] + jnp.sum(piece, axis=0, keepdims=True)
    rows[...] = jnp.zeros_like(rows)
    for j in range(3):
        rows[j : j + 1, :] = sums[j]


def last_kernel(micros, *refs):
    meta, tokens, gh, vectors, key_value, up_row, rows, router_rows = refs[:8]
    normed = refs[8 : 8 + micros]
    part = refs[8 + micros : 8 + 2 * micros]
    kept = refs[8 + 2 * micros : 8 + 3 * micros]
    got = refs[8 + 3 * micros : 8 + 4 * micros]
    input_grad, own, sent, bundle = refs[8 + 4 * micros :]
    _, tok, width = tokens.shape
    key_rows = 0.0
    gain_sum = jnp.zeros((1, width), f32)
    shift_sum = jnp.zeros((1, width), f32)
    for m in range(micros):
        at = slice(m * tok, (m + 1) * tok)
        grad_kv = (kept[m][0].astype(f32) + got[m][0].astype(f32)).astype(b16)
        key_rows = key_rows + dot(grad_kv, normed[m][...], ((0,), (0,)))
        grad = part[m][...] + dot(grad_kv, key_value[...], ((1,), (1,)))
        unit, spread = normalize(tokens[m].astype(f32))
        input_grad[m] = gh[at, :] + norm_back(grad * vectors[0:1, :], unit, spread)
        gain_sum = gain_sum + jnp.sum(grad * unit, axis=0, keepdims=True)
        shift_sum = shift_sum + jnp.sum(grad, axis=0, keepdims=True)
    at = key_rows.shape[0]
    pad = router_rows.shape[0]
    bundle[:at, :] = key_rows.astype(b16)
    bundle[at : at + pad, :] = router_rows[...].astype(b16)
    count = up_row.shape[1] // width
    pieces = [up_row[:, i * width : (i + 1) * width] for i in range(count)]
    pieces += [rows[0:3, :], gain_sum, shift_sum]
    left = bundle.shape[0] - at - pad - count - 5
    pieces.append(jnp.zeros((left, width), f32))
    bundle[at + pad :, :] = jnp.concatenate(pieces, axis=0).astype(b16)
    half = own.shape[0]
    own[...] = bundle[pl.ds(pl.multiple_of(meta[1] * half, 16), half), :]
    sent[...] = bundle[pl.ds(pl.multiple_of((1 - meta[1]) * half, 16), half), :]


def order_kernel(chunk, meta, own_low, own_high, got_low, got_high, down, up):
    tile = down.shape[0]
    per = tile // chunk
    step = pl.program_id(0)
    half = own_low.shape[0] // chunk

    def sorted_rows(low, high, place):
        blocks = []
        for i in range(per):
            slot = (step * per + i) ^ place
            at = pl.multiple_of((slot & (half - 1)) * chunk, chunk)
            rows = jnp.where(slot < half, low[pl.ds(at, chunk), :].astype(f32), high[pl.ds(at, chunk), :].astype(f32))
            blocks.append(rows)
        return blocks[0] if per == 1 else jnp.concatenate(blocks, axis=0)

    own = sorted_rows(own_low, own_high, meta[2])
    got = sorted_rows(got_low, got_high, meta[3])

    @pl.when(meta[1] == 0)
    def _():
        down[...] = own
        up[...] = got.T

    @pl.when(meta[1] != 0)
    def _():
        down[...] = got
        up[...] = own.T


def small_kernel(dims, meta, table, weights, own, got, wq, wo, keys, router, up_row, *outs):
    both, pad, rows = dims
    bundle = outs[-1]
    half, width = own.shape
    bundle[pl.ds(pl.multiple_of(meta[1] * half, 16), half), :] = own[...]
    bundle[pl.ds(pl.multiple_of((1 - meta[1]) * half, 16), half), :] = got[...]
    keys[...] = bundle[:both, :].astype(f32).T
    values = bundle[both:, :].astype(f32)
    router[...] = values[: router.shape[0], :]
    count = up_row.shape[0] // width
    for i in range(count):
        up_row[i * width : (i + 1) * width] = values[pad + i]
    for i, out in enumerate(outs[:-1]):
        out[...] = values[pad + count + i]
    size = wq.shape[0]
    for k in range(2 * size // rows):
        at = pl.multiple_of(table[k] * rows, 16)
        target = wq if k * rows < size else wo
        begin = k * rows % size
        target[begin : begin + rows, :] = weights[pl.ds(at, rows), :].astype(f32)


def shards(
    tokens, routes, lengths, gain_one, shift_one, router, key_value, w_query, w_out,
    gain_two, shift_two, w_up, up_bias, w_down, down_bias, cotangent,
):
    groups = lax.axis_size("expert")
    batch = lax.axis_size("batch")
    me = lax.axis_index("expert").astype(jnp.int32)
    mine = lax.axis_index("batch").astype(jnp.int32)
    micros, tok, width = tokens.shape
    top = routes.shape[2]
    local, _, head = w_query.shape
    experts = local * groups
    every = experts * head
    size = local * head
    hidden_units = w_up.shape[1]
    group_bits, batch_bits = log2(groups), log2(batch)
    chips = groups * batch // 2
    chunk = hidden_units // chips
    tile, block = min(256, tok), min(256, tok)
    tiles = tok // tile
    span = top * tile
    pad = -(-experts // 16) * 16
    both = 2 * head
    total = micros * tok
    core = me & 1

    x_bits = [("expert", bit) for bit in range(1, group_bits)]
    b_bits = [("batch", bit) for bit in range(batch_bits)]
    orders = (x_bits + b_bits, b_bits[:2] + x_bits + b_bits[2:])
    hops = list(zip(*orders))

    def place_of(order, expert, row):
        out = jnp.int32(0)
        for i, (axis, bit) in enumerate(order):
            index = expert if axis == "expert" else row
            out = out | (((index >> bit) & 1) << (len(order) - 1 - i))
        return out

    def by_core(first, second):
        return jnp.where(core == 0, first, second)

    high = group_bits - 1
    offsets = jnp.arange(groups, dtype=jnp.int32)
    away = offsets ^ me
    slots = (away >> 1) | ((away & 1) << high)
    devices = (((offsets << 1) & (groups - 1)) | (offsets >> high)) ^ me
    places = [place_of(order, me, mine) for order in orders]
    place_own, place_other = by_core(places[0], places[1]), by_core(places[1], places[0])
    meta = jnp.concatenate([jnp.stack([me, core, place_own, place_other]), slots, devices])
    rows_w = -(-2 * size // (16 * batch)) * 16
    subs = jnp.arange(2 * size // rows_w, dtype=jnp.int32)
    tables = [place_of(order, devices[:, None], subs[None, :]) for order in orders]
    table = jnp.where(
        (offsets < groups // 2)[:, None],
        by_core(tables[0], tables[1]) ^ place_own,
        by_core(tables[1], tables[0]) ^ place_other,
    )
    final_table = place_of(b_bits, me, subs) ^ place_of(b_bits, me, mine)
    lens = lengths.reshape(micros, lengths.shape[2])

    def gather(values):
        pieces = [values]
        for axis, bit in x_bits + [("expert", 0)]:
            pieces = pieces + [flip(p, axis, bit) for p in pieces]
        return pieces

    vmem = pl.BlockSpec(memory_space=pltpu.VMEM)
    smem = pl.BlockSpec(memory_space=pltpu.SMEM)

    def call(kernel, scalars, arrays, outs, scratch=(), limit=16, flops=0, exps=0):
        return pl.pallas_call(
            kernel,
            in_specs=[smem] * len(scalars) + [vmem] * len(arrays),
            out_specs=[vmem] * len(outs),
            out_shape=[jax.ShapeDtypeStruct(*o) for o in outs],
            scratch_shapes=[pltpu.VMEM(*s) for s in scratch],
            compiler_params=pltpu.CompilerParams(vmem_limit_bytes=limit * MIB),
            cost_estimate=pl.CostEstimate(flops=flops, bytes_accessed=0, transcendentals=exps),
        )(*scalars, *arrays)

    wq = gather(w_query.transpose(0, 2, 1).reshape(size, width))
    vectors = jnp.stack([gain_one, shift_one, gain_two, shift_two, down_bias]).astype(f32)
    router_t = router.T
    routes_t = routes.transpose(0, 2, 1)

    normed, kv_pieces, gates = [], [], []
    for m in range(micros):
        n, kv, g = call(
            functools.partial(first_kernel, m),
            [],
            [tokens, routes_t, vectors, router_t, key_value],
            [((tok, width), b16), ((tok, both), b16), ((8, tok), f32)],
            flops=2 * tok * width * both,
        )
        normed.append(n)
        gates.append(g)
        kv_pieces.append(gather(kv))
    wo = gather(w_out.reshape(size, width))

    dims = (groups, tok, head, tile, block, top, local)
    keys, keys_t, qt, ot, lse, mixt = [], [], [], [], [], []
    keys_all = groups * tok
    work = 2 * tok * top * keys_all * both
    for m in range(micros):
        results = call(
            functools.partial(forward_kernel, dims, m),
            [meta, lens],
            [normed[m], routes_t, gates[m]] + kv_pieces[m] + wq,
            [
                ((keys_all, both), b16), ((both, keys_all), b16), ((tiles, head, span), b16),
                ((tiles, head, span), f32), ((tiles, 1, span), f32), ((every, tok), b16),
            ],
            [((head, span), f32)],
            flops=2 * work,
            exps=tok * top * keys_all,
        )
        for target, value in zip((keys, keys_t, qt, ot, lse, mixt), results):
            target.append(value)

    f_tile = 512
    block_out, gh, own, sent, up_row, ffn_rows = call(
        functools.partial(ffn_kernel, (chunk, f_tile, min(512, tok), micros, groups)),
        [meta],
        [tokens, cotangent.reshape(total, width), vectors, w_up, up_bias.reshape(1, -1).astype(f32), w_down]
        + mixt + wo,
        [
            ((total, width), b16), ((total, width), f32), ((hidden_units, width), b16),
            ((hidden_units, width), b16), ((1, hidden_units), f32), ((8, width), f32),
        ],
        [
            ((total, width), f32), ((total, width), b16), ((total, width), f32),
            ((total, width), f32), ((total, f_tile), b16), ((total, f_tile), b16),
        ],
        limit=32,
        flops=12 * total * width * hidden_units,
    )

    def halve(keep, got, ways):
        count = keep.shape[0] // 2
        moving = hop(add(keep[count:], got[count:]), ways, groups, batch)
        return add(keep[:count], got[:count]), moving

    keep, got = own, flip(sent, "expert", 0)
    for ways in hops:
        keep, got = halve(keep, got, ways)
    whole = add(keep, got)
    for ways in hops[:0:-1]:
        whole = jnp.concatenate([whole, hop(whole, ways, groups, batch)], axis=0)
    own_low, got_low = whole, flip(whole, "expert", 0)
    own_high = hop(whole, hops[0], groups, batch)
    got_high = flip(own_high, "expert", 0)

    part, gq, kept, arrived = [], [], [], []
    for m in range(micros):
        p, keep, sent, g = call(
            functools.partial(backward_kernel, dims, m),
            [meta, lens],
            [gh, routes_t, gates[m], keys[m], keys_t[m], qt[m], ot[m], lse[m], router_t] + wq + wo,
            [
                ((tok, width), f32), ((groups // 2, tok, both), b16),
                ((groups // 2, tok, both), b16), ((every + pad, tok), b16),
            ],
            [((keys_all, both), f32), ((head, span), f32)],
            flops=5 * work,
            exps=tok * top * keys_all,
        )
        part.append(p)
        gq.append(g)
        count = groups // 2
        got = flip(sent, "expert", 0)
        for way in x_bits[::-1]:
            count //= 2
            moving = add(keep[count:], got[count:])
            keep = add(keep[:count], got[:count])
            got = flip(moving, *way)
        kept.append(keep)
        arrived.append(got)
    w_own, w_sent, router_rows = call(
        functools.partial(weights_kernel, (groups, size, tok, micros), rows_w),
        [table],
        [gh] + gq + normed + mixt,
        [((chips * rows_w, width), b16), ((chips * rows_w, width), b16), ((pad, width), f32)],
        flops=4 * total * every * width,
    )
    rows_all = both + pad + 16
    half = -(-rows_all // 32) * 16
    input_grad, b_own, b_sent = call(
        functools.partial(last_kernel, micros),
        [meta],
        [tokens, gh, vectors, key_value, up_row, ffn_rows, router_rows] + normed + part + kept + arrived,
        [((micros, tok, width), f32), ((half, width), b16), ((half, width), b16)],
        [((2 * half, width), b16)],
        flops=8 * total * width * both,
    )

    keep, got = w_own, flip(w_sent, "expert", 0)
    bundle = add(b_own, flip(b_sent, "expert", 0))
    for ways in hops:
        count = keep.shape[0] // 2
        moving = jnp.concatenate([add(keep[count:], got[count:]), bundle], axis=0)
        keep = add(keep[:count], got[:count])
        moving = hop(moving, ways, groups, batch)
        got = moving[:count]
        bundle = add(bundle, moving[count:])
    weights = add(keep, got)
    for way in b_bits[::-1]:
        weights = jnp.concatenate([weights, flip(weights, *way)], axis=0)

    wq_grad, wo_grad, grad_key_value, grad_router, grad_up_bias, *rows = call(
        functools.partial(small_kernel, (both, pad, rows_w)),
        [meta, final_table],
        [weights, bundle, flip(bundle, "expert", 0)],
        [
            ((size, width), f32), ((size, width), f32), ((width, both), f32),
            ((experts, width), f32), ((hidden_units,), f32),
        ] + [((width,), f32)] * 5,
        [((2 * half, width), b16)],
    )
    grad_down_bias, grad_gain_two, grad_shift_two, grad_gain_one, grad_shift_one = rows

    o_tile = 256

    def full(shape):
        return pl.BlockSpec(shape, lambda j, meta: (0,) * len(shape))

    grad_down, grad_up = pl.pallas_call(
        functools.partial(order_kernel, chunk),
        grid_spec=pltpu.PrefetchScalarGridSpec(
            num_scalar_prefetch=1,
            grid=(hidden_units // o_tile,),
            in_specs=[full(own_low.shape)] * 4,
            out_specs=[
                pl.BlockSpec((o_tile, width), lambda j, meta: (j, 0)),
                pl.BlockSpec((width, o_tile), lambda j, meta: (0, j)),
            ],
        ),
        out_shape=[
            jax.ShapeDtypeStruct((hidden_units, width), f32),
            jax.ShapeDtypeStruct((width, hidden_units), f32),
        ],
        compiler_params=pltpu.CompilerParams(vmem_limit_bytes=20 * MIB),
    )(meta, own_low, own_high, got_low, got_high)

    return (
        block_out.reshape(micros, tok, width),
        input_grad,
        grad_gain_one,
        grad_shift_one,
        grad_router.T,
        grad_key_value,
        wq_grad.reshape(local, head, width).transpose(0, 2, 1),
        wo_grad.reshape(local, head, width),
        grad_gain_two,
        grad_shift_two,
        grad_up,
        grad_up_bias,
        grad_down,
        grad_down_bias,
    )


def solution(mesh):
    split = P(None, ("batch", "expert"), None)
    own = P("expert", None, None)
    in_specs = (
        split, split, P(None, "batch", None), P(), P(), P(), P(), own, own, P(), P(), P(), P(), P(),
        P(), split,
    )
    out_specs = (split, split, P(), P(), P(), P(), own, own, P(), P(), P(), P(), P(), P())
    return jax.shard_map(shards, mesh=mesh, in_specs=in_specs, out_specs=out_specs, check_vma=False)
```

time: 242 us -> 191 us (0.79)
  starting transfers between devices: 63.2 us -> 44.9 us
  Pallas kernels: 71.4 us -> 55.3 us
  waiting for transfers between devices: 80.3 us -> 73.6 us
  other arithmetic: 8.33 us -> 2.18 us
    ppermute x29 -> x25, waiting for transfers between devices: 80.3 us -> 25.9 us  [flip(): return lax.ppermute(values, axis, [(i, i ^ 1 << bit) for i in range(size)])]
    ppermute x0 -> x12, waiting for transfers between devices: none -> 47.8 us  [hop(): return lax.ppermute(values, ('batch', 'expert'), pairs)]
    ppermute x29 -> x25, starting transfers between devices: 63.2 us -> 25.4 us  [flip(): return lax.ppermute(values, axis, [(i, i ^ 1 << bit) for i in range(size)])]
    ppermute x0 -> x12, starting transfers between devices: none -> 19.5 us  [hop(): return lax.ppermute(values, ('batch', 'expert'), pairs)]
    pallas_call x5 -> x10, Pallas kernels: 62.6 us -> 48.2 us  [call(): pl.pallas_call(kernel, in_specs=[smem] * len(scalars) + [vmem] * len(arra...]
    unnamed x35 -> x43, local copies, waits for them, and re-layouts: 3.55 us -> 9.84 us
    reshape x6 -> x0, local copies, waits for them, and re-layouts: 4.86 us -> none  [row(): return vector.reshape(1, -1)]
    slice x6 -> x0, local copies, waits for them, and re-layouts: 4.24 us -> none  [the longest x1 1.43 us: shards(): wo = all_weights[:, size:].reshape(every, width)]
  transfers between devices with their start and end apart: 29 -> 37, of which waited for: 15 -> 19; matrix products, arithmetic and copies ran while one was open for 8% -> 3% of each run, Pallas kernels for 10% -> 14%
where the time goes in v2:
time: 191 us; the launch traced here: 190 us
  waiting for transfers between devices  73.6 us (39%)
  Pallas kernels  55.3 us (29%)
  starting transfers between devices  44.9 us (24%)
  local copies, waits for them, and re-layouts  13.4 us (7%)
  other arithmetic  2.18 us (1%)
    pallas_call x10, Pallas kernels, call(): pl.pallas_call(kernel, in_specs=[smem] * len(scalars) + [vmem] * len(arra...  48.2 us
    ppermute x12, waiting for transfers between devices, hop(): return lax.ppermute(values, ('batch', 'expert'), pairs)  47.8 us
    ppermute x25, waiting for transfers between devices, flip(): return lax.ppermute(values, axis, [(i, i ^ 1 << bit) for i in range(size)])  25.9 us
    ppermute x25, starting transfers between devices, flip(): return lax.ppermute(values, axis, [(i, i ^ 1 << bit) for i in range(size)])  25.4 us
    ppermute x12, starting transfers between devices, hop(): return lax.ppermute(values, ('batch', 'expert'), pairs)  19.5 us
    unnamed x43, local copies, waits for them, and re-layouts  9.84 us
    pallas_call x1, Pallas kernels, shards(): pl.pallas_call(functools.partial(order_kernel, chunk), grid_spec=pltpu.Pr...  7.1 us
  transfers between devices with their start and end apart: 37, of which 19 were waited for; matrix products, arithmetic and copies ran while one was open for 3% of the time, Pallas kernels for 14%

profile of v2, /device:TPU:0, one launch (start us, length us, event | category | flops | bytes accessed | tf_op | source)
XLA Modules:
  0.0 190.4 jit_solution(17038488464402955081)
XLA Ops:
  0.7 3.0 %collective-permute-start.3 = (bf16[192,512]{1,0:T(8,128)(2,1)}, bf16[192,512]{1,0:T(8,128)(2,1)S(1)}, u32[]{:S(2)}, u32[]{:S(2)}) collective-permute-start(bf16[192,512]{1,0:T(8,128)(2,1)} %bitcast.33), channel_id=1, source_target_pairs={{0,2},{1,3},{2,0},{3,1},{4,6},{5,7},{6,4},{7,5},{8,10},{9,11},{10,... | collective-permute-start | bytes 589832 | tf_op jit(solution)/shard_map/ppermute | solution.py:27
  7.8 1.2 copy-done
  9.1 0.9 copy-done.2
  11.5 0.7 shard_map.263
  12.2 2.1 %collective-permute-start = (bf16[512,128]{1,0:T(8,128)(2,1)S(1)}, bf16[512,128]{1,0:T(8,128)(2,1)S(1)}, u32[]{:S(2)}, u32[]{:S(2)}) collective-permute-start(bf16[512,128]{1,0:T(8,128)(2,1)S(1)} %get-tuple-element.66.refs_5_), channel_id=1, source_target_pairs={{0,2},{1,3},{2,0},{3,1},{4,6},{5,7},{6,4},{7,5},{8,10},{9,11},{10,... | collective-permute-start | bytes 393224 | tf_op jit(solution)/shard_map/ppermute | solution.py:27
  14.9 3.1 %collective-permute-done.6.refs_6_ = bf16[512,128]{1,0:T(8,128)(2,1)} collective-permute-done((bf16[512,128]{1,0:T(8,128)(2,1)S(1)}, bf16[512,128]{1,0:T(8,128)(2,1)}, u32[]{:S(2)}, u32[]{:S(2)}) %collective-permute-start.6) | collective-permute-done | bytes 131104 | tf_op jit(solution)/shard_map/ppermute | solution.py:27
  18.7 2.0 %collective-permute-done.refs_6_ = bf16[512,128]{1,0:T(8,128)(2,1)S(1)} collective-permute-done((bf16[512,128]{1,0:T(8,128)(2,1)S(1)}, bf16[512,128]{1,0:T(8,128)(2,1)S(1)}, u32[]{:S(2)}, u32[]{:S(2)}) %collective-permute-start) | collective-permute-done | bytes 131104 | tf_op jit(solution)/shard_map/ppermute | solution.py:27
  22.7 0.8 collective-permute-done.9.refs_10_.refs_16_
  24.7 0.9 copy-done.12
  25.6 0.9 copy-done.14
  26.5 0.9 copy-done.16
  27.4 0.9 copy-done.18
  28.3 3.5 %shard_map.264 = (bf16[2048,128]{1,0:T(8,128)(2,1)S(1)}, bf16[128,2048]{1,0:T(8,128)(2,1)S(1)}, bf16[2,64,768]{2,1,0:T(8,128)(2,1)S(1)}, f32[2,64,768]{2,1,0:T(8...) custom-call(s32[12]{0:T(128)S(1)} %concatenate.37.refs_0_.meta, s32[2,8]{1,0:T(2,128)S(1)} %bitcast.44, ...), custom_call_target="tpu_custom_call" | custom-call | flops 1610612736 | tf_op jit(solution)/shard_map/pallas_call | solution.py:521
  31.8 4.2 %shard_map.266 = (bf16[2048,128]{1,0:T(8,128)(2,1)S(1)}, bf16[128,2048]{1,0:T(8,128)(2,1)S(1)}, bf16[2,64,768]{2,1,0:T(8,128)(2,1)S(1)}, f32[2,64,768]{2,1,0:T(8...) custom-call(s32[12]{0:T(128)S(1)} %concatenate.37.refs_0_.meta, s32[2,8]{1,0:T(2,128)S(1)} %bitcast.45, ...), custom_call_target="tpu_custom_call" | custom-call | flops 1610612736 | tf_op jit(solution)/shard_map/pallas_call | solution.py:521
  36.1 21.4 %shard_map.267 = (bf16[1024,512]{1,0:T(8,128)(2,1)}, f32[1024,512]{1,0:T(8,128)S(1)}, bf16[2048,512]{1,0:T(8,128)(2,1)S(1)}, bf16[2048,512]{1,0:T(8,128)(2,1)S(1...) custom-call(s32[12]{0:T(128)S(1)} %concatenate.37.refs_0_.meta, bf16[2,512,512]{2,1,0:T(8,128)(2,1)S(1)} %copy-done.1, ...), custom_call_target="tpu_custom_call" | custom-call | flops 12884901888 | tf_op jit(solution)/shard_map/pallas_call | solution.py:521
  57.5 3.1 %collective-permute-start.26 = (bf16[2048,512]{1,0:T(8,128)(2,1)S(1)}, bf16[2048,512]{1,0:T(8,128)(2,1)S(1)}, u32[]{:S(2)}, u32[]{:S(2)}) collective-permute-start(bf16[2048,512]{1,0:T(8,128)(2,1)S(1)} %get-tuple-element.109), channel_id=1, source_target_pairs={{0,1},{1,0},{2,3},{3,2},{4,5},{5,4},{6,7},{7,6},{8,9},{9,8},{10,11... | collective-permute-start | bytes 6291464 | tf_op jit(solution)/shard_map/ppermute | solution.py:27
  60.6 3.8 %collective-permute-done.26 = bf16[2048,512]{1,0:T(8,128)(2,1)S(1)} collective-permute-done((bf16[2048,512]{1,0:T(8,128)(2,1)S(1)}, bf16[2048,512]{1,0:T(8,128)(2,1)S(1)}, u32[]{:S(2)}, u32[]{:S(2)}) %collective-permute-start.26) | collective-permute-done | bytes 2097184 | tf_op jit(solution)/shard_map/ppermute | solution.py:27
  65.0 5.6 %collective-permute-start.27 = (bf16[1024,512]{1,0:T(8,128)(2,1)S(1)}, bf16[1024,512]{1,0:T(8,128)(2,1)S(1)}, u32[]{:S(2)}, u32[]{:S(2)}) collective-permute-start(bf16[1024,512]{1,0:T(8,128)(2,1)S(1)} %get-tuple-element.115), channel_id=1, source_target_pairs={{0,2},{1,5},{2,0},{3,7},{4,6},{5,1},{6,4},{7,3},{8,10},{9,13},{10,... | collective-permute-start | bytes 3145736 | tf_op jit(solution)/shard_map/ppermute | solution.py:37
  70.7 4.9 %shard_map.269 = (f32[512,512]{1,0:T(8,128)S(1)}, bf16[2,512,128]{2,1,0:T(8,128)(2,1)S(1)}, bf16[2,512,128]{2,1,0:T(8,128)(2,1)S(1)}, bf16[784,512]{1,0:T(8,128)(2,1)S(1)}) custom-call(s32[12]{0:T(128)S(1)} %concatenate.37.refs_0_.meta, s32[2,8]{1,0:T(2,128)S(1)} %bitcast.46, f32[1024,512]{1,0:T(8,128)S(1)} %get-tuple-element.73.refs_2_.refs_1_, ...), custom_call_target="tpu_custom_call" | custom-call | flops 4026531840 | tf_op jit(solution)/shard_map/pallas_call | solution.py:521
  75.7 4.7 %shard_map.268 = (f32[512,512]{1,0:T(8,128)S(1)}, bf16[2,512,128]{2,1,0:T(8,128)(2,1)S(1)}, bf16[2,512,128]{2,1,0:T(8,128)(2,1)S(1)}, bf16[784,512]{1,0:T(8,128)(2,1)S(1)}) custom-call(s32[12]{0:T(128)S(1)} %concatenate.37.refs_0_.meta, s32[2,8]{1,0:T(2,128)S(1)} %bitcast.47, f32[1024,512]{1,0:T(8,128)S(1)} %get-tuple-element.73.refs_2_.refs_1_, ...), custom_call_target="tpu_custom_call" | custom-call | flops 4026531840 | tf_op jit(solution)/shard_map/pallas_call | solution.py:521
  80.5 1.8 collective-permute-start.12
  82.2 1.2 collective-permute-done.27
  83.7 4.0 %collective-permute-start.28 = (bf16[512,512]{1,0:T(8,128)(2,1)S(1)}, bf16[512,512]{1,0:T(8,128)(2,1)S(1)}, u32[]{:S(2)}, u32[]{:S(2)}) collective-permute-start(bf16[512,512]{1,0:T(8,128)(2,1)S(1)} %get-tuple-element.117), channel_id=1, source_target_pairs={{0,4},{1,9},{2,6},{3,11},{4,0},{5,13},{6,2},{7,15},{8,12},{9,1},{1... | collective-permute-start | bytes 1572872 | tf_op jit(solution)/shard_map/ppermute | solution.py:37
  87.8 9.8 %collective-permute-start.15 = (bf16[1,512,128]{2,1,0:T(8,128)(2,1)S(1)}, bf16[1,512,128]{2,1,0:T(8,128)(2,1)S(1)}, u32[]{:S(2)}, u32[]{:S(2)}) collective-permute-start(bf16[1,512,128]{2,1,0:T(8,128)(2,1)S(1)} %get-tuple-element.124), channel_id=1, source_target_pairs={{0,2},{1,3},{2,0},{3,1},{4,6},{5,7},{6,4},{7,5},{8,10},{9,11},{10,... | collective-permute-start | bytes 393224 | tf_op jit(solution)/shard_map/ppermute | solution.py:27
  97.8 2.5 %shard_map.270 = (bf16[768,512]{1,0:T(8,128)(2,1)S(1)}, bf16[768,512]{1,0:T(8,128)(2,1)S(1)}, f32[16,512]{1,0:T(8,128)S(1)}) custom-call(s32[4,8]{1,0:T(4,128)S(1)} %xor_select_fusion.refs_0_, f32[1024,512]{1,0:T(8,128)S(1)} %get-tuple-element.73.refs_2_.refs_1_, bf16[784,512]{1,0:T(8,128)(2,1)S(1)} %get-tuple-element.81.refs_2_, ...), custom_call_target="tpu_custom_call" | custom-call | flops 1610612736 | tf_op jit(solution)/shard_map/pallas_call | solution.py:521
  100.4 1.5 collective-permute-done.15.refs_15_
  101.9 2.3 %collective-permute-done.14.refs_14_ = bf16[1,512,128]{2,1,0:T(8,128)(2,1)S(1)} collective-permute-done((bf16[1,512,128]{2,1,0:T(8,128)(2,1)S(1)}, bf16[1,512,128]{2,1,0:T(8,128)(2,1)S(1)}, u32[]{:S(2)}, u32[]{:S(2)}) %collective-permute-start.14) | collective-permute-done | bytes 131104 | tf_op jit(solution)/shard_map/ppermute | solution.py:27
  104.2 3.8 %shard_map.271 = (f32[2,512,512]{2,1,0:T(8,128)}, bf16[80,512]{1,0:T(8,128)(2,1)S(1)}, bf16[80,512]{1,0:T(8,128)(2,1)S(1)}) custom-call(s32[12]{0:T(128)S(1)} %concatenate.37.refs_0_.meta, bf16[2,512,512]{2,1,0:T(8,128)(2,1)S(1)} %copy-done.1, f32[1024,512]{1,0:T(8,128)S(1)} %get-tuple-element.73.refs_2_.refs_1_, ...), custom_call_target="tpu_custom_call" | custom-call | flops 536870912 | tf_op jit(solution)/shard_map/pallas_call | solution.py:521
  109.3 5.3 %collective-permute-done.29 = bf16[256,512]{1,0:T(8,128)(2,1)S(1)} collective-permute-done((bf16[256,512]{1,0:T(8,128)(2,1)S(1)}, bf16[256,512]{1,0:T(8,128)(2,1)S(1)}, u32[]{:S(2)}, u32[]{:S(2)}) %collective-permute-start.29) | collective-permute-done | bytes 262176 | tf_op jit(solution)/shard_map/ppermute | solution.py:37
  114.6 1.1 collective-permute-start.30
  115.9 1.8 collective-permute-start.18
  117.7 7.0 %collective-permute-done.30 = bf16[128,512]{1,0:T(8,128)(2,1)S(1)} collective-permute-done((bf16[128,512]{1,0:T(8,128)(2,1)S(1)}, bf16[128,512]{1,0:T(8,128)(2,1)S(1)}, u32[]{:S(2)}, u32[]{:S(2)}) %collective-permute-start.30) | collective-permute-done | bytes 131104 | tf_op jit(solution)/shard_map/ppermute | solution.py:37
  124.9 6.3 %collective-permute-done.31 = bf16[128,512]{1,0:T(8,128)(2,1)S(1)} collective-permute-done((bf16[128,512]{1,0:T(8,128)(2,1)S(1)}, bf16[128,512]{1,0:T(8,128)(2,1)S(1)}, u32[]{:S(2)}, u32[]{:S(2)}) %collective-permute-start.31) | collective-permute-done | bytes 131104 | tf_op jit(solution)/shard_map/ppermute | solution.py:37
  131.5 6.2 %collective-permute-done.32 = bf16[256,512]{1,0:T(8,128)(2,1)S(1)} collective-permute-done((bf16[256,512]{1,0:T(8,128)(2,1)S(1)}, bf16[256,512]{1,0:T(8,128)(2,1)S(1)}, u32[]{:S(2)}, u32[]{:S(2)}) %collective-permute-start.32) | collective-permute-done | bytes 262176 | tf_op jit(solution)/shard_map/ppermute | solution.py:37
  137.8 2.1 %collective-permute-start.19 = (bf16[272,512]{1,0:T(8,128)(2,1)S(1)}, bf16[272,512]{1,0:T(8,128)(2,1)S(1)}, u32[]{:S(2)}, u32[]{:S(2)}) collective-permute-start(bf16[272,512]{1,0:T(8,128)(2,1)S(1)} %pad_maximum_fusion.4), channel_id=1, source_target_pairs={{0,4},{1,9},{2,6},{3,11},{4,0},{5,13},{6,2},{7,15},{8,12},{9,1},{1... | collective-permute-start | bytes 835592 | tf_op jit(solution)/shard_map/ppermute | solution.py:37
  139.9 10.1 %collective-permute-done.19 = bf16[272,512]{1,0:T(8,128)(2,1)S(1)} collective-permute-done((bf16[272,512]{1,0:T(8,128)(2,1)S(1)}, bf16[272,512]{1,0:T(8,128)(2,1)S(1)}, u32[]{:S(2)}, u32[]{:S(2)}) %collective-permute-start.19) | collective-permute-done | bytes 278560 | tf_op jit(solution)/shard_map/ppermute | solution.py:37
  150.1 1.6 collective-permute-start.34
  151.8 6.9 %collective-permute-done.20 = bf16[176,512]{1,0:T(8,128)(2,1)S(1)} collective-permute-done((bf16[176,512]{1,0:T(8,128)(2,1)S(1)}, bf16[176,512]{1,0:T(8,128)(2,1)S(1)}, u32[]{:S(2)}, u32[]{:S(2)}) %collective-permute-start.20) | collective-permute-done | bytes 180256 | tf_op jit(solution)/shard_map/ppermute | solution.py:37
  158.8 2.5 %collective-permute-start.21 = (bf16[128,512]{1,0:T(8,128)(2,1)S(1)}, bf16[128,512]{1,0:T(8,128)(2,1)S(1)}, u32[]{:S(2)}, u32[]{:S(2)}) collective-permute-start(bf16[128,512]{1,0:T(8,128)(2,1)S(1)} %pad_maximum_fusion.8), channel_id=1, source_target_pairs={{0,16},{1,17},{2,18},{3,19},{4,20},{5,21},{6,22},{7,23},{8,24},{9,... | collective-permute-start | bytes 393224 | tf_op jit(solution)/shard_map/ppermute | solution.py:37
  161.3 3.7 %collective-permute-done.34.own_high = bf16[1024,512]{1,0:T(8,128)(2,1)S(1)} collective-permute-done((bf16[1024,512]{1,0:T(8,128)(2,1)S(1)}, bf16[1024,512]{1,0:T(8,128)(2,1)S(1)}, u32[]{:S(2)}, u32[]{:S(2)}) %collective-permute-start.34) | collective-permute-done | bytes 1048608 | tf_op jit(solution)/shard_map/ppermute | solution.py:37
  164.9 1.2 collective-permute-done.21
  166.1 1.2 collective-permute-start.22
  167.3 3.9 %collective-permute-done.22 = bf16[48,512]{1,0:T(8,128)(2,1)S(1)} collective-permute-done((bf16[48,512]{1,0:T(8,128)(2,1)S(1)}, bf16[48,512]{1,0:T(8,128)(2,1)S(1)}, u32[]{:S(2)}, u32[]{:S(2)}) %collective-permute-start.22) | collective-permute-done | bytes 49184 | tf_op jit(solution)/shard_map/ppermute | solution.py:27
  171.2 1.7 collective-permute-start.23
  172.9 3.0 %collective-permute-done.23 = bf16[96,512]{1,0:T(8,128)(2,1)S(1)} collective-permute-done((bf16[96,512]{1,0:T(8,128)(2,1)S(1)}, bf16[96,512]{1,0:T(8,128)(2,1)S(1)}, u32[]{:S(2)}, u32[]{:S(2)}) %collective-permute-start.23) | collective-permute-done | bytes 98336 | tf_op jit(solution)/shard_map/ppermute | solution.py:27
  176.7 4.9 %collective-permute-done.24 = bf16[192,512]{1,0:T(8,128)(2,1)S(1)} collective-permute-done((bf16[192,512]{1,0:T(8,128)(2,1)S(1)}, bf16[192,512]{1,0:T(8,128)(2,1)S(1)}, u32[]{:S(2)}, u32[]{:S(2)}) %collective-permute-start.24) | collective-permute-done | bytes 196640 | tf_op jit(solution)/shard_map/ppermute | solution.py:27
  181.7 1.6 shard_map.272
  183.3 7.1 %shard_map.273 = (f32[2048,512]{1,0:T(8,128)}, f32[512,2048]{1,0:T(8,128)}) custom-call(s32[12]{0:T(128)S(1)} %concatenate.37.refs_0_.meta, bf16[1024,512]{1,0:T(8,128)(2,1)S(1)} %pad_maximum_fusion.own_low, bf16[1024,512]{1,0:T(8,128)(2,1)S(1)} %collective-permute-done.34.own_high, bf16[1024,512]{1,0:T(8,128)(2,1)S(1)} %collective-permute-done.35.got_low, ...), custom_call_target="tpu_custom_call" | custom-call | tf_op jit(solution)/shard_map/pallas_call | solution.py:676
  (123 shorter events, 14.7 us)
Async XLA Ops:
  0.6 20.8 %copy-start.20 = (bf16[2048]{0:T(1024)(128)(2,1)S(1)}, bf16[2048]{0:T(1024)(128)(2,1)}, u32[]{:S(2)}) copy-start(bf16[2048]{0:T(1024)(128)(2,1)} %param.28) | copy-start | bytes 12292
  0.7 24.0 %copy-start.19 = (s32[2,1,8]{2,1,0:T(1,128)S(1)}, s32[2,1,8]{2,1,0:T(1,128)}, u32[]{:S(2)}) copy-start(s32[2,1,8]{2,1,0:T(1,128)} %param.18) | copy-start | bytes 196
  0.7 13.9 %collective-permute-start.3 = (bf16[192,512]{1,0:T(8,128)(2,1)}, bf16[192,512]{1,0:T(8,128)(2,1)S(1)}, u32[]{:S(2)}, u32[]{:S(2)}) collective-permute-start(bf16[192,512]{1,0:T(8,128)(2,1)} %bitcast.33), channel_id=1, source_target_pairs={{0,2},{1,3},{2,0},{3,1},{4,6},{5,7},{6,4},{7,5},{8,10},{9,11},{10,... | collective-permute-start | bytes 589832 | tf_op jit(solution)/shard_map/ppermute | solution.py:27
  7.8 1.2 copy-start
  10.7 3.7 %copy-start.9 = (bf16[3,512,64]{1,2,0:T(8,128)(2,1)S(1)}, bf16[3,512,64]{1,2,0:T(8,128)(2,1)}, u32[]{:S(2)}) copy-start(bf16[3,512,64]{1,2,0:T(8,128)(2,1)} %param.23) | copy-start | bytes 589828
  10.7 3.7 %copy-start.10 = (bf16[3,64,512]{2,1,0:T(8,128)(2,1)S(1)}, bf16[3,64,512]{2,1,0:T(8,128)(2,1)}, u32[]{:S(2)}) copy-start(bf16[3,64,512]{2,1,0:T(8,128)(2,1)} %param.24) | copy-start | bytes 589828
  11.4 6.6 %collective-permute-start.6 = (bf16[512,128]{1,0:T(8,128)(2,1)S(1)}, bf16[512,128]{1,0:T(8,128)(2,1)}, u32[]{:S(2)}, u32[]{:S(2)}) collective-permute-start(bf16[512,128]{1,0:T(8,128)(2,1)S(1)} %get-tuple-element.70.refs_5_), channel_id=1, source_target_pairs={{0,2},{1,3},{2,0},{3,1},{4,6},{5,7},{6,4},{7,5},{8,10},{9,11},{10,... | collective-permute-start | bytes 393224 | tf_op jit(solution)/shard_map/ppermute | solution.py:27
  12.2 8.5 %collective-permute-start = (bf16[512,128]{1,0:T(8,128)(2,1)S(1)}, bf16[512,128]{1,0:T(8,128)(2,1)S(1)}, u32[]{:S(2)}, u32[]{:S(2)}) collective-permute-start(bf16[512,128]{1,0:T(8,128)(2,1)S(1)} %get-tuple-element.66.refs_5_), channel_id=1, source_target_pairs={{0,2},{1,3},{2,0},{3,1},{4,6},{5,7},{6,4},{7,5},{8,10},{9,11},{10,... | collective-permute-start | bytes 393224 | tf_op jit(solution)/shard_map/ppermute | solution.py:27
  14.3 8.3 %collective-permute-start.4 = (bf16[192,512]{1,0:T(8,128)(2,1)S(1)}, bf16[192,512]{1,0:T(8,128)(2,1)S(1)}, u32[]{:S(2)}, u32[]{:S(2)}) collective-permute-start(bf16[192,512]{1,0:T(8,128)(2,1)S(1)} %bitcast.34), channel_id=1, source_target_pairs={{0,1},{1,0},{2,3},{3,2},{4,5},{5,4},{6,7},{7,6},{8,9},{9,8},{10,11... | collective-permute-start | bytes 589832 | tf_op jit(solution)/shard_map/ppermute | solution.py:27
  14.4 9.1 %collective-permute-start.9 = (bf16[192,512]{1,0:T(8,128)(2,1)S(1)}, bf16[192,512]{1,0:T(8,128)(2,1)S(1)}, u32[]{:S(2)}, u32[]{:S(2)}) collective-permute-start(bf16[192,512]{1,0:T(8,128)(2,1)S(1)} %bitcast.39), channel_id=1, source_target_pairs={{0,2},{1,3},{2,0},{3,1},{4,6},{5,7},{6,4},{7,5},{8,10},{9,11},{10,... | collective-permute-start | bytes 589832 | tf_op jit(solution)/shard_map/ppermute | solution.py:27
  14.5 10.1 %collective-permute-start.5 = (bf16[192,512]{1,0:T(8,128)(2,1)S(1)}, bf16[192,512]{1,0:T(8,128)(2,1)S(1)}, u32[]{:S(2)}, u32[]{:S(2)}) collective-permute-start(bf16[192,512]{1,0:T(8,128)(2,1)S(1)} %collective-permute-done.3.refs_10_.refs_12_), channel_id=1, source_target_pairs={{0,1},{1,0},{2,3},{3,2},{4,5},{5,4},{6,7},{7,6},{8,9},{9,8},{10,11... | collective-permute-start | bytes 589832 | tf_op jit(solution)/shard_map/ppermute | solution.py:27
  18.0 3.5 %collective-permute-start.1 = (bf16[512,128]{1,0:T(8,128)(2,1)S(1)}, bf16[512,128]{1,0:T(8,128)(2,1)S(1)}, u32[]{:S(2)}, u32[]{:S(2)}) collective-permute-start(bf16[512,128]{1,0:T(8,128)(2,1)S(1)} %get-tuple-element.66.refs_5_), channel_id=1, source_target_pairs={{0,1},{1,0},{2,3},{3,2},{4,5},{5,4},{6,7},{7,6},{8,9},{9,8},{10,11... | collective-permute-start | bytes 393224 | tf_op jit(solution)/shard_map/ppermute | solution.py:27
  20.7 2.7 %collective-permute-start.2 = (bf16[512,128]{1,0:T(8,128)(2,1)S(1)}, bf16[512,128]{1,0:T(8,128)(2,1)S(1)}, u32[]{:S(2)}, u32[]{:S(2)}) collective-permute-start(bf16[512,128]{1,0:T(8,128)(2,1)S(1)} %collective-permute-done.refs_6_), channel_id=1, source_target_pairs={{0,1},{1,0},{2,3},{3,2},{4,5},{5,4},{6,7},{7,6},{8,9},{9,8},{10,11... | collective-permute-start | bytes 393224 | tf_op jit(solution)/shard_map/ppermute | solution.py:27
  22.2 13.9 %collective-permute-start.10 = (bf16[192,512]{1,0:T(8,128)(2,1)S(1)}, bf16[192,512]{1,0:T(8,128)(2,1)S(1)}, u32[]{:S(2)}, u32[]{:S(2)}) collective-permute-start(bf16[192,512]{1,0:T(8,128)(2,1)S(1)} %bitcast.40), channel_id=1, source_target_pairs={{0,1},{1,0},{2,3},{3,2},{4,5},{5,4},{6,7},{7,6},{8,9},{9,8},{10,11... | collective-permute-start | bytes 589832 | tf_op jit(solution)/shard_map/ppermute | solution.py:27
  22.7 9.1 %collective-permute-start.7 = (bf16[512,128]{1,0:T(8,128)(2,1)S(1)}, bf16[512,128]{1,0:T(8,128)(2,1)S(1)}, u32[]{:S(2)}, u32[]{:S(2)}) collective-permute-start(bf16[512,128]{1,0:T(8,128)(2,1)S(1)} %get-tuple-element.70.refs_5_), channel_id=1, source_target_pairs={{0,1},{1,0},{2,3},{3,2},{4,5},{5,4},{6,7},{7,6},{8,9},{9,8},{10,11... | collective-permute-start | bytes 393224 | tf_op jit(solution)/shard_map/ppermute | solution.py:27
  23.5 8.3 %collective-permute-start.8 = (bf16[512,128]{1,0:T(8,128)(2,1)}, bf16[512,128]{1,0:T(8,128)(2,1)S(1)}, u32[]{:S(2)}, u32[]{:S(2)}) collective-permute-start(bf16[512,128]{1,0:T(8,128)(2,1)} %collective-permute-done.6.refs_6_), channel_id=1, source_target_pairs={{0,1},{1,0},{2,3},{3,2},{4,5},{5,4},{6,7},{7,6},{8,9},{9,8},{10,11... | collective-permute-start | bytes 393224 | tf_op jit(solution)/shard_map/ppermute | solution.py:27
  24.1 11.9 %collective-permute-start.11 = (bf16[192,512]{1,0:T(8,128)(2,1)S(1)}, bf16[192,512]{1,0:T(8,128)(2,1)S(1)}, u32[]{:S(2)}, u32[]{:S(2)}) collective-permute-start(bf16[192,512]{1,0:T(8,128)(2,1)S(1)} %collective-permute-done.9.refs_10_.refs_16_), channel_id=1, source_target_pairs={{0,1},{1,0},{2,3},{3,2},{4,5},{5,4},{6,7},{7,6},{8,9},{9,8},{10,11... | collective-permute-start | bytes 589832 | tf_op jit(solution)/shard_map/ppermute | solution.py:27
  28.3 7.8 %copy-start.8 = (bf16[2,512,512]{2,1,0:T(8,128)(2,1)S(1)}, bf16[2,512,512]{2,1,0:T(8,128)(2,1)}, u32[]{:S(2)}) copy-start(bf16[2,512,512]{2,1,0:T(8,128)(2,1)} %param.31) | copy-start | bytes 3145732
  31.8 4.3 %copy-start.1 = (bf16[2,512,512]{2,1,0:T(8,128)(2,1)S(1)}, bf16[2,512,512]{2,1,0:T(8,128)(2,1)}, u32[]{:S(2)}) copy-start(bf16[2,512,512]{2,1,0:T(8,128)(2,1)} %refs_1_.3) | copy-start | bytes 3145732
  31.8 4.3 %copy-start.6 = (bf16[512,2048]{1,0:T(8,128)(2,1)S(1)}, bf16[512,2048]{1,0:T(8,128)(2,1)}, u32[]{:S(2)}) copy-start(bf16[512,2048]{1,0:T(8,128)(2,1)} %refs_4_.2) | copy-start | bytes 6291460
  31.8 4.3 %copy-start.7 = (bf16[2048,512]{1,0:T(8,128)(2,1)S(1)}, bf16[2048,512]{1,0:T(8,128)(2,1)}, u32[]{:S(2)}) copy-start(bf16[2048,512]{1,0:T(8,128)(2,1)} %refs_6_.1) | copy-start | bytes 6291460
  57.5 6.9 %collective-permute-start.26 = (bf16[2048,512]{1,0:T(8,128)(2,1)S(1)}, bf16[2048,512]{1,0:T(8,128)(2,1)S(1)}, u32[]{:S(2)}, u32[]{:S(2)}) collective-permute-start(bf16[2048,512]{1,0:T(8,128)(2,1)S(1)} %get-tuple-element.109), channel_id=1, source_target_pairs={{0,1},{1,0},{2,3},{3,2},{4,5},{5,4},{6,7},{7,6},{8,9},{9,8},{10,11... | collective-permute-start | bytes 6291464 | tf_op jit(solution)/shard_map/ppermute | solution.py:27
  64.4 6.3 %copy-start.5 = (bf16[512,12]{0,1:T(8,128)(2,1)S(1)}, bf16[512,12]{0,1:T(8,128)(2,1)}, u32[]{:S(2)}) copy-start(bf16[512,12]{0,1:T(8,128)(2,1)} %param.21) | copy-start | bytes 36868
  65.0 18.4 %collective-permute-start.27 = (bf16[1024,512]{1,0:T(8,128)(2,1)S(1)}, bf16[1024,512]{1,0:T(8,128)(2,1)S(1)}, u32[]{:S(2)}, u32[]{:S(2)}) collective-permute-start(bf16[1024,512]{1,0:T(8,128)(2,1)S(1)} %get-tuple-element.115), channel_id=1, source_target_pairs={{0,2},{1,5},{2,0},{3,7},{4,6},{5,1},{6,4},{7,3},{8,10},{9,13},{10,... | collective-permute-start | bytes 3145736 | tf_op jit(solution)/shard_map/ppermute | solution.py:37
  75.6 12.0 %collective-permute-start.13 = (bf16[2,512,128]{2,1,0:T(8,128)(2,1)S(1)}, bf16[2,512,128]{2,1,0:T(8,128)(2,1)S(1)}, u32[]{:S(2)}, u32[]{:S(2)}) collective-permute-start(bf16[2,512,128]{2,1,0:T(8,128)(2,1)S(1)} %get-tuple-element.94), channel_id=1, source_target_pairs={{0,1},{1,0},{2,3},{3,2},{4,5},{5,4},{6,7},{7,6},{8,9},{9,8},{10,11... | collective-permute-start | bytes 786440 | tf_op jit(solution)/shard_map/ppermute | solution.py:27
  80.5 17.1 %collective-permute-start.12 = (bf16[2,512,128]{2,1,0:T(8,128)(2,1)S(1)}, bf16[2,512,128]{2,1,0:T(8,128)(2,1)S(1)}, u32[]{:S(2)}, u32[]{:S(2)}) collective-permute-start(bf16[2,512,128]{2,1,0:T(8,128)(2,1)S(1)} %get-tuple-element.92), channel_id=1, source_target_pairs={{0,1},{1,0},{2,3},{3,2},{4,5},{5,4},{6,7},{7,6},{8,9},{9,8},{10,11... | collective-permute-start | bytes 786440 | tf_op jit(solution)/shard_map/ppermute | solution.py:27
  83.7 24.3 %collective-permute-start.28 = (bf16[512,512]{1,0:T(8,128)(2,1)S(1)}, bf16[512,512]{1,0:T(8,128)(2,1)S(1)}, u32[]{:S(2)}, u32[]{:S(2)}) collective-permute-start(bf16[512,512]{1,0:T(8,128)(2,1)S(1)} %get-tuple-element.117), channel_id=1, source_target_pairs={{0,4},{1,9},{2,6},{3,11},{4,0},{5,13},{6,2},{7,15},{8,12},{9,1},{1... | collective-permute-start | bytes 1572872 | tf_op jit(solution)/shard_map/ppermute | solution.py:37
  87.8 14.1 %collective-permute-start.15 = (bf16[1,512,128]{2,1,0:T(8,128)(2,1)S(1)}, bf16[1,512,128]{2,1,0:T(8,128)(2,1)S(1)}, u32[]{:S(2)}, u32[]{:S(2)}) collective-permute-start(bf16[1,512,128]{2,1,0:T(8,128)(2,1)S(1)} %get-tuple-element.124), channel_id=1, source_target_pairs={{0,2},{1,3},{2,0},{3,1},{4,6},{5,7},{6,4},{7,5},{8,10},{9,11},{10,... | collective-permute-start | bytes 393224 | tf_op jit(solution)/shard_map/ppermute | solution.py:27
  97.7 6.5 %collective-permute-start.14 = (bf16[1,512,128]{2,1,0:T(8,128)(2,1)S(1)}, bf16[1,512,128]{2,1,0:T(8,128)(2,1)S(1)}, u32[]{:S(2)}, u32[]{:S(2)}) collective-permute-start(bf16[1,512,128]{2,1,0:T(8,128)(2,1)S(1)} %get-tuple-element.126), channel_id=1, source_target_pairs={{0,2},{1,3},{2,0},{3,1},{4,6},{5,7},{6,4},{7,5},{8,10},{9,11},{10,... | collective-permute-start | bytes 393224 | tf_op jit(solution)/shard_map/ppermute | solution.py:27
  97.8 6.4 %copy-start.3 = (bf16[512,128]{1,0:T(8,128)(2,1)S(1)}, bf16[512,128]{1,0:T(8,128)(2,1)}, u32[]{:S(2)}) copy-start(bf16[512,128]{1,0:T(8,128)(2,1)} %refs_4_.3) | copy-start | bytes 393220
  100.3 15.4 %collective-permute-start.16 = (bf16[768,512]{1,0:T(8,128)(2,1)S(1)}, bf16[768,512]{1,0:T(8,128)(2,1)S(1)}, u32[]{:S(2)}, u32[]{:S(2)}) collective-permute-start(bf16[768,512]{1,0:T(8,128)(2,1)S(1)} %get-tuple-element.97), channel_id=1, source_target_pairs={{0,1},{1,0},{2,3},{3,2},{4,5},{5,4},{6,7},{7,6},{8,9},{9,8},{10,11... | collective-permute-start | bytes 2359304 | tf_op jit(solution)/shard_map/ppermute | solution.py:27
  108.0 1.3 collective-permute-start.17
  108.1 6.4 %collective-permute-start.29 = (bf16[256,512]{1,0:T(8,128)(2,1)S(1)}, bf16[256,512]{1,0:T(8,128)(2,1)S(1)}, u32[]{:S(2)}, u32[]{:S(2)}) collective-permute-start(bf16[256,512]{1,0:T(8,128)(2,1)S(1)} %get-tuple-element.121), channel_id=1, source_target_pairs={{0,8},{1,3},{2,10},{3,1},{4,12},{5,7},{6,14},{7,5},{8,0},{9,11},{1... | collective-permute-start | bytes 786440 | tf_op jit(solution)/shard_map/ppermute | solution.py:37
  114.6 10.2 %collective-permute-start.30 = (bf16[128,512]{1,0:T(8,128)(2,1)S(1)}, bf16[128,512]{1,0:T(8,128)(2,1)S(1)}, u32[]{:S(2)}, u32[]{:S(2)}) collective-permute-start(bf16[128,512]{1,0:T(8,128)(2,1)S(1)} %add_convert_fusion.11), channel_id=1, source_target_pairs={{0,16},{1,17},{2,18},{3,19},{4,20},{5,21},{6,22},{7,23},{8,24},{9,... | collective-permute-start | bytes 393224 | tf_op jit(solution)/shard_map/ppermute | solution.py:37
  115.9 15.4 %collective-permute-start.18 = (bf16[464,512]{1,0:T(8,128)(2,1)S(1)}, bf16[464,512]{1,0:T(8,128)(2,1)S(1)}, u32[]{:S(2)}, u32[]{:S(2)}) collective-permute-start(bf16[464,512]{1,0:T(8,128)(2,1)S(1)} %pad_maximum_fusion.2), channel_id=1, source_target_pairs={{0,2},{1,5},{2,0},{3,7},{4,6},{5,1},{6,4},{7,3},{8,10},{9,13},{10,... | collective-permute-start | bytes 1425416 | tf_op jit(solution)/shard_map/ppermute | solution.py:37
  124.8 6.4 %collective-permute-start.31 = (bf16[128,512]{1,0:T(8,128)(2,1)S(1)}, bf16[128,512]{1,0:T(8,128)(2,1)S(1)}, u32[]{:S(2)}, u32[]{:S(2)}) collective-permute-start(bf16[128,512]{1,0:T(8,128)(2,1)S(1)} %add_convert_fusion.10), channel_id=1, source_target_pairs={{0,16},{1,17},{2,18},{3,19},{4,20},{5,21},{6,22},{7,23},{8,24},{9,... | collective-permute-start | bytes 393224 | tf_op jit(solution)/shard_map/ppermute | solution.py:37
  131.2 6.4 %collective-permute-start.32 = (bf16[256,512]{1,0:T(8,128)(2,1)S(1)}, bf16[256,512]{1,0:T(8,128)(2,1)S(1)}, u32[]{:S(2)}, u32[]{:S(2)}) collective-permute-start(bf16[256,512]{1,0:T(8,128)(2,1)S(1)} %pad_maximum_fusion.5), channel_id=1, source_target_pairs={{0,8},{1,3},{2,10},{3,1},{4,12},{5,7},{6,14},{7,5},{8,0},{9,11},{1... | collective-permute-start | bytes 786440 | tf_op jit(solution)/shard_map/ppermute | solution.py:37
  137.7 12.3 %collective-permute-start.33 = (bf16[512,512]{1,0:T(8,128)(2,1)S(1)}, bf16[512,512]{1,0:T(8,128)(2,1)S(1)}, u32[]{:S(2)}, u32[]{:S(2)}) collective-permute-start(bf16[512,512]{1,0:T(8,128)(2,1)S(1)} %pad_maximum_fusion.1), channel_id=1, source_target_pairs={{0,4},{1,9},{2,6},{3,11},{4,0},{5,13},{6,2},{7,15},{8,12},{9,1},{1... | collective-permute-start | bytes 1572872 | tf_op jit(solution)/shard_map/ppermute | solution.py:37
  137.8 12.1 %collective-permute-start.19 = (bf16[272,512]{1,0:T(8,128)(2,1)S(1)}, bf16[272,512]{1,0:T(8,128)(2,1)S(1)}, u32[]{:S(2)}, u32[]{:S(2)}) collective-permute-start(bf16[272,512]{1,0:T(8,128)(2,1)S(1)} %pad_maximum_fusion.4), channel_id=1, source_target_pairs={{0,4},{1,9},{2,6},{3,11},{4,0},{5,13},{6,2},{7,15},{8,12},{9,1},{1... | collective-permute-start | bytes 835592 | tf_op jit(solution)/shard_map/ppermute | solution.py:37
  150.1 14.9 %collective-permute-start.34 = (bf16[1024,512]{1,0:T(8,128)(2,1)S(1)}, bf16[1024,512]{1,0:T(8,128)(2,1)S(1)}, u32[]{:S(2)}, u32[]{:S(2)}) collective-permute-start(bf16[1024,512]{1,0:T(8,128)(2,1)S(1)} %pad_maximum_fusion.own_low), channel_id=1, source_target_pairs={{0,2},{1,5},{2,0},{3,7},{4,6},{5,1},{6,4},{7,3},{8,10},{9,13},{10,... | collective-permute-start | bytes 3145736 | tf_op jit(solution)/shard_map/ppermute | solution.py:37
  151.7 7.0 %collective-permute-start.20 = (bf16[176,512]{1,0:T(8,128)(2,1)S(1)}, bf16[176,512]{1,0:T(8,128)(2,1)S(1)}, u32[]{:S(2)}, u32[]{:S(2)}) collective-permute-start(bf16[176,512]{1,0:T(8,128)(2,1)S(1)} %pad_maximum_fusion.7), channel_id=1, source_target_pairs={{0,8},{1,3},{2,10},{3,1},{4,12},{5,7},{6,14},{7,5},{8,0},{9,11},{1... | collective-permute-start | bytes 540680 | tf_op jit(solution)/shard_map/ppermute | solution.py:37
  158.8 7.3 %collective-permute-start.21 = (bf16[128,512]{1,0:T(8,128)(2,1)S(1)}, bf16[128,512]{1,0:T(8,128)(2,1)S(1)}, u32[]{:S(2)}, u32[]{:S(2)}) collective-permute-start(bf16[128,512]{1,0:T(8,128)(2,1)S(1)} %pad_maximum_fusion.8), channel_id=1, source_target_pairs={{0,16},{1,17},{2,18},{3,19},{4,20},{5,21},{6,22},{7,23},{8,24},{9,... | collective-permute-start | bytes 393224 | tf_op jit(solution)/shard_map/ppermute | solution.py:37
  161.3 22.0 %collective-permute-start.35 = (bf16[1024,512]{1,0:T(8,128)(2,1)S(1)}, bf16[1024,512]{1,0:T(8,128)(2,1)S(1)}, u32[]{:S(2)}, u32[]{:S(2)}) collective-permute-start(bf16[1024,512]{1,0:T(8,128)(2,1)S(1)} %pad_maximum_fusion.own_low), channel_id=1, source_target_pairs={{0,1},{1,0},{2,3},{3,2},{4,5},{5,4},{6,7},{7,6},{8,9},{9,8},{10,11... | collective-permute-start | bytes 3145736 | tf_op jit(solution)/shard_map/ppermute | solution.py:27
  164.9 18.4 %collective-permute-start.36 = (bf16[1024,512]{1,0:T(8,128)(2,1)S(1)}, bf16[1024,512]{1,0:T(8,128)(2,1)}, u32[]{:S(2)}, u32[]{:S(2)}) collective-permute-start(bf16[1024,512]{1,0:T(8,128)(2,1)S(1)} %collective-permute-done.34.own_high), channel_id=1, source_target_pairs={{0,1},{1,0},{2,3},{3,2},{4,5},{5,4},{6,7},{7,6},{8,9},{9,8},{10,11... | collective-permute-start | bytes 3145736 | tf_op jit(solution)/shard_map/ppermute | solution.py:27
  166.1 5.1 %collective-permute-start.22 = (bf16[48,512]{1,0:T(8,128)(2,1)S(1)}, bf16[48,512]{1,0:T(8,128)(2,1)S(1)}, u32[]{:S(2)}, u32[]{:S(2)}) collective-permute-start(bf16[48,512]{1,0:T(8,128)(2,1)S(1)} %add_convert_fusion.24), channel_id=1, source_target_pairs={{0,16},{4,20},{8,24},{12,28},{16,0},{20,4},{24,8},{28,12},{1,17},{... | collective-permute-start | bytes 147464 | tf_op jit(solution)/shard_map/ppermute | solution.py:27
  171.2 4.7 %collective-permute-start.23 = (bf16[96,512]{1,0:T(8,128)(2,1)S(1)}, bf16[96,512]{1,0:T(8,128)(2,1)S(1)}, u32[]{:S(2)}, u32[]{:S(2)}) collective-permute-start(bf16[96,512]{1,0:T(8,128)(2,1)S(1)} %pad_maximum_fusion.9), channel_id=1, source_target_pairs={{0,8},{4,12},{8,0},{12,4},{16,24},{20,28},{24,16},{28,20},{1,9},{5... | collective-permute-start | bytes 294920 | tf_op jit(solution)/shard_map/ppermute | solution.py:27
  175.9 5.7 %collective-permute-start.24 = (bf16[192,512]{1,0:T(8,128)(2,1)S(1)}, bf16[192,512]{1,0:T(8,128)(2,1)S(1)}, u32[]{:S(2)}, u32[]{:S(2)}) collective-permute-start(bf16[192,512]{1,0:T(8,128)(2,1)S(1)} %pad_maximum_fusion.6), channel_id=1, source_target_pairs={{0,4},{4,0},{8,12},{12,8},{16,20},{20,16},{24,28},{28,24},{1,5},{5... | collective-permute-start | bytes 589832 | tf_op jit(solution)/shard_map/ppermute | solution.py:27
  176.6 5.0 %collective-permute-start.25 = (bf16[80,512]{1,0:T(8,128)(2,1)S(1)}, bf16[80,512]{1,0:T(8,128)(2,1)S(1)}, u32[]{:S(2)}, u32[]{:S(2)}) collective-permute-start(bf16[80,512]{1,0:T(8,128)(2,1)S(1)} %add_convert_fusion.19.own), channel_id=1, source_target_pairs={{0,1},{1,0},{2,3},{3,2},{4,5},{5,4},{6,7},{7,6},{8,9},{9,8},{10,11... | collective-permute-start | bytes 245768 | tf_op jit(solution)/shard_map/ppermute | solution.py:27
  (10 other events, 7.9 us)

commit v3 on v2

--- a/solution.py
+++ b/solution.py
@@ -37,6 +37,10 @@
     return lax.ppermute(values, ("batch", "expert"), pairs)
 
 
+def after(values, token):
+    return lax.optimization_barrier((values, token))[0]
+
+
 def add(left, right):
     return (left.astype(f32) + right.astype(f32)).astype(b16)
 
@@ -52,33 +56,53 @@
     return spread * (grad - jnp.mean(grad, axis=-1, keepdims=True) - unit * inner)
 
 
-def first_kernel(micro, tokens, routes, vectors, router, key_value, normed, kv, gates):
-    unit, _ = normalize(tokens[micro].astype(f32))
-    rows = (unit * vectors[0:1, :] + vectors[1:2, :]).astype(b16)
-    normed[...] = rows
-    kv[...] = dot(rows, key_value[...]).astype(b16)
-    logits = dot(router[...], rows, ((1,), (1,)))
-    ids = lax.broadcasted_iota(jnp.int32, logits.shape, 0)
-    top = routes.shape[1]
-    chosen = [
-        jnp.sum(jnp.where(ids == routes[micro, k : k + 1, :], logits, 0.0), axis=0, keepdims=True)
-        for k in range(top)
-    ]
-    peak = functools.reduce(jnp.maximum, chosen)
-    powers = [jnp.exp(c - peak) for c in chosen]
-    total = sum(powers)
-    for k in range(top):
-        gates[k : k + 1, :] = powers[k] / total
-
-
-def bounds(lens, micro, first, count):
+def load(pairs, sems):
+    copies = [pltpu.make_async_copy(a, b, sems.at[i]) for i, (a, b) in enumerate(pairs)]
+    for copy in copies:
+        copy.start()
+    for copy in copies:
+        copy.wait()
+
+
+def row(vector):
+    return vector[...].astype(f32).reshape(1, -1)
+
+
+def first_kernel(micros, *refs):
+    far = refs[:6]
+    normed = refs[6 : 6 + micros]
+    kv = refs[6 + micros : 6 + 2 * micros]
+    gates = refs[6 + 2 * micros : 6 + 3 * micros]
+    near = refs[6 + 3 * micros : -1]
+    load(list(zip(far, near)), refs[-1])
+    tokens, key_value, router, routes, gain, shift = near
+    top = routes.shape[0]
+    for m in range(micros):
+        unit, _ = normalize(tokens[m].astype(f32))
+        rows = (unit * row(gain) + row(shift)).astype(b16)
+        normed[m][...] = rows
+        kv[m][...] = dot(rows, key_value[...]).astype(b16)
+        logits = dot(router[...], rows, ((1,), (1,)))
+        ids = lax.broadcasted_iota(jnp.int32, logits.shape, 0)
+        chosen = [
+            jnp.sum(jnp.where(ids == routes[k, m : m + 1, :], logits, 0.0), axis=0, keepdims=True)
+            for k in range(top)
+        ]
+        peak = functools.reduce(jnp.maximum, chosen)
+        powers = [jnp.exp(c - peak) for c in chosen]
+        total = sum(powers)
+        for k in range(top):
+            gates[m][k : k + 1, :] = powers[k] / total
+
+
+def bounds(lens, first, count):
     place = first + lax.broadcasted_iota(jnp.int32, (1, count), 1)
     run = jnp.int32(0)
     low = jnp.int32(0)
     high = jnp.int32(0)
     start = jnp.zeros((1, count), jnp.int32)
-    for j in range(lens.shape[1]):
-        run = run + lens[micro, j]
+    for length in lens:
+        run = run + length
         start = jnp.where(place >= run, run, start)
         low = jnp.where(first >= run, run, low)
         high = jnp.where(first + count - 1 >= run, run, high)
@@ -128,27 +152,31 @@
 
 
 def forward_kernel(dims, micro, *refs):
-    groups, tok, head, tile, block, top, local = dims
-    meta, lens, normed, routes, gates = refs[:5]
-    pieces_kv = refs[5 : 5 + groups]
-    weights = refs[5 + groups : 5 + 2 * groups]
-    kv, kvt, qt, ot, lse, mixt, acc = refs[5 + 2 * groups :]
+    groups, tok, head, tile, block, top, local, pieces_all = dims
+    meta, normed, routes, gates = refs[:4]
+    pieces_kv = refs[4 : 4 + groups]
+    weights = refs[4 + groups : 4 + 2 * groups]
+    kv, kvt, qt, ot, lse, mixt, acc, held, routes_near, sems = refs[4 + 2 * groups :]
     me = meta[0]
     experts = expert_ids(meta, groups, local)
-    for s, piece in enumerate(pieces_kv):
-        kv[s * tok : (s + 1) * tok, :] = piece[...]
-        kvt[:, s * tok : (s + 1) * tok] = piece[...].T
-    table = head_table(weights, normed[...], local, head)
+    pairs = [(piece, kv.at[pl.ds(s * tok, tok), :]) for s, piece in enumerate(pieces_kv)]
+    pairs += [(piece, held.at[s]) for s, piece in enumerate(weights)]
+    load(pairs + [(routes, routes_near)], sems)
+    routes = routes_near
+    lens = [meta[4 + 2 * groups + micro * pieces_all + j] for j in range(pieces_all)]
+    for s in range(groups):
+        kvt[:, s * tok : (s + 1) * tok] = kv[s * tok : (s + 1) * tok, :].T
+    table = head_table([held.at[s] for s in range(groups)], normed[...], local, head)
     for i in range(tok // tile):
         cols = slice(i * tile, (i + 1) * tile)
-        ids = [routes[micro, k : k + 1, cols] for k in range(top)]
+        ids = [routes[k, micro : micro + 1, cols] for k in range(top)]
         part = [t[:, cols] for t in table]
         heads = [gather_rows(part, row, experts, head) for row in ids]
         query = jnp.concatenate(heads, axis=1).astype(b16) * jnp.asarray(0.125, b16)
         qt[i] = query
         padded = jnp.concatenate([query, jnp.zeros_like(query)], axis=0)
         first = me * tok + i * tile
-        place, start, low, high = bounds(lens, micro, first, tile)
+        place, start, low, high = bounds(lens, first, tile)
         place = jnp.concatenate([place] * top, axis=1)
         start = jnp.concatenate([start] * top, axis=1)
         acc[...] = jnp.zeros_like(acc)
@@ -183,20 +211,22 @@
 
 
 def backward_kernel(dims, micro, *refs):
-    groups, tok, head, tile, block, top, local = dims
-    meta, lens, gh, routes, gates, kv, kvt, qt, ot, lse, router = refs[:11]
-    wq = refs[11 : 11 + groups]
-    wo = refs[11 + groups : 11 + 2 * groups]
-    part, keep, sent, gq, dkv, dq = refs[11 + 2 * groups :]
+    groups, tok, head, tile, block, top, local, pieces_all = dims
+    meta, gh, routes, gates, kv, kvt, qt, ot, lse, router = refs[:10]
+    wq = refs[10 : 10 + groups]
+    wo = refs[10 + groups : 10 + 2 * groups]
+    part, keep, sent, gq, chosen_rows, token, dkv, dq = refs[10 + 2 * groups :]
+    token[...] = jnp.zeros_like(token)
+    lens = [meta[4 + 2 * groups + micro * pieces_all + j] for j in range(pieces_all)]
     me = meta[0]
     experts = expert_ids(meta, groups, local)
     every = len(experts) * head
-    pad = gq.shape[0] - every
+    pad = chosen_rows.shape[0]
     dkv[...] = jnp.zeros_like(dkv)
     table = head_table(wo, gh[micro * tok : (micro + 1) * tok, :].astype(b16), local, head)
     for i in range(tok // tile):
         cols = slice(i * tile, (i + 1) * tile)
-        ids = [routes[micro, k : k + 1, cols] for k in range(top)]
+        ids = [routes[k, micro : micro + 1, cols] for k in range(top)]
         cut = [t[:, cols] for t in table]
         back = [gather_rows(cut, row, experts, head) for row in ids]
         weights = [gates[k : k + 1, cols] for k in range(top)]
@@ -209,7 +239,7 @@
         inner = sum(w * g for w, g in zip(weights, grad_gates))
         chosen = [w * (g - inner) for w, g in zip(weights, grad_gates)]
         names = lax.broadcasted_iota(jnp.int32, (pad, tile), 0)
-        gq[every:, cols] = spread_rows(
+        chosen_rows[:, cols] = spread_rows(
             [jnp.broadcast_to(c, (pad, tile)) for c in chosen], ids, names
         ).astype(b16)
         grad = jnp.concatenate([w * b for w, b in zip(weights, back)], axis=1).astype(b16)
@@ -219,7 +249,7 @@
         grad_pad = jnp.concatenate([jnp.zeros_like(grad), grad], axis=0)
         level = lse[i]
         first = me * tok + i * tile
-        place, start, low, high = bounds(lens, micro, first, tile)
+        place, start, low, high = bounds(lens, first, tile)
         place = jnp.concatenate([place] * top, axis=1)
         start = jnp.concatenate([start] * top, axis=1)
         dq[...] = jnp.zeros_like(dq)
@@ -250,7 +280,7 @@
         keep[s] = dkv[s * tok : (s + 1) * tok, :].astype(b16)
         sent[s] = dkv[(half + s) * tok : (half + s + 1) * tok, :].astype(b16)
     size = local * head
-    total = dot(gq[every : every + router.shape[0], :], router[...], ((0,), (0,)))
+    total = dot(chosen_rows[: router.shape[0], :], router[...], ((0,), (0,)))
     for s in range(groups):
         total = total + dot(gq[s * size : (s + 1) * size, :], wq[s][...], ((0,), (0,)))
     part[...] = total
@@ -258,13 +288,11 @@
 
 def weights_kernel(dims, rows, *refs):
     groups, size, tok, micros = dims
-    table, gh = refs[:2]
-    gq = refs[2 : 2 + micros]
-    normed = refs[2 + micros : 2 + 2 * micros]
-    mixt = refs[2 + 2 * micros : 2 + 3 * micros]
-    own, sent, router_rows = refs[2 + 3 * micros :]
-    every = groups * size
-    router_rows[...] = sum(dot(g[every:, :], n[...]) for g, n in zip(gq, normed))
+    table, _, gh = refs[:3]
+    gq = refs[3 : 3 + micros]
+    normed = refs[3 + micros : 3 + 2 * micros]
+    mixt = refs[3 + 2 * micros : 3 + 3 * micros]
+    own, sent = refs[3 + 3 * micros :]
     grads = [gh[m * tok : (m + 1) * tok, :].astype(b16) for m in range(micros)]
     for s in range(groups):
         at = slice(s * size, (s + 1) * size)
@@ -280,11 +308,11 @@
 
 def ffn_kernel(dims, *refs):
     chunk, tile, sub, micros, groups = dims
-    meta, tokens, cotan, vectors, w_up, up_bias, w_down = refs[:7]
-    mixt = refs[7 : 7 + micros]
-    wo = refs[7 + micros : 7 + micros + groups]
-    block_out, gh, own, sent, up_row, rows = refs[7 + micros + groups : 13 + micros + groups]
-    hidden, second, acc, grad_acc, act_s, gu_s = refs[13 + micros + groups :]
+    meta, tokens, cotan, gain, shift, down_bias, w_up, up_bias, w_down = refs[:9]
+    mixt = refs[9 : 9 + micros]
+    wo = refs[9 + micros : 9 + micros + groups]
+    block_out, gh, own, sent, up_row, rows = refs[9 + micros + groups : 15 + micros + groups]
+    hidden, second, acc, grad_acc, act_s, gu_s = refs[15 + micros + groups :]
     total, width = hidden.shape
     tok = tokens.shape[1]
     size = wo[0].shape[0]
@@ -296,7 +324,7 @@
         values = tokens[m].astype(f32) + mixed
         hidden[at, :] = values
         unit, _ = normalize(values)
-        second[at, :] = (unit * vectors[2:3, :] + vectors[3:4, :]).astype(b16)
+        second[at, :] = (unit * row(gain) + row(shift)).astype(b16)
     acc[...] = jnp.zeros_like(acc)
     grad_acc[...] = jnp.zeros_like(grad_acc)
     c0 = 0.7978845608028654
@@ -306,7 +334,7 @@
     def one_tile(step, carry):
         base = pl.multiple_of(step * tile, tile)
         span = pl.ds(base, tile)
-        bias = up_bias[:, span]
+        bias = up_bias[:, span].astype(f32)
         up_sum = jnp.zeros((1, tile), f32)
         for i in range(total // sub):
             at = slice(i * sub, (i + 1) * sub)
@@ -351,10 +379,10 @@
         at = slice(i * sub, (i + 1) * sub)
         rows_now = hidden[at, :]
         cot = cotan[at, :].astype(f32)
-        block_out[at, :] = (rows_now + acc[at, :] + vectors[4:5, :]).astype(b16)
+        block_out[at, :] = (rows_now + acc[at, :] + row(down_bias)).astype(b16)
         unit, spread = normalize(rows_now)
         grad = grad_acc[at, :]
-        gh[at, :] = cot + norm_back(grad * vectors[2:3, :], unit, spread)
+        gh[at, :] = cot + norm_back(grad * row(gain), unit, spread)
         for j, piece in enumerate((cot, grad * unit, grad)):
             sums[j] = sums[j] + jnp.sum(piece, axis=0, keepdims=True)
     rows[...] = jnp.zeros_like(rows)
@@ -363,12 +391,13 @@
 
 
 def last_kernel(micros, *refs):
-    meta, tokens, gh, vectors, key_value, up_row, rows, router_rows = refs[:8]
-    normed = refs[8 : 8 + micros]
-    part = refs[8 + micros : 8 + 2 * micros]
-    kept = refs[8 + 2 * micros : 8 + 3 * micros]
-    got = refs[8 + 3 * micros : 8 + 4 * micros]
-    input_grad, own, sent, bundle = refs[8 + 4 * micros :]
+    meta, tokens, gh, gain, key_value, up_row, rows = refs[:7]
+    normed = refs[7 : 7 + micros]
+    part = refs[7 + micros : 7 + 2 * micros]
+    kept = refs[7 + 2 * micros : 7 + 3 * micros]
+    got = refs[7 + 3 * micros : 7 + 4 * micros]
+    chosen = refs[7 + 4 * micros : 7 + 5 * micros]
+    input_grad, own, sent, bundle = refs[7 + 5 * micros :]
     _, tok, width = tokens.shape
     key_rows = 0.0
     gain_sum = jnp.zeros((1, width), f32)
@@ -379,13 +408,14 @@
         key_rows = key_rows + dot(grad_kv, normed[m][...], ((0,), (0,)))
         grad = part[m][...] + dot(grad_kv, key_value[...], ((1,), (1,)))
         unit, spread = normalize(tokens[m].astype(f32))
-        input_grad[m] = gh[at, :] + norm_back(grad * vectors[0:1, :], unit, spread)
+        input_grad[m] = gh[at, :] + norm_back(grad * row(gain), unit, spread)
         gain_sum = gain_sum + jnp.sum(grad * unit, axis=0, keepdims=True)
         shift_sum = shift_sum + jnp.sum(grad, axis=0, keepdims=True)
     at = key_rows.shape[0]
-    pad = router_rows.shape[0]
+    pad = chosen[0].shape[0]
     bundle[:at, :] = key_rows.astype(b16)
-    bundle[at : at + pad, :] = router_rows[...].astype(b16)
+    router_rows = sum(dot(c[...], n[...]) for c, n in zip(chosen, normed))
+    bundle[at : at + pad, :] = router_rows.astype(b16)
     count = up_row.shape[1] // width
     pieces = [up_row[:, i * width : (i + 1) * width] for i in range(count)]
     pieces += [rows[0:3, :], gain_sum, shift_sum]
@@ -397,33 +427,32 @@
     sent[...] = bundle[pl.ds(pl.multiple_of((1 - meta[1]) * half, 16), half), :]
 
 
-def order_kernel(chunk, meta, own_low, own_high, got_low, got_high, down, up):
+def order_kernel(chunk, top, side, meta, own, got, *refs):
+    down, up = refs[-2:]
     tile = down.shape[0]
     per = tile // chunk
-    step = pl.program_id(0)
-    half = own_low.shape[0] // chunk
-
-    def sorted_rows(low, high, place):
+    half = own.shape[0] // chunk
+
+    def sorted_rows(ref, place):
+        first = (pl.program_id(0) * per) ^ (place & (half - 1))
         blocks = []
         for i in range(per):
-            slot = (step * per + i) ^ place
-            at = pl.multiple_of((slot & (half - 1)) * chunk, chunk)
-            rows = jnp.where(slot < half, low[pl.ds(at, chunk), :].astype(f32), high[pl.ds(at, chunk), :].astype(f32))
-            blocks.append(rows)
+            at = pl.multiple_of((first ^ i) * chunk, chunk)
+            blocks.append(ref[pl.ds(at, chunk), :].astype(f32))
         return blocks[0] if per == 1 else jnp.concatenate(blocks, axis=0)
 
-    own = sorted_rows(own_low, own_high, meta[2])
-    got = sorted_rows(got_low, got_high, meta[3])
+    own_rows = sorted_rows(own, meta[2])
+    got_rows = sorted_rows(got, meta[3])
 
     @pl.when(meta[1] == 0)
     def _():
-        down[...] = own
-        up[...] = got.T
+        down[...] = own_rows
+        up[...] = got_rows.T
 
     @pl.when(meta[1] != 0)
     def _():
-        down[...] = got
-        up[...] = own.T
+        down[...] = got_rows
+        up[...] = own_rows.T
 
 
 def small_kernel(dims, meta, table, weights, own, got, wq, wo, keys, router, up_row, *outs):
@@ -496,82 +525,104 @@
     devices = (((offsets << 1) & (groups - 1)) | (offsets >> high)) ^ me
     places = [place_of(order, me, mine) for order in orders]
     place_own, place_other = by_core(places[0], places[1]), by_core(places[1], places[0])
-    meta = jnp.concatenate([jnp.stack([me, core, place_own, place_other]), slots, devices])
+    meta = jnp.concatenate(
+        [jnp.stack([me, core, place_own, place_other]), slots, devices, lengths.reshape(-1)]
+    )
     rows_w = -(-2 * size // (16 * batch)) * 16
     subs = jnp.arange(2 * size // rows_w, dtype=jnp.int32)
-    tables = [place_of(order, devices[:, None], subs[None, :]) for order in orders]
+    tables = [
+        place_of(order, devices[:, None], subs[None, :]) ^ place_of(order, me, mine)
+        for order in orders
+    ]
     table = jnp.where(
         (offsets < groups // 2)[:, None],
-        by_core(tables[0], tables[1]) ^ place_own,
-        by_core(tables[1], tables[0]) ^ place_other,
+        by_core(tables[0], tables[1]),
+        by_core(tables[1], tables[0]),
     )
     final_table = place_of(b_bits, me, subs) ^ place_of(b_bits, me, mine)
-    lens = lengths.reshape(micros, lengths.shape[2])
-
-    def gather(values):
+
+    def gather_far(values):
         pieces = [values]
-        for axis, bit in x_bits + [("expert", 0)]:
+        for axis, bit in x_bits:
             pieces = pieces + [flip(p, axis, bit) for p in pieces]
         return pieces
 
+    def gather_near(pieces):
+        return pieces + [flip(p, "expert", 0) for p in pieces]
+
+    def gather(values):
+        return gather_near(gather_far(values))
+
     vmem = pl.BlockSpec(memory_space=pltpu.VMEM)
     smem = pl.BlockSpec(memory_space=pltpu.SMEM)
 
-    def call(kernel, scalars, arrays, outs, scratch=(), limit=16, flops=0, exps=0):
+    def call(kernel, scalars, arrays, outs, scratch=(), limit=16, cost=1, far=(), sems=0):
+        marks = [pltpu.SemaphoreType.DMA((sems,))] if sems else []
+        far_spec = pl.BlockSpec(memory_space=pltpu.HBM)
         return pl.pallas_call(
             kernel,
-            in_specs=[smem] * len(scalars) + [vmem] * len(arrays),
+            in_specs=[smem] * len(scalars) + [far_spec if i in far else vmem for i in range(len(arrays))],
             out_specs=[vmem] * len(outs),
             out_shape=[jax.ShapeDtypeStruct(*o) for o in outs],
-            scratch_shapes=[pltpu.VMEM(*s) for s in scratch],
+            scratch_shapes=[pltpu.VMEM(*s) for s in scratch] + marks,
             compiler_params=pltpu.CompilerParams(vmem_limit_bytes=limit * MIB),
-            cost_estimate=pl.CostEstimate(flops=flops, bytes_accessed=0, transcendentals=exps),
-        )(*scalars, *arrays)
+            cost_estimate=pl.CostEstimate(flops=int(cost * 1.1e9), bytes_accessed=0, transcendentals=0),
+        )(
+            *scalars,
+            *[pltpu.with_memory_space_constraint(x, pltpu.HBM) if i in far else x for i, x in enumerate(arrays)],
+        )
 
     wq = gather(w_query.transpose(0, 2, 1).reshape(size, width))
-    vectors = jnp.stack([gain_one, shift_one, gain_two, shift_two, down_bias]).astype(f32)
     router_t = router.T
-    routes_t = routes.transpose(0, 2, 1)
-
-    normed, kv_pieces, gates = [], [], []
-    for m in range(micros):
-        n, kv, g = call(
-            functools.partial(first_kernel, m),
-            [],
-            [tokens, routes_t, vectors, router_t, key_value],
-            [((tok, width), b16), ((tok, both), b16), ((8, tok), f32)],
-            flops=2 * tok * width * both,
-        )
-        normed.append(n)
-        gates.append(g)
-        kv_pieces.append(gather(kv))
+    routes_t = routes.transpose(2, 0, 1)
+    results = call(
+        functools.partial(first_kernel, micros),
+        [],
+        [tokens, key_value, router_t, routes_t, gain_one, shift_one],
+        [((tok, width), b16)] * micros + [((tok, both), b16)] * micros + [((8, tok), f32)] * micros,
+        [
+            ((micros, tok, width), b16), ((width, both), b16), ((experts, width), b16),
+            ((top, micros, tok), jnp.int32), ((width,), b16), ((width,), b16),
+        ],
+        cost=2.4,
+        far=range(6),
+        sems=6,
+    )
+    normed, gates = list(results[:micros]), results[2 * micros :]
+    kv_pieces = [gather_far(kv) for kv in results[micros : 2 * micros]]
     wo = gather(w_out.reshape(size, width))
 
-    dims = (groups, tok, head, tile, block, top, local)
+    dims = (groups, tok, head, tile, block, top, local, lengths.shape[2])
     keys, keys_t, qt, ot, lse, mixt = [], [], [], [], [], []
     keys_all = groups * tok
     work = 2 * tok * top * keys_all * both
     for m in range(micros):
+        if m > 0:
+            kv_pieces[m] = after(kv_pieces[m], lse[m - 1])
         results = call(
             functools.partial(forward_kernel, dims, m),
-            [meta, lens],
-            [normed[m], routes_t, gates[m]] + kv_pieces[m] + wq,
+            [meta],
+            [normed[m], routes_t, gates[m]] + gather_near(kv_pieces[m]) + wq,
             [
                 ((keys_all, both), b16), ((both, keys_all), b16), ((tiles, head, span), b16),
                 ((tiles, head, span), f32), ((tiles, 1, span), f32), ((every, tok), b16),
             ],
-            [((head, span), f32)],
-            flops=2 * work,
-            exps=tok * top * keys_all,
+            [((head, span), f32), ((groups, size, width), b16), ((top, micros, tok), jnp.int32)],
+            cost=5,
+            far=(1, *range(3, 3 + 2 * groups)),
+            sems=2 * groups + 1,
         )
         for target, value in zip((keys, keys_t, qt, ot, lse, mixt), results):
             target.append(value)
 
     f_tile = 512
-    block_out, gh, own, sent, up_row, ffn_rows = call(
+    block_out, gh, ffn_own, ffn_sent, up_row, ffn_rows = call(
         functools.partial(ffn_kernel, (chunk, f_tile, min(512, tok), micros, groups)),
         [meta],
-        [tokens, cotangent.reshape(total, width), vectors, w_up, up_bias.reshape(1, -1).astype(f32), w_down]
+        [
+            tokens, cotangent.reshape(total, width), gain_two, shift_two, down_bias, w_up,
+            up_bias.reshape(1, -1), w_down,
+        ]
         + mixt + wo,
         [
             ((total, width), b16), ((total, width), f32), ((hidden_units, width), b16),
@@ -582,40 +633,26 @@
             ((total, width), f32), ((total, f_tile), b16), ((total, f_tile), b16),
         ],
         limit=32,
-        flops=12 * total * width * hidden_units,
-    )
-
-    def halve(keep, got, ways):
-        count = keep.shape[0] // 2
-        moving = hop(add(keep[count:], got[count:]), ways, groups, batch)
-        return add(keep[:count], got[:count]), moving
-
-    keep, got = own, flip(sent, "expert", 0)
-    for ways in hops:
-        keep, got = halve(keep, got, ways)
-    whole = add(keep, got)
-    for ways in hops[:0:-1]:
-        whole = jnp.concatenate([whole, hop(whole, ways, groups, batch)], axis=0)
-    own_low, got_low = whole, flip(whole, "expert", 0)
-    own_high = hop(whole, hops[0], groups, batch)
-    got_high = flip(own_high, "expert", 0)
-
-    part, gq, kept, arrived = [], [], [], []
+        cost=11,
+    )
+
+    part, gq, chosen, kept, arrived, tokens_back = [], [], [], [], [], []
     for m in range(micros):
-        p, keep, sent, g = call(
+        p, keep, sent, g, c, token = call(
             functools.partial(backward_kernel, dims, m),
-            [meta, lens],
+            [meta],
             [gh, routes_t, gates[m], keys[m], keys_t[m], qt[m], ot[m], lse[m], router_t] + wq + wo,
             [
                 ((tok, width), f32), ((groups // 2, tok, both), b16),
-                ((groups // 2, tok, both), b16), ((every + pad, tok), b16),
+                ((groups // 2, tok, both), b16), ((every, tok), b16), ((pad, tok), b16), ((8, 128), f32),
             ],
             [((keys_all, both), f32), ((head, span), f32)],
-            flops=5 * work,
-            exps=tok * top * keys_all,
+            cost=9,
         )
         part.append(p)
         gq.append(g)
+        chosen.append(c)
+        tokens_back.append(token)
         count = groups // 2
         got = flip(sent, "expert", 0)
         for way in x_bits[::-1]:
@@ -625,34 +662,87 @@
             got = flip(moving, *way)
         kept.append(keep)
         arrived.append(got)
-    w_own, w_sent, router_rows = call(
+    def halve(keep, got, ways):
+        count = keep.shape[0] // 2
+        moving = hop(add(keep[count:], got[count:]), ways, groups, batch)
+        return add(keep[:count], got[:count]), moving
+
+    marks = []
+    keep, got = ffn_own, flip(ffn_sent, "expert", 0)
+    for ways in hops:
+        keep, got = halve(keep, got, ways)
+        marks.append(got)
+    whole = add(keep, got)
+
+    w_own, w_sent = call(
         functools.partial(weights_kernel, (groups, size, tok, micros), rows_w),
         [table],
-        [gh] + gq + normed + mixt,
-        [((chips * rows_w, width), b16), ((chips * rows_w, width), b16), ((pad, width), f32)],
-        flops=4 * total * every * width,
+        [marks[2], gh] + gq + normed + mixt,
+        [((chips * rows_w, width), b16), ((chips * rows_w, width), b16)],
+        cost=1.5,
+        far=(0,),
     )
     rows_all = both + pad + 16
     half = -(-rows_all // 32) * 16
     input_grad, b_own, b_sent = call(
         functools.partial(last_kernel, micros),
         [meta],
-        [tokens, gh, vectors, key_value, up_row, ffn_rows, router_rows] + normed + part + kept + arrived,
+        [tokens, gh, gain_one, key_value, up_row, ffn_rows] + normed + part + kept + arrived + chosen,
         [((micros, tok, width), f32), ((half, width), b16), ((half, width), b16)],
         [((2 * half, width), b16)],
-        flops=8 * total * width * both,
-    )
+        cost=3.8,
+    )
+
+    o_tile = 256
+    o_count = hidden_units // o_tile // 2
+    top_bit = log2(chips) - 1
+
+    def ordered(side, own, got, filled):
+        def block(which):
+            def index(j, meta):
+                place = jnp.where(meta[1] == which, meta[2], meta[3])
+                return j + ((place >> top_bit) ^ side) * o_count
+
+            return index
+
+        down_at, up_at = block(0), block(1)
+        near = pl.BlockSpec(own.shape, lambda j, meta: (0, 0))
+        return pl.pallas_call(
+            functools.partial(order_kernel, chunk, top_bit, side),
+            grid_spec=pltpu.PrefetchScalarGridSpec(
+                num_scalar_prefetch=1,
+                grid=(o_count,),
+                in_specs=[near, near] + [pl.BlockSpec(memory_space=pl.ANY)] * len(filled),
+                out_specs=[
+                    pl.BlockSpec((o_tile, width), lambda j, meta: (down_at(j, meta), 0)),
+                    pl.BlockSpec((width, o_tile), lambda j, meta: (0, up_at(j, meta))),
+                ],
+            ),
+            out_shape=[
+                jax.ShapeDtypeStruct((hidden_units, width), f32),
+                jax.ShapeDtypeStruct((width, hidden_units), f32),
+            ],
+            input_output_aliases={3 + i: i for i in range(len(filled))},
+            compiler_params=pltpu.CompilerParams(vmem_limit_bytes=16 * MIB),
+            cost_estimate=pl.CostEstimate(flops=0, bytes_accessed=hidden_units * width * 6, transcendentals=0),
+        )(meta, own, got, *filled)
 
     keep, got = w_own, flip(w_sent, "expert", 0)
     bundle = add(b_own, flip(b_sent, "expert", 0))
-    for ways in hops:
+    for up, (ways, back) in enumerate(zip(hops, hops[::-1])):
         count = keep.shape[0] // 2
         moving = jnp.concatenate([add(keep[count:], got[count:]), bundle], axis=0)
         keep = add(keep[:count], got[:count])
+        arrived_rows = hop(whole, back, groups, batch)
         moving = hop(moving, ways, groups, batch)
+        if up < len(hops) - 1:
+            whole = jnp.concatenate([whole, arrived_rows], axis=0)
         got = moving[:count]
         bundle = add(bundle, moving[count:])
+    own_low, own_high = whole, arrived_rows
+    got_low, got_high = flip(own_low, "expert", 0), flip(own_high, "expert", 0)
     weights = add(keep, got)
+    filled = ordered(0, own_low, got_low, ())
     for way in b_bits[::-1]:
         weights = jnp.concatenate([weights, flip(weights, *way)], axis=0)
 
@@ -668,28 +758,7 @@
     )
     grad_down_bias, grad_gain_two, grad_shift_two, grad_gain_one, grad_shift_one = rows
 
-    o_tile = 256
-
-    def full(shape):
-        return pl.BlockSpec(shape, lambda j, meta: (0,) * len(shape))
-
-    grad_down, grad_up = pl.pallas_call(
-        functools.partial(order_kernel, chunk),
-        grid_spec=pltpu.PrefetchScalarGridSpec(
-            num_scalar_prefetch=1,
-            grid=(hidden_units // o_tile,),
-            in_specs=[full(own_low.shape)] * 4,
-            out_specs=[
-                pl.BlockSpec((o_tile, width), lambda j, meta: (j, 0)),
-                pl.BlockSpec((width, o_tile), lambda j, meta: (0, j)),
-            ],
-        ),
-        out_shape=[
-            jax.ShapeDtypeStruct((hidden_units, width), f32),
-            jax.ShapeDtypeStruct((width, hidden_units), f32),
-        ],
-        compiler_params=pltpu.CompilerParams(vmem_limit_bytes=20 * MIB),
-    )(meta, own_low, own_high, got_low, got_high)
+    grad_down, grad_up = ordered(1, own_high, got_high, filled)
 
     return (
         block_out.reshape(micros, tok, width),

time: 191 us -> 180 us (0.942)
  local copies, waits for them, and re-layouts: 13.4 us -> 2.87 us
  starting transfers between devices: 44.9 us -> 36.1 us
  Pallas kernels: 55.3 us -> 59.6 us
  waiting for transfers between devices: 73.6 us -> 76.9 us
    ppermute x25, starting transfers between devices: 25.4 us -> 15.1 us  [flip(): return lax.ppermute(values, axis, [(i, i ^ 1 << bit) for i in range(size)])]
    unnamed x43 -> x65, local copies, waits for them, and re-layouts: 9.84 us -> 2.7 us
    ppermute x12, waiting for transfers between devices: 47.8 us -> 53.5 us  [hop(): return lax.ppermute(values, ('batch', 'expert'), pairs)]
    pallas_call x11, Pallas kernels: 55.3 us -> 59.6 us  [the longest x9 51.8 us: call(): pl.pallas_call(kernel, in_specs=[smem] * len(scalars) + [far_spec if i in...]
    another operation x6 -> x0, local copies, waits for them, and re-layouts: 3.44 us -> none  [shards(): jnp.stack([gain_one, shift_one, gain_two, shift_two, down_bias]).astype(f32)]
    ppermute x25, waiting for transfers between devices: 25.9 us -> 23.4 us  [flip(): return lax.ppermute(values, axis, [(i, i ^ 1 << bit) for i in range(size)])]
  transfers between devices with their start and end apart: 37 -> 37, of which waited for: 19 -> 21; matrix products, arithmetic and copies ran while one was open for 3% -> 2% of each run, Pallas kernels for 14% -> 19%
where the time goes in v3:
time: 180 us; the launch traced here: 179 us
  waiting for transfers between devices  76.9 us (43%)
  Pallas kernels  59.6 us (33%)
  starting transfers between devices  36.1 us (20%)
  local copies, waits for them, and re-layouts  2.87 us (2%)
  other arithmetic  2.83 us (2%)
    ppermute x12, waiting for transfers between devices, hop(): return lax.ppermute(values, ('batch', 'expert'), pairs)  53.5 us
    pallas_call x9, Pallas kernels, call(): pl.pallas_call(kernel, in_specs=[smem] * len(scalars) + [far_spec if i in...  51.8 us
    ppermute x25, waiting for transfers between devices, flip(): return lax.ppermute(values, axis, [(i, i ^ 1 << bit) for i in range(size)])  23.4 us
    ppermute x12, starting transfers between devices, hop(): return lax.ppermute(values, ('batch', 'expert'), pairs)  21 us
    ppermute x25, starting transfers between devices, flip(): return lax.ppermute(values, axis, [(i, i ^ 1 << bit) for i in range(size)])  15.1 us
    pallas_call x2, Pallas kernels, ordered(): pl.pallas_call(functools.partial(order_kernel, chunk, top_bit, side), gri...  7.79 us
  transfers between devices with their start and end apart: 37, of which 21 were waited for; matrix products, arithmetic and copies ran while one was open for 2% of the time, Pallas kernels for 19%

profile of v3, /device:TPU:0, one launch (start us, length us, event | category | flops | bytes accessed | tf_op | source)
XLA Modules:
  0.0 179.5 jit_solution(5974914449854768357)
XLA Ops:
  0.6 3.0 %collective-permute-start.3 = (bf16[192,512]{1,0:T(8,128)(2,1)}, bf16[192,512]{1,0:T(8,128)(2,1)S(1)}, u32[]{:S(2)}, u32[]{:S(2)}) collective-permute-start(bf16[192,512]{1,0:T(8,128)(2,1)} %bitcast.18), channel_id=1, source_target_pairs={{0,2},{1,3},{2,0},{3,1},{4,6},{5,7},{6,4},{7,5},{8,10},{9,11},{10,... | collective-permute-start | bytes 589832 | tf_op jit(solution)/shard_map/ppermute | solution.py:27
  3.7 2.5 %shard_map.263 = (bf16[512,512]{1,0:T(8,128)(2,1)S(1)}, bf16[512,512]{1,0:T(8,128)(2,1)S(1)}, bf16[512,128]{1,0:T(8,128)(2,1)S(1)}, bf16[512,128]{1,0:T(8,128)(2...) custom-call(bf16[2,512,512]{2,1,0:T(8,128)(2,1)} %refs_1_.5, bf16[512,128]{1,0:T(8,128)(2,1)} %refs_4_.5, ...), custom_call_target="tpu_custom_call" | custom-call | flops 2640000000 | tf_op jit(solution)/shard_map/pallas_call | solution.py:562
  6.3 2.9 %collective-permute-done.3.refs_9_.refs_11_ = bf16[192,512]{1,0:T(8,128)(2,1)S(1)} collective-permute-done((bf16[192,512]{1,0:T(8,128)(2,1)}, bf16[192,512]{1,0:T(8,128)(2,1)S(1)}, u32[]{:S(2)}, u32[]{:S(2)}) %collective-permute-start.3) | collective-permute-done | bytes 196640 | tf_op jit(solution)/shard_map/ppermute | solution.py:27
  9.3 0.5 collective-permute-start.1
  9.8 1.8 collective-permute-done.refs_5_
  11.6 1.8 %collective-permute-start.9 = (bf16[192,512]{1,0:T(8,128)(2,1)S(1)}, bf16[192,512]{1,0:T(8,128)(2,1)S(1)}, u32[]{:S(2)}, u32[]{:S(2)}) collective-permute-start(bf16[192,512]{1,0:T(8,128)(2,1)S(1)} %bitcast.24), channel_id=1, source_target_pairs={{0,2},{1,3},{2,0},{3,1},{4,6},{5,7},{6,4},{7,5},{8,10},{9,11},{10,... | collective-permute-start | bytes 589832 | tf_op jit(solution)/shard_map/ppermute | solution.py:27
  13.4 0.5 broadcast.205
  13.9 0.7 reduce.3
  15.9 4.9 %shard_map.264 = (bf16[2048,128]{1,0:T(8,128)(2,1)S(1)}, bf16[128,2048]{1,0:T(8,128)(2,1)S(1)}, bf16[2,64,768]{2,1,0:T(8,128)(2,1)S(1)}, f32[2,64,768]{2,1,0:T(8...) custom-call(s32[28]{0:T(128)S(1)} %concatenate.37.refs_0_.meta, ...), custom_call_target="tpu_custom_call" | custom-call | flops 5500000256 | tf_op jit(solution)/shard_map/pallas_call | solution.py:562
  20.8 0.9 collective-permute-done.6.refs_5_
  23.2 0.5 copy-done.30
  23.9 5.4 %shard_map.265 = (bf16[2048,128]{1,0:T(8,128)(2,1)S(1)}, bf16[128,2048]{1,0:T(8,128)(2,1)S(1)}, bf16[2,64,768]{2,1,0:T(8,128)(2,1)S(1)}, f32[2,64,768]{2,1,0:T(8...) custom-call(s32[28]{0:T(128)S(1)} %concatenate.37.refs_0_.meta, ...), custom_call_target="tpu_custom_call" | custom-call | flops 5500000256 | tf_op jit(solution)/shard_map/pallas_call | solution.py:562
  29.4 21.3 %shard_map.266 = (bf16[1024,512]{1,0:T(8,128)(2,1)}, f32[1024,512]{1,0:T(8,128)S(1)}, bf16[2048,512]{1,0:T(8,128)(2,1)S(1)}, bf16[2048,512]{1,0:T(8,128)(2,1)S(1...) custom-call(s32[28]{0:T(128)S(1)} %concatenate.37.refs_0_.meta, bf16[2,512,512]{2,1,0:T(8,128)(2,1)S(1)} %copy-done.3, ...), custom_call_target="tpu_custom_call" | custom-call | flops 12099999744 | tf_op jit(solution)/shard_map/pallas_call | solution.py:562
  50.7 1.4 collective-permute-start.16
  52.1 3.7 %collective-permute-done.16 = bf16[2048,512]{1,0:T(8,128)(2,1)S(1)} collective-permute-done((bf16[2048,512]{1,0:T(8,128)(2,1)S(1)}, bf16[2048,512]{1,0:T(8,128)(2,1)S(1)}, u32[]{:S(2)}, u32[]{:S(2)}) %collective-permute-start.16) | collective-permute-done | bytes 2097184 | tf_op jit(solution)/shard_map/ppermute | solution.py:27
  55.9 0.6 add_convert_fusion.1
  56.5 9.9 %collective-permute-start.17 = (bf16[1024,512]{1,0:T(8,128)(2,1)S(1)}, bf16[1024,512]{1,0:T(8,128)(2,1)S(1)}, u32[]{:S(2)}, u32[]{:S(2)}) collective-permute-start(bf16[1024,512]{1,0:T(8,128)(2,1)S(1)} %get-tuple-element.125), channel_id=1, source_target_pairs={{0,2},{1,5},{2,0},{3,7},{4,6},{5,1},{6,4},{7,3},{8,10},{9,13},{10,... | collective-permute-start | bytes 3145736 | tf_op jit(solution)/shard_map/ppermute | solution.py:37
  66.5 4.9 %shard_map.268 = (f32[512,512]{1,0:T(8,128)S(1)}, bf16[2,512,128]{2,1,0:T(8,128)(2,1)S(1)}, bf16[2,512,128]{2,1,0:T(8,128)(2,1)S(1)}, bf16[768,512]{1,0:T(8,128)...) custom-call(s32[28]{0:T(128)S(1)} %concatenate.37.refs_0_.meta, ...), custom_call_target="tpu_custom_call" | custom-call | flops 9900000256 | tf_op jit(solution)/shard_map/pallas_call | solution.py:562
  71.5 7.6 %collective-permute-done.17 = bf16[1024,512]{1,0:T(8,128)(2,1)S(1)} collective-permute-done((bf16[1024,512]{1,0:T(8,128)(2,1)S(1)}, bf16[1024,512]{1,0:T(8,128)(2,1)S(1)}, u32[]{:S(2)}, u32[]{:S(2)}) %collective-permute-start.17) | collective-permute-done | bytes 1048608 | tf_op jit(solution)/shard_map/ppermute | solution.py:37
  79.5 1.0 collective-permute-start.18
  80.5 5.0 %shard_map.267 = (f32[512,512]{1,0:T(8,128)S(1)}, bf16[2,512,128]{2,1,0:T(8,128)(2,1)S(1)}, bf16[2,512,128]{2,1,0:T(8,128)(2,1)S(1)}, bf16[768,512]{1,0:T(8,128)...) custom-call(s32[28]{0:T(128)S(1)} %concatenate.37.refs_0_.meta, ...), custom_call_target="tpu_custom_call" | custom-call | flops 9900000256 | tf_op jit(solution)/shard_map/pallas_call | solution.py:562
  85.5 3.2 %collective-permute-done.18 = bf16[512,512]{1,0:T(8,128)(2,1)S(1)} collective-permute-done((bf16[512,512]{1,0:T(8,128)(2,1)S(1)}, bf16[512,512]{1,0:T(8,128)(2,1)S(1)}, u32[]{:S(2)}, u32[]{:S(2)}) %collective-permute-start.18) | collective-permute-done | bytes 524320 | tf_op jit(solution)/shard_map/ppermute | solution.py:37
  88.8 0.8 collective-permute-start.19
  89.7 4.6 %collective-permute-start.15 = (bf16[1,512,128]{2,1,0:T(8,128)(2,1)S(1)}, bf16[1,512,128]{2,1,0:T(8,128)(2,1)S(1)}, u32[]{:S(2)}, u32[]{:S(2)}) collective-permute-start(bf16[1,512,128]{2,1,0:T(8,128)(2,1)S(1)} %get-tuple-element.134), channel_id=1, source_target_pairs={{0,2},{1,3},{2,0},{3,1},{4,6},{5,7},{6,4},{7,5},{8,10},{9,11},{10,... | collective-permute-start | bytes 393224 | tf_op jit(solution)/shard_map/ppermute | solution.py:27
  94.5 0.8 collective-permute-done.19.refs_1_
  95.3 0.7 copy-done.22
  96.0 2.4 %shard_map.270 = (bf16[768,512]{1,0:T(8,128)(2,1)S(1)}, bf16[768,512]{1,0:T(8,128)(2,1)S(1)}) custom-call(s32[4,8]{1,0:T(4,128)S(1)} %select_select_fusion.refs_0_, bf16[256,512]{1,0:T(8,128)(2,1)} %copy-done.22, f32[1024,512]{1,0:T(8,128)S(1)} %get-tuple-element.81.refs_1_.refs_2_, bf16[768,512]{1,0:T(8,128)(2,1)S(1)} %get-tuple-element.104.refs_3_, ...), custom_call_target="tpu_custom_call" | custom-call | flops 1650000000 | tf_op jit(solution)/shard_map/pallas_call | solution.py:562
  98.4 1.2 collective-permute-start.20
  99.6 1.9 %collective-permute-done.14.refs_13_ = bf16[1,512,128]{2,1,0:T(8,128)(2,1)S(1)} collective-permute-done((bf16[1,512,128]{2,1,0:T(8,128)(2,1)S(1)}, bf16[1,512,128]{2,1,0:T(8,128)(2,1)S(1)}, u32[]{:S(2)}, u32[]{:S(2)}) %collective-permute-start.14) | collective-permute-done | bytes 131104 | tf_op jit(solution)/shard_map/ppermute | solution.py:27
  101.5 3.9 %shard_map.269 = (f32[2,512,512]{2,1,0:T(8,128)}, bf16[80,512]{1,0:T(8,128)(2,1)S(1)}, bf16[80,512]{1,0:T(8,128)(2,1)S(1)}) custom-call(s32[28]{0:T(128)S(1)} %concatenate.37.refs_0_.meta, bf16[2,512,512]{2,1,0:T(8,128)(2,1)S(1)} %copy-done.3, f32[1024,512]{1,0:T(8,128)S(1)} %get-tuple-element.81.refs_1_.refs_2_, bf16[512]{0:T(512)(128)(2,1)S(1)} %copy-done.21, ...), custom_call_target="tpu_custom_call" | custom-call | flops 4180000000 | tf_op jit(solution)/shard_map/pallas_call | solution.py:562
  105.6 3.5 %collective-permute-start.30 = (bf16[128,512]{1,0:T(8,128)(2,1)S(1)}, bf16[128,512]{1,0:T(8,128)(2,1)S(1)}, u32[]{:S(2)}, u32[]{:S(2)}) collective-permute-start(bf16[128,512]{1,0:T(8,128)(2,1)S(1)} %add_convert_fusion.11), channel_id=1, source_target_pairs={{0,16},{1,17},{2,18},{3,19},{4,20},{5,21},{6,22},{7,23},{8,24},{9,... | collective-permute-start | bytes 393224 | tf_op jit(solution)/shard_map/ppermute | solution.py:37
  109.1 6.8 %collective-permute-done.30 = bf16[128,512]{1,0:T(8,128)(2,1)S(1)} collective-permute-done((bf16[128,512]{1,0:T(8,128)(2,1)S(1)}, bf16[128,512]{1,0:T(8,128)(2,1)S(1)}, u32[]{:S(2)}, u32[]{:S(2)}) %collective-permute-start.30) | collective-permute-done | bytes 131104 | tf_op jit(solution)/shard_map/ppermute | solution.py:37
  116.3 1.5 collective-permute-start.22
  117.8 6.8 %collective-permute-done.31 = bf16[128,512]{1,0:T(8,128)(2,1)S(1)} collective-permute-done((bf16[128,512]{1,0:T(8,128)(2,1)S(1)}, bf16[128,512]{1,0:T(8,128)(2,1)S(1)}, u32[]{:S(2)}, u32[]{:S(2)}) %collective-permute-start.31) | collective-permute-done | bytes 131104 | tf_op jit(solution)/shard_map/ppermute | solution.py:37
  124.7 6.4 %collective-permute-done.32 = bf16[256,512]{1,0:T(8,128)(2,1)S(1)} collective-permute-done((bf16[256,512]{1,0:T(8,128)(2,1)S(1)}, bf16[256,512]{1,0:T(8,128)(2,1)S(1)}, u32[]{:S(2)}, u32[]{:S(2)}) %collective-permute-start.32) | collective-permute-done | bytes 262176 | tf_op jit(solution)/shard_map/ppermute | solution.py:37
  131.6 1.8 %collective-permute-start.23 = (bf16[272,512]{1,0:T(8,128)(2,1)S(1)}, bf16[272,512]{1,0:T(8,128)(2,1)S(1)}, u32[]{:S(2)}, u32[]{:S(2)}) collective-permute-start(bf16[272,512]{1,0:T(8,128)(2,1)S(1)} %pad_maximum_fusion.4), channel_id=1, source_target_pairs={{0,4},{1,9},{2,6},{3,11},{4,0},{5,13},{6,2},{7,15},{8,12},{9,1},{1... | collective-permute-start | bytes 835592 | tf_op jit(solution)/shard_map/ppermute | solution.py:37
  133.4 6.9 %collective-permute-done.33 = bf16[512,512]{1,0:T(8,128)(2,1)S(1)} collective-permute-done((bf16[512,512]{1,0:T(8,128)(2,1)S(1)}, bf16[512,512]{1,0:T(8,128)(2,1)S(1)}, u32[]{:S(2)}, u32[]{:S(2)}) %collective-permute-start.33) | collective-permute-done | bytes 524320 | tf_op jit(solution)/shard_map/ppermute | solution.py:37
  140.4 1.6 collective-permute-start.34
  142.0 3.2 %collective-permute-done.23 = bf16[272,512]{1,0:T(8,128)(2,1)S(1)} collective-permute-done((bf16[272,512]{1,0:T(8,128)(2,1)S(1)}, bf16[272,512]{1,0:T(8,128)(2,1)S(1)}, u32[]{:S(2)}, u32[]{:S(2)}) %collective-permute-start.23) | collective-permute-done | bytes 278560 | tf_op jit(solution)/shard_map/ppermute | solution.py:37
  145.5 5.4 %collective-permute-done.24 = bf16[176,512]{1,0:T(8,128)(2,1)S(1)} collective-permute-done((bf16[176,512]{1,0:T(8,128)(2,1)S(1)}, bf16[176,512]{1,0:T(8,128)(2,1)S(1)}, u32[]{:S(2)}, u32[]{:S(2)}) %collective-permute-start.24) | collective-permute-done | bytes 180256 | tf_op jit(solution)/shard_map/ppermute | solution.py:37
  151.2 6.0 %collective-permute-done.34.own = bf16[1024,512]{1,0:T(8,128)(2,1)S(1)} collective-permute-done((bf16[1024,512]{1,0:T(8,128)(2,1)S(1)}, bf16[1024,512]{1,0:T(8,128)(2,1)S(1)}, u32[]{:S(2)}, u32[]{:S(2)}) %collective-permute-start.34) | collective-permute-done | bytes 1048608 | tf_op jit(solution)/shard_map/ppermute | solution.py:37
  157.2 0.5 collective-permute-done.25
  157.8 5.0 %collective-permute-done.26 = bf16[48,512]{1,0:T(8,128)(2,1)S(1)} collective-permute-done((bf16[48,512]{1,0:T(8,128)(2,1)S(1)}, bf16[48,512]{1,0:T(8,128)(2,1)S(1)}, u32[]{:S(2)}, u32[]{:S(2)}) %collective-permute-start.26) | collective-permute-done | bytes 49184 | tf_op jit(solution)/shard_map/ppermute | solution.py:27
  163.0 4.6 %collective-permute-done.27 = bf16[96,512]{1,0:T(8,128)(2,1)S(1)} collective-permute-done((bf16[96,512]{1,0:T(8,128)(2,1)S(1)}, bf16[96,512]{1,0:T(8,128)(2,1)S(1)}, u32[]{:S(2)}, u32[]{:S(2)}) %collective-permute-start.27) | collective-permute-done | bytes 98336 | tf_op jit(solution)/shard_map/ppermute | solution.py:27
  168.0 3.3 %shard_map.272 = (f32[2048,512]{1,0:T(8,128)}, f32[512,2048]{1,0:T(8,128)}) custom-call(s32[28]{0:T(128)S(1)} %concatenate.37.refs_0_.meta, bf16[1024,512]{1,0:T(8,128)(2,1)S(1)} %pad_maximum_fusion.own, bf16[1024,512]{1,0:T(8,128)(2,1)S(1)} %collective-permute-done.36.got), custom_call_target="tpu_custom_call" | custom-call | bytes 6291456 | tf_op jit(solution)/shard_map/pallas_call | solution.py:710
  171.3 2.0 %collective-permute-done.28 = bf16[192,512]{1,0:T(8,128)(2,1)S(1)} collective-permute-done((bf16[192,512]{1,0:T(8,128)(2,1)S(1)}, bf16[192,512]{1,0:T(8,128)(2,1)S(1)}, u32[]{:S(2)}, u32[]{:S(2)}) %collective-permute-start.28) | collective-permute-done | bytes 196640 | tf_op jit(solution)/shard_map/ppermute | solution.py:27
  173.3 1.6 shard_map.271
  175.0 4.5 %shard_map.273 = (f32[2048,512]{1,0:T(8,128)}, f32[512,2048]{1,0:T(8,128)}) custom-call(s32[28]{0:T(128)S(1)} %concatenate.37.refs_0_.meta, bf16[1024,512]{1,0:T(8,128)(2,1)S(1)} %collective-permute-done.34.own, bf16[1024,512]{1,0:T(8,128)(2,1)} %collective-permute-done.35.got, ...), custom_call_target="tpu_custom_call", output_to_operand_aliasing={{0}: (3, {}), {1}: (4, {})} | custom-call | bytes 6291456 | tf_op jit(solution)/shard_map/pallas_call | solution.py:710
  (140 shorter events, 6.6 us)
Async XLA Ops:
  0.6 8.6 %collective-permute-start.3 = (bf16[192,512]{1,0:T(8,128)(2,1)}, bf16[192,512]{1,0:T(8,128)(2,1)S(1)}, u32[]{:S(2)}, u32[]{:S(2)}) collective-permute-start(bf16[192,512]{1,0:T(8,128)(2,1)} %bitcast.18), channel_id=1, source_target_pairs={{0,2},{1,3},{2,0},{3,1},{4,6},{5,7},{6,4},{7,5},{8,10},{9,11},{10,... | collective-permute-start | bytes 589832 | tf_op jit(solution)/shard_map/ppermute | solution.py:27
  3.7 7.9 %copy-start.6 = (bf16[3,64,512]{2,1,0:T(8,128)(2,1)S(1)}, bf16[3,64,512]{2,1,0:T(8,128)(2,1)}, u32[]{:S(2)}) copy-start(bf16[3,64,512]{2,1,0:T(8,128)(2,1)} %param.24) | copy-start | bytes 589828
  3.7 10.2 %copy-start.25 = (s32[2,1,8]{2,1,0:T(1,128)S(1)}, s32[2,1,8]{2,1,0:T(1,128)}, u32[]{:S(2)}) copy-start(s32[2,1,8]{2,1,0:T(1,128)} %param.18) | copy-start | bytes 196
  6.1 9.0 %copy-start.15 = (bf16[512,128]{1,0:T(8,128)(2,1)}, bf16[512,128]{1,0:T(8,128)(2,1)S(1)}, u32[]{:S(2)}) copy-start(bf16[512,128]{1,0:T(8,128)(2,1)S(1)} %get-tuple-element.71.refs_4_) | copy-start | bytes 393220
  6.1 15.6 %copy-start.14 = (bf16[512,128]{1,0:T(8,128)(2,1)}, bf16[512,128]{1,0:T(8,128)(2,1)S(1)}, u32[]{:S(2)}) copy-start(bf16[512,128]{1,0:T(8,128)(2,1)S(1)} %get-tuple-element.77.refs_4_) | copy-start | bytes 393220
  6.2 5.4 %collective-permute-start = (bf16[512,128]{1,0:T(8,128)(2,1)S(1)}, bf16[512,128]{1,0:T(8,128)(2,1)S(1)}, u32[]{:S(2)}, u32[]{:S(2)}) collective-permute-start(bf16[512,128]{1,0:T(8,128)(2,1)S(1)} %get-tuple-element.71.refs_4_), channel_id=1, source_target_pairs={{0,2},{1,3},{2,0},{3,1},{4,6},{5,7},{6,4},{7,5},{8,10},{9,11},{10,... | collective-permute-start | bytes 393224 | tf_op jit(solution)/shard_map/ppermute | solution.py:27
  6.3 8.8 %collective-permute-start.4 = (bf16[192,512]{1,0:T(8,128)(2,1)S(1)}, bf16[192,512]{1,0:T(8,128)(2,1)S(1)}, u32[]{:S(2)}, u32[]{:S(2)}) collective-permute-start(bf16[192,512]{1,0:T(8,128)(2,1)S(1)} %bitcast.21), channel_id=1, source_target_pairs={{0,1},{1,0},{2,3},{3,2},{4,5},{5,4},{6,7},{7,6},{8,9},{9,8},{10,11... | collective-permute-start | bytes 589832 | tf_op jit(solution)/shard_map/ppermute | solution.py:27
  9.3 5.9 %collective-permute-start.5 = (bf16[192,512]{1,0:T(8,128)(2,1)S(1)}, bf16[192,512]{1,0:T(8,128)(2,1)S(1)}, u32[]{:S(2)}, u32[]{:S(2)}) collective-permute-start(bf16[192,512]{1,0:T(8,128)(2,1)S(1)} %collective-permute-done.3.refs_9_.refs_11_), channel_id=1, source_target_pairs={{0,1},{1,0},{2,3},{3,2},{4,5},{5,4},{6,7},{7,6},{8,9},{9,8},{10,11... | collective-permute-start | bytes 589832 | tf_op jit(solution)/shard_map/ppermute | solution.py:27
  9.3 5.5 %collective-permute-start.1 = (bf16[512,128]{1,0:T(8,128)(2,1)S(1)}, bf16[512,128]{1,0:T(8,128)(2,1)S(1)}, u32[]{:S(2)}, u32[]{:S(2)}) collective-permute-start(bf16[512,128]{1,0:T(8,128)(2,1)S(1)} %get-tuple-element.71.refs_4_), channel_id=1, source_target_pairs={{0,1},{1,0},{2,3},{3,2},{4,5},{5,4},{6,7},{7,6},{8,9},{9,8},{10,11... | collective-permute-start | bytes 393224 | tf_op jit(solution)/shard_map/ppermute | solution.py:27
  11.6 3.5 %collective-permute-start.2 = (bf16[512,128]{1,0:T(8,128)(2,1)S(1)}, bf16[512,128]{1,0:T(8,128)(2,1)S(1)}, u32[]{:S(2)}, u32[]{:S(2)}) collective-permute-start(bf16[512,128]{1,0:T(8,128)(2,1)S(1)} %collective-permute-done.refs_5_), channel_id=1, source_target_pairs={{0,1},{1,0},{2,3},{3,2},{4,5},{5,4},{6,7},{7,6},{8,9},{9,8},{10,11... | collective-permute-start | bytes 393224 | tf_op jit(solution)/shard_map/ppermute | solution.py:27
  11.6 10.8 %collective-permute-start.9 = (bf16[192,512]{1,0:T(8,128)(2,1)S(1)}, bf16[192,512]{1,0:T(8,128)(2,1)S(1)}, u32[]{:S(2)}, u32[]{:S(2)}) collective-permute-start(bf16[192,512]{1,0:T(8,128)(2,1)S(1)} %bitcast.24), channel_id=1, source_target_pairs={{0,2},{1,3},{2,0},{3,1},{4,6},{5,7},{6,4},{7,5},{8,10},{9,11},{10,... | collective-permute-start | bytes 589832 | tf_op jit(solution)/shard_map/ppermute | solution.py:27
  14.8 7.0 %collective-permute-start.6 = (bf16[512,128]{1,0:T(8,128)(2,1)S(1)}, bf16[512,128]{1,0:T(8,128)(2,1)S(1)}, u32[]{:S(2)}, u32[]{:S(2)}) collective-permute-start(bf16[512,128]{1,0:T(8,128)(2,1)S(1)} %get-tuple-element.77.refs_4_), channel_id=1, source_target_pairs={{0,2},{1,3},{2,0},{3,1},{4,6},{5,7},{6,4},{7,5},{8,10},{9,11},{10,... | collective-permute-start | bytes 393224 | tf_op jit(solution)/shard_map/ppermute | solution.py:27
  15.9 6.5 %copy-start.24 = (bf16[2048]{0:T(1024)(128)(2,1)S(1)}, bf16[2048]{0:T(1024)(128)(2,1)}, u32[]{:S(2)}) copy-start(bf16[2048]{0:T(1024)(128)(2,1)} %param.28) | copy-start | bytes 12292
  21.7 1.3 collective-permute-start.7
  21.8 1.4 collective-permute-start.8
  22.2 7.1 %collective-permute-start.10 = (bf16[192,512]{1,0:T(8,128)(2,1)S(1)}, bf16[192,512]{1,0:T(8,128)(2,1)S(1)}, u32[]{:S(2)}, u32[]{:S(2)}) collective-permute-start(bf16[192,512]{1,0:T(8,128)(2,1)S(1)} %bitcast.25), channel_id=1, source_target_pairs={{0,1},{1,0},{2,3},{3,2},{4,5},{5,4},{6,7},{7,6},{8,9},{9,8},{10,11... | collective-permute-start | bytes 589832 | tf_op jit(solution)/shard_map/ppermute | solution.py:27
  22.4 7.0 %collective-permute-start.11 = (bf16[192,512]{1,0:T(8,128)(2,1)S(1)}, bf16[192,512]{1,0:T(8,128)(2,1)S(1)}, u32[]{:S(2)}, u32[]{:S(2)}) collective-permute-start(bf16[192,512]{1,0:T(8,128)(2,1)S(1)} %collective-permute-done.9.refs_12_.refs_15_), channel_id=1, source_target_pairs={{0,1},{1,0},{2,3},{3,2},{4,5},{5,4},{6,7},{7,6},{8,9},{9,8},{10,11... | collective-permute-start | bytes 589832 | tf_op jit(solution)/shard_map/ppermute | solution.py:27
  50.7 5.2 %collective-permute-start.16 = (bf16[2048,512]{1,0:T(8,128)(2,1)S(1)}, bf16[2048,512]{1,0:T(8,128)(2,1)S(1)}, u32[]{:S(2)}, u32[]{:S(2)}) collective-permute-start(bf16[2048,512]{1,0:T(8,128)(2,1)S(1)} %get-tuple-element.103), channel_id=1, source_target_pairs={{0,1},{1,0},{2,3},{3,2},{4,5},{5,4},{6,7},{7,6},{8,9},{9,8},{10,11... | collective-permute-start | bytes 6291464 | tf_op jit(solution)/shard_map/ppermute | solution.py:27
  55.9 10.6 %copy-start.5 = (bf16[3,512,64]{1,2,0:T(8,128)(2,1)S(1)}, bf16[3,512,64]{1,2,0:T(8,128)(2,1)}, u32[]{:S(2)}) copy-start(bf16[3,512,64]{1,2,0:T(8,128)(2,1)} %param.23) | copy-start | bytes 589828
  55.9 10.6 %copy-start.8 = (bf16[192,512]{1,0:T(8,128)(2,1)S(1)}, bf16[192,512]{1,0:T(8,128)(2,1)}, u32[]{:S(2)}) copy-start(bf16[192,512]{1,0:T(8,128)(2,1)} %copy-done.7) | copy-start | bytes 589828
  55.9 10.6 %copy-start.10 = (bf16[192,512]{1,0:T(8,128)(2,1)S(1)}, bf16[192,512]{1,0:T(8,128)(2,1)}, u32[]{:S(2)}) copy-start(bf16[192,512]{1,0:T(8,128)(2,1)} %copy-done.9) | copy-start | bytes 589828
  55.9 10.6 %copy-start.12 = (bf16[192,512]{1,0:T(8,128)(2,1)S(1)}, bf16[192,512]{1,0:T(8,128)(2,1)}, u32[]{:S(2)}) copy-start(bf16[192,512]{1,0:T(8,128)(2,1)} %copy-done.11) | copy-start | bytes 589828
  55.9 10.6 %copy-start.16 = (bf16[512,12]{0,1:T(8,128)(2,1)S(1)}, bf16[512,12]{0,1:T(8,128)(2,1)}, u32[]{:S(2)}) copy-start(bf16[512,12]{0,1:T(8,128)(2,1)} %param.21) | copy-start | bytes 36868
  55.9 10.6 %copy-start.17 = (s32[2,512,3]{1,0,2:T(2,128)S(1)}, s32[2,512,3]{1,0,2:T(2,128)}, u32[]{:S(2)}) copy-start(s32[2,512,3]{1,0,2:T(2,128)} %param.17) | copy-start | bytes 36868
  56.5 22.7 %collective-permute-start.17 = (bf16[1024,512]{1,0:T(8,128)(2,1)S(1)}, bf16[1024,512]{1,0:T(8,128)(2,1)S(1)}, u32[]{:S(2)}, u32[]{:S(2)}) collective-permute-start(bf16[1024,512]{1,0:T(8,128)(2,1)S(1)} %get-tuple-element.125), channel_id=1, source_target_pairs={{0,2},{1,5},{2,0},{3,7},{4,6},{5,1},{6,4},{7,3},{8,10},{9,13},{10,... | collective-permute-start | bytes 3145736 | tf_op jit(solution)/shard_map/ppermute | solution.py:37
  71.5 18.2 %collective-permute-start.13 = (bf16[2,512,128]{2,1,0:T(8,128)(2,1)S(1)}, bf16[2,512,128]{2,1,0:T(8,128)(2,1)S(1)}, u32[]{:S(2)}, u32[]{:S(2)}) collective-permute-start(bf16[2,512,128]{2,1,0:T(8,128)(2,1)S(1)} %get-tuple-element.98), channel_id=1, source_target_pairs={{0,1},{1,0},{2,3},{3,2},{4,5},{5,4},{6,7},{7,6},{8,9},{9,8},{10,11... | collective-permute-start | bytes 786440 | tf_op jit(solution)/shard_map/ppermute | solution.py:27
  79.5 9.2 %collective-permute-start.18 = (bf16[512,512]{1,0:T(8,128)(2,1)S(1)}, bf16[512,512]{1,0:T(8,128)(2,1)S(1)}, u32[]{:S(2)}, u32[]{:S(2)}) collective-permute-start(bf16[512,512]{1,0:T(8,128)(2,1)S(1)} %get-tuple-element.127), channel_id=1, source_target_pairs={{0,4},{1,9},{2,6},{3,11},{4,0},{5,13},{6,2},{7,15},{8,12},{9,1},{1... | collective-permute-start | bytes 1572872 | tf_op jit(solution)/shard_map/ppermute | solution.py:37
  85.4 8.9 %collective-permute-start.12 = (bf16[2,512,128]{2,1,0:T(8,128)(2,1)S(1)}, bf16[2,512,128]{2,1,0:T(8,128)(2,1)S(1)}, u32[]{:S(2)}, u32[]{:S(2)}) collective-permute-start(bf16[2,512,128]{2,1,0:T(8,128)(2,1)S(1)} %get-tuple-element.96), channel_id=1, source_target_pairs={{0,1},{1,0},{2,3},{3,2},{4,5},{5,4},{6,7},{7,6},{8,9},{9,8},{10,11... | collective-permute-start | bytes 786440 | tf_op jit(solution)/shard_map/ppermute | solution.py:27
  88.8 6.4 %collective-permute-start.19 = (bf16[256,512]{1,0:T(8,128)(2,1)S(1)}, bf16[256,512]{1,0:T(8,128)(2,1)S(1)}, u32[]{:S(2)}, u32[]{:S(2)}) collective-permute-start(bf16[256,512]{1,0:T(8,128)(2,1)S(1)} %get-tuple-element.131), channel_id=1, source_target_pairs={{0,8},{1,3},{2,10},{3,1},{4,12},{5,7},{6,14},{7,5},{8,0},{9,11},{1... | collective-permute-start | bytes 786440 | tf_op jit(solution)/shard_map/ppermute | solution.py:37
  89.7 9.9 %collective-permute-start.15 = (bf16[1,512,128]{2,1,0:T(8,128)(2,1)S(1)}, bf16[1,512,128]{2,1,0:T(8,128)(2,1)S(1)}, u32[]{:S(2)}, u32[]{:S(2)}) collective-permute-start(bf16[1,512,128]{2,1,0:T(8,128)(2,1)S(1)} %get-tuple-element.134), channel_id=1, source_target_pairs={{0,2},{1,3},{2,0},{3,1},{4,6},{5,7},{6,4},{7,5},{8,10},{9,11},{10,... | collective-permute-start | bytes 393224 | tf_op jit(solution)/shard_map/ppermute | solution.py:27
  94.4 7.1 %collective-permute-start.14 = (bf16[1,512,128]{2,1,0:T(8,128)(2,1)S(1)}, bf16[1,512,128]{2,1,0:T(8,128)(2,1)S(1)}, u32[]{:S(2)}, u32[]{:S(2)}) collective-permute-start(bf16[1,512,128]{2,1,0:T(8,128)(2,1)S(1)} %get-tuple-element.136), channel_id=1, source_target_pairs={{0,2},{1,3},{2,0},{3,1},{4,6},{5,7},{6,4},{7,5},{8,10},{9,11},{10,... | collective-permute-start | bytes 393224 | tf_op jit(solution)/shard_map/ppermute | solution.py:27
  98.4 17.6 %collective-permute-start.20 = (bf16[768,512]{1,0:T(8,128)(2,1)S(1)}, bf16[768,512]{1,0:T(8,128)(2,1)S(1)}, u32[]{:S(2)}, u32[]{:S(2)}) collective-permute-start(bf16[768,512]{1,0:T(8,128)(2,1)S(1)} %get-tuple-element.107), channel_id=1, source_target_pairs={{0,1},{1,0},{2,3},{3,2},{4,5},{5,4},{6,7},{7,6},{8,9},{9,8},{10,11... | collective-permute-start | bytes 2359304 | tf_op jit(solution)/shard_map/ppermute | solution.py:27
  105.4 3.7 %collective-permute-start.21 = (bf16[80,512]{1,0:T(8,128)(2,1)S(1)}, bf16[80,512]{1,0:T(8,128)(2,1)S(1)}, u32[]{:S(2)}, u32[]{:S(2)}) collective-permute-start(bf16[80,512]{1,0:T(8,128)(2,1)S(1)} %get-tuple-element.109), channel_id=1, source_target_pairs={{0,1},{1,0},{2,3},{3,2},{4,5},{5,4},{6,7},{7,6},{8,9},{9,8},{10,11... | collective-permute-start | bytes 245768 | tf_op jit(solution)/shard_map/ppermute | solution.py:27
  105.6 10.3 %collective-permute-start.30 = (bf16[128,512]{1,0:T(8,128)(2,1)S(1)}, bf16[128,512]{1,0:T(8,128)(2,1)S(1)}, u32[]{:S(2)}, u32[]{:S(2)}) collective-permute-start(bf16[128,512]{1,0:T(8,128)(2,1)S(1)} %add_convert_fusion.11), channel_id=1, source_target_pairs={{0,16},{1,17},{2,18},{3,19},{4,20},{5,21},{6,22},{7,23},{8,24},{9,... | collective-permute-start | bytes 393224 | tf_op jit(solution)/shard_map/ppermute | solution.py:37
  116.0 8.6 %collective-permute-start.31 = (bf16[128,512]{1,0:T(8,128)(2,1)S(1)}, bf16[128,512]{1,0:T(8,128)(2,1)S(1)}, u32[]{:S(2)}, u32[]{:S(2)}) collective-permute-start(bf16[128,512]{1,0:T(8,128)(2,1)S(1)} %add_convert_fusion.10), channel_id=1, source_target_pairs={{0,16},{1,17},{2,18},{3,19},{4,20},{5,21},{6,22},{7,23},{8,24},{9,... | collective-permute-start | bytes 393224 | tf_op jit(solution)/shard_map/ppermute | solution.py:37
  116.3 15.1 %collective-permute-start.22 = (bf16[464,512]{1,0:T(8,128)(2,1)S(1)}, bf16[464,512]{1,0:T(8,128)(2,1)S(1)}, u32[]{:S(2)}, u32[]{:S(2)}) collective-permute-start(bf16[464,512]{1,0:T(8,128)(2,1)S(1)} %pad_maximum_fusion.2), channel_id=1, source_target_pairs={{0,2},{1,5},{2,0},{3,7},{4,6},{5,1},{6,4},{7,3},{8,10},{9,13},{10,... | collective-permute-start | bytes 1425416 | tf_op jit(solution)/shard_map/ppermute | solution.py:37
  124.6 6.4 %collective-permute-start.32 = (bf16[256,512]{1,0:T(8,128)(2,1)S(1)}, bf16[256,512]{1,0:T(8,128)(2,1)S(1)}, u32[]{:S(2)}, u32[]{:S(2)}) collective-permute-start(bf16[256,512]{1,0:T(8,128)(2,1)S(1)} %pad_maximum_fusion.5), channel_id=1, source_target_pairs={{0,8},{1,3},{2,10},{3,1},{4,12},{5,7},{6,14},{7,5},{8,0},{9,11},{1... | collective-permute-start | bytes 786440 | tf_op jit(solution)/shard_map/ppermute | solution.py:37
  131.1 9.2 %collective-permute-start.33 = (bf16[512,512]{1,0:T(8,128)(2,1)S(1)}, bf16[512,512]{1,0:T(8,128)(2,1)S(1)}, u32[]{:S(2)}, u32[]{:S(2)}) collective-permute-start(bf16[512,512]{1,0:T(8,128)(2,1)S(1)} %pad_maximum_fusion.1), channel_id=1, source_target_pairs={{0,4},{1,9},{2,6},{3,11},{4,0},{5,13},{6,2},{7,15},{8,12},{9,1},{1... | collective-permute-start | bytes 1572872 | tf_op jit(solution)/shard_map/ppermute | solution.py:37
  131.6 13.6 %collective-permute-start.23 = (bf16[272,512]{1,0:T(8,128)(2,1)S(1)}, bf16[272,512]{1,0:T(8,128)(2,1)S(1)}, u32[]{:S(2)}, u32[]{:S(2)}) collective-permute-start(bf16[272,512]{1,0:T(8,128)(2,1)S(1)} %pad_maximum_fusion.4), channel_id=1, source_target_pairs={{0,4},{1,9},{2,6},{3,11},{4,0},{5,13},{6,2},{7,15},{8,12},{9,1},{1... | collective-permute-start | bytes 835592 | tf_op jit(solution)/shard_map/ppermute | solution.py:37
  140.4 16.8 %collective-permute-start.34 = (bf16[1024,512]{1,0:T(8,128)(2,1)S(1)}, bf16[1024,512]{1,0:T(8,128)(2,1)S(1)}, u32[]{:S(2)}, u32[]{:S(2)}) collective-permute-start(bf16[1024,512]{1,0:T(8,128)(2,1)S(1)} %pad_maximum_fusion.own), channel_id=1, source_target_pairs={{0,2},{1,5},{2,0},{3,7},{4,6},{5,1},{6,4},{7,3},{8,10},{9,13},{10,... | collective-permute-start | bytes 3145736 | tf_op jit(solution)/shard_map/ppermute | solution.py:37
  145.3 5.6 %collective-permute-start.24 = (bf16[176,512]{1,0:T(8,128)(2,1)S(1)}, bf16[176,512]{1,0:T(8,128)(2,1)S(1)}, u32[]{:S(2)}, u32[]{:S(2)}) collective-permute-start(bf16[176,512]{1,0:T(8,128)(2,1)S(1)} %pad_maximum_fusion.7), channel_id=1, source_target_pairs={{0,8},{1,3},{2,10},{3,1},{4,12},{5,7},{6,14},{7,5},{8,0},{9,11},{1... | collective-permute-start | bytes 540680 | tf_op jit(solution)/shard_map/ppermute | solution.py:37
  145.4 22.6 %collective-permute-start.36 = (bf16[1024,512]{1,0:T(8,128)(2,1)S(1)}, bf16[1024,512]{1,0:T(8,128)(2,1)S(1)}, u32[]{:S(2)}, u32[]{:S(2)}) collective-permute-start(bf16[1024,512]{1,0:T(8,128)(2,1)S(1)} %pad_maximum_fusion.own), channel_id=1, source_target_pairs={{0,1},{1,0},{2,3},{3,2},{4,5},{5,4},{6,7},{7,6},{8,9},{9,8},{10,11... | collective-permute-start | bytes 3145736 | tf_op jit(solution)/shard_map/ppermute | solution.py:27
  150.9 6.8 %collective-permute-start.25 = (bf16[128,512]{1,0:T(8,128)(2,1)S(1)}, bf16[128,512]{1,0:T(8,128)(2,1)S(1)}, u32[]{:S(2)}, u32[]{:S(2)}) collective-permute-start(bf16[128,512]{1,0:T(8,128)(2,1)S(1)} %pad_maximum_fusion.8), channel_id=1, source_target_pairs={{0,16},{1,17},{2,18},{3,19},{4,20},{5,21},{6,22},{7,23},{8,24},{9,... | collective-permute-start | bytes 393224 | tf_op jit(solution)/shard_map/ppermute | solution.py:37
  157.2 17.8 %collective-permute-start.35 = (bf16[1024,512]{1,0:T(8,128)(2,1)S(1)}, bf16[1024,512]{1,0:T(8,128)(2,1)}, u32[]{:S(2)}, u32[]{:S(2)}) collective-permute-start(bf16[1024,512]{1,0:T(8,128)(2,1)S(1)} %collective-permute-done.34.own), channel_id=1, source_target_pairs={{0,1},{1,0},{2,3},{3,2},{4,5},{5,4},{6,7},{7,6},{8,9},{9,8},{10,11... | collective-permute-start | bytes 3145736 | tf_op jit(solution)/shard_map/ppermute | solution.py:27
  157.7 5.1 %collective-permute-start.26 = (bf16[48,512]{1,0:T(8,128)(2,1)S(1)}, bf16[48,512]{1,0:T(8,128)(2,1)S(1)}, u32[]{:S(2)}, u32[]{:S(2)}) collective-permute-start(bf16[48,512]{1,0:T(8,128)(2,1)S(1)} %add_convert_fusion.24), channel_id=1, source_target_pairs={{0,16},{4,20},{8,24},{12,28},{16,0},{20,4},{24,8},{28,12},{1,17},{... | collective-permute-start | bytes 147464 | tf_op jit(solution)/shard_map/ppermute | solution.py:27
  162.9 4.7 %collective-permute-start.27 = (bf16[96,512]{1,0:T(8,128)(2,1)S(1)}, bf16[96,512]{1,0:T(8,128)(2,1)S(1)}, u32[]{:S(2)}, u32[]{:S(2)}) collective-permute-start(bf16[96,512]{1,0:T(8,128)(2,1)S(1)} %pad_maximum_fusion.9), channel_id=1, source_target_pairs={{0,8},{4,12},{8,0},{12,4},{16,24},{20,28},{24,16},{28,20},{1,9},{5... | collective-permute-start | bytes 294920 | tf_op jit(solution)/shard_map/ppermute | solution.py:27
  167.6 5.7 %collective-permute-start.28 = (bf16[192,512]{1,0:T(8,128)(2,1)S(1)}, bf16[192,512]{1,0:T(8,128)(2,1)S(1)}, u32[]{:S(2)}, u32[]{:S(2)}) collective-permute-start(bf16[192,512]{1,0:T(8,128)(2,1)S(1)} %pad_maximum_fusion.6), channel_id=1, source_target_pairs={{0,4},{4,0},{8,12},{12,8},{16,20},{20,16},{24,28},{28,24},{1,5},{5... | collective-permute-start | bytes 589832 | tf_op jit(solution)/shard_map/ppermute | solution.py:27
  167.9 5.4 %collective-permute-start.29 = (bf16[80,512]{1,0:T(8,128)(2,1)S(1)}, bf16[80,512]{1,0:T(8,128)(2,1)S(1)}, u32[]{:S(2)}, u32[]{:S(2)}) collective-permute-start(bf16[80,512]{1,0:T(8,128)(2,1)S(1)} %add_convert_fusion.19.own), channel_id=1, source_target_pairs={{0,1},{1,0},{2,3},{3,2},{4,5},{5,4},{6,7},{7,6},{8,9},{9,8},{10,11... | collective-permute-start | bytes 245768 | tf_op jit(solution)/shard_map/ppermute | solution.py:27
  (21 other events, 71.9 us)

commit v4 on v3

--- a/solution.py
+++ b/solution.py
@@ -391,13 +391,13 @@
 
 
 def last_kernel(micros, *refs):
-    meta, tokens, gh, gain, key_value, up_row, rows = refs[:7]
-    normed = refs[7 : 7 + micros]
-    part = refs[7 + micros : 7 + 2 * micros]
-    kept = refs[7 + 2 * micros : 7 + 3 * micros]
-    got = refs[7 + 3 * micros : 7 + 4 * micros]
-    chosen = refs[7 + 4 * micros : 7 + 5 * micros]
-    input_grad, own, sent, bundle = refs[7 + 5 * micros :]
+    meta, _, tokens, gh, gain, key_value, up_row, rows = refs[:8]
+    normed = refs[8 : 8 + micros]
+    part = refs[8 + micros : 8 + 2 * micros]
+    kept = refs[8 + 2 * micros : 8 + 3 * micros]
+    got = refs[8 + 3 * micros : 8 + 4 * micros]
+    chosen = refs[8 + 4 * micros : 8 + 5 * micros]
+    input_grad, own, sent, bundle = refs[8 + 5 * micros :]
     _, tok, width = tokens.shape
     key_rows = 0.0
     gain_sum = jnp.zeros((1, width), f32)
@@ -669,7 +669,9 @@
 
     marks = []
     keep, got = ffn_own, flip(ffn_sent, "expert", 0)
-    for ways in hops:
+    for i, ways in enumerate(hops):
+        if 0 < i <= 2 and i <= micros:
+            keep, gq[i - 1] = lax.optimization_barrier((keep, gq[i - 1]))
         keep, got = halve(keep, got, ways)
         marks.append(got)
     whole = add(keep, got)
@@ -677,7 +679,7 @@
     w_own, w_sent = call(
         functools.partial(weights_kernel, (groups, size, tok, micros), rows_w),
         [table],
-        [marks[2], gh] + gq + normed + mixt,
+        [marks[1], gh] + gq + normed + mixt,
         [((chips * rows_w, width), b16), ((chips * rows_w, width), b16)],
         cost=1.5,
         far=(0,),
@@ -687,10 +689,11 @@
     input_grad, b_own, b_sent = call(
         functools.partial(last_kernel, micros),
         [meta],
-        [tokens, gh, gain_one, key_value, up_row, ffn_rows] + normed + part + kept + arrived + chosen,
+        [marks[3], tokens, gh, gain_one, key_value, up_row, ffn_rows] + normed + part + kept + arrived + chosen,
         [((micros, tok, width), f32), ((half, width), b16), ((half, width), b16)],
         [((2 * half, width), b16)],
         cost=3.8,
+        far=(0,),
     )
 
     o_tile = 256
@@ -728,23 +731,39 @@
         )(meta, own, got, *filled)
 
     keep, got = w_own, flip(w_sent, "expert", 0)
-    bundle = add(b_own, flip(b_sent, "expert", 0))
+    bundle = None
     for up, (ways, back) in enumerate(zip(hops, hops[::-1])):
         count = keep.shape[0] // 2
-        moving = jnp.concatenate([add(keep[count:], got[count:]), bundle], axis=0)
+        moving = add(keep[count:], got[count:])
         keep = add(keep[:count], got[:count])
+        if up == 1:
+            bundle = add(b_own, flip(b_sent, "expert", 0))
+        if up > 0:
+            moving = jnp.concatenate([moving, bundle], axis=0)
         arrived_rows = hop(whole, back, groups, batch)
         moving = hop(moving, ways, groups, batch)
         if up < len(hops) - 1:
             whole = jnp.concatenate([whole, arrived_rows], axis=0)
+        if up == len(hops) - 1:
+            arrived_rows, moving = lax.optimization_barrier((arrived_rows, moving))
         got = moving[:count]
-        bundle = add(bundle, moving[count:])
+        if up > 0:
+            bundle = add(bundle, moving[count:])
+    bundle = add(bundle, hop(bundle, hops[0], groups, batch))
     own_low, own_high = whole, arrived_rows
     got_low, got_high = flip(own_low, "expert", 0), flip(own_high, "expert", 0)
     weights = add(keep, got)
-    filled = ordered(0, own_low, got_low, ())
-    for way in b_bits[::-1]:
-        weights = jnp.concatenate([weights, flip(weights, *way)], axis=0)
+    ways_up = b_bits[::-1]
+    for i, way in enumerate(ways_up):
+        came = flip(weights, *way)
+        if i == len(ways_up) - 3:
+            filled = ordered(0, own_low, got_low, ())
+            came, *filled = lax.optimization_barrier((came, *filled))
+        if i == len(ways_up) - 2:
+            filled = ordered(1, own_high, got_high, filled)
+            came, *filled = lax.optimization_barrier((came, *filled))
+        weights = jnp.concatenate([weights, came], axis=0)
+    grad_down, grad_up = filled
 
     wq_grad, wo_grad, grad_key_value, grad_router, grad_up_bias, *rows = call(
         functools.partial(small_kernel, (both, pad, rows_w)),
@@ -758,7 +777,6 @@
     )
     grad_down_bias, grad_gain_two, grad_shift_two, grad_gain_one, grad_shift_one = rows
 
-    grad_down, grad_up = ordered(1, own_high, got_high, filled)
 
     return (
         block_out.reshape(micros, tok, width),

time: 180 us -> 171 us (0.950)
  waiting for transfers between devices: 76.9 us -> 57.8 us
  starting transfers between devices: 36.1 us -> 45.4 us
    ppermute x12 -> x13, waiting for transfers between devices: 53.5 us -> 41.2 us  [hop(): return lax.ppermute(values, ('batch', 'expert'), pairs)]
    ppermute x25, waiting for transfers between devices: 23.4 us -> 16.6 us  [flip(): return lax.ppermute(values, axis, [(i, i ^ 1 << bit) for i in range(size)])]
    ppermute x25, starting transfers between devices: 15.1 us -> 21.4 us  [flip(): return lax.ppermute(values, axis, [(i, i ^ 1 << bit) for i in range(size)])]
    ppermute x12 -> x13, starting transfers between devices: 21 us -> 24 us  [hop(): return lax.ppermute(values, ('batch', 'expert'), pairs)]
  transfers between devices with their start and end apart: 37 -> 38, of which waited for: 21 -> 17; matrix products, arithmetic and copies ran while one was open for 2% -> 2% of each run, Pallas kernels for 19% -> 22%
where the time goes in v4:
time: 171 us
  Pallas kernels  59.9 us (35%)
  waiting for transfers between devices  57.8 us (34%)
  starting transfers between devices  45.4 us (27%)
  other arithmetic  3.72 us (2%)
  local copies, waits for them, and re-layouts  2.83 us (2%)
    pallas_call x9, Pallas kernels, call(): pl.pallas_call(kernel, in_specs=[smem] * len(scalars) + [far_spec if i in...  52.2 us
    ppermute x13, waiting for transfers between devices, hop(): return lax.ppermute(values, ('batch', 'expert'), pairs)  41.2 us
    ppermute x13, starting transfers between devices, hop(): return lax.ppermute(values, ('batch', 'expert'), pairs)  24 us
    ppermute x25, starting transfers between devices, flip(): return lax.ppermute(values, axis, [(i, i ^ 1 << bit) for i in range(size)])  21.4 us
    ppermute x25, waiting for transfers between devices, flip(): return lax.ppermute(values, axis, [(i, i ^ 1 << bit) for i in range(size)])  16.6 us
    pallas_call x2, Pallas kernels, ordered(): pl.pallas_call(functools.partial(order_kernel, chunk, top_bit, side), gri...  7.79 us
  transfers between devices with their start and end apart: 38, of which 17 were waited for; matrix products, arithmetic and copies ran while one was open for 2% of the time, Pallas kernels for 22%

profile of v4, /device:TPU:0, one launch (start us, length us, event | category | flops | bytes accessed | tf_op | source)
XLA Modules:
  0.0 171.1 jit_solution(3989159401763137120)
XLA Ops:
  0.6 3.0 %collective-permute-start.3 = (bf16[192,512]{1,0:T(8,128)(2,1)}, bf16[192,512]{1,0:T(8,128)(2,1)S(1)}, u32[]{:S(2)}, u32[]{:S(2)}) collective-permute-start(bf16[192,512]{1,0:T(8,128)(2,1)} %bitcast.18), channel_id=1, source_target_pairs={{0,2},{1,3},{2,0},{3,1},{4,6},{5,7},{6,4},{7,5},{8,10},{9,11},{10,... | collective-permute-start | bytes 589832 | tf_op jit(solution)/shard_map/ppermute | solution.py:27
  3.7 2.5 %shard_map.263 = (bf16[512,512]{1,0:T(8,128)(2,1)S(1)}, bf16[512,512]{1,0:T(8,128)(2,1)S(1)}, bf16[512,128]{1,0:T(8,128)(2,1)S(1)}, bf16[512,128]{1,0:T(8,128)(2...) custom-call(bf16[2,512,512]{2,1,0:T(8,128)(2,1)} %refs_2_.1, bf16[512,128]{1,0:T(8,128)(2,1)} %refs_5_.5, ...), custom_call_target="tpu_custom_call" | custom-call | flops 2640000000 | tf_op jit(solution)/shard_map/pallas_call | solution.py:562
  6.3 2.9 %collective-permute-done.3.refs_9_.refs_11_ = bf16[192,512]{1,0:T(8,128)(2,1)S(1)} collective-permute-done((bf16[192,512]{1,0:T(8,128)(2,1)}, bf16[192,512]{1,0:T(8,128)(2,1)S(1)}, u32[]{:S(2)}, u32[]{:S(2)}) %collective-permute-start.3) | collective-permute-done | bytes 196640 | tf_op jit(solution)/shard_map/ppermute | solution.py:27
  9.3 0.5 collective-permute-start.1
  9.8 1.8 %collective-permute-done.refs_5_ = bf16[512,128]{1,0:T(8,128)(2,1)S(1)} collective-permute-done((bf16[512,128]{1,0:T(8,128)(2,1)S(1)}, bf16[512,128]{1,0:T(8,128)(2,1)S(1)}, u32[]{:S(2)}, u32[]{:S(2)}) %collective-permute-start) | collective-permute-done | bytes 131104 | tf_op jit(solution)/shard_map/ppermute | solution.py:27
  11.6 1.8 %collective-permute-start.9 = (bf16[192,512]{1,0:T(8,128)(2,1)S(1)}, bf16[192,512]{1,0:T(8,128)(2,1)S(1)}, u32[]{:S(2)}, u32[]{:S(2)}) collective-permute-start(bf16[192,512]{1,0:T(8,128)(2,1)S(1)} %bitcast.24), channel_id=1, source_target_pairs={{0,2},{1,3},{2,0},{3,1},{4,6},{5,7},{6,4},{7,5},{8,10},{9,11},{10,... | collective-permute-start | bytes 589832 | tf_op jit(solution)/shard_map/ppermute | solution.py:27
  13.4 0.5 broadcast.205
  13.9 0.7 reduce.3
  15.9 4.9 %shard_map.264 = (bf16[2048,128]{1,0:T(8,128)(2,1)S(1)}, bf16[128,2048]{1,0:T(8,128)(2,1)S(1)}, bf16[2,64,768]{2,1,0:T(8,128)(2,1)S(1)}, f32[2,64,768]{2,1,0:T(8...) custom-call(s32[28]{0:T(128)S(1)} %concatenate.34.refs_0_.meta, ...), custom_call_target="tpu_custom_call" | custom-call | flops 5500000256 | tf_op jit(solution)/shard_map/pallas_call | solution.py:562
  20.8 0.9 collective-permute-done.6.refs_5_
  23.9 5.4 %shard_map.265 = (bf16[2048,128]{1,0:T(8,128)(2,1)S(1)}, bf16[128,2048]{1,0:T(8,128)(2,1)S(1)}, bf16[2,64,768]{2,1,0:T(8,128)(2,1)S(1)}, f32[2,64,768]{2,1,0:T(8...) custom-call(s32[28]{0:T(128)S(1)} %concatenate.34.refs_0_.meta, ...), custom_call_target="tpu_custom_call" | custom-call | flops 5500000256 | tf_op jit(solution)/shard_map/pallas_call | solution.py:562
  29.4 21.5 %shard_map.266 = (bf16[1024,512]{1,0:T(8,128)(2,1)}, f32[1024,512]{1,0:T(8,128)S(1)}, bf16[2048,512]{1,0:T(8,128)(2,1)S(1)}, bf16[2048,512]{1,0:T(8,128)(2,1)S(1...) custom-call(s32[28]{0:T(128)S(1)} %concatenate.34.refs_0_.meta, bf16[2,512,512]{2,1,0:T(8,128)(2,1)S(1)} %copy-done.3, ...), custom_call_target="tpu_custom_call" | custom-call | flops 12099999744 | tf_op jit(solution)/shard_map/pallas_call | solution.py:562
  51.0 2.4 %collective-permute-start.12 = (bf16[2048,512]{1,0:T(8,128)(2,1)S(1)}, bf16[2048,512]{1,0:T(8,128)(2,1)S(1)}, u32[]{:S(2)}, u32[]{:S(2)}) collective-permute-start(bf16[2048,512]{1,0:T(8,128)(2,1)S(1)} %get-tuple-element.94), channel_id=1, source_target_pairs={{0,1},{1,0},{2,3},{3,2},{4,5},{5,4},{6,7},{7,6},{8,9},{9,8},{10,11... | collective-permute-start | bytes 6291464 | tf_op jit(solution)/shard_map/ppermute | solution.py:27
  53.4 3.8 %collective-permute-done.12 = bf16[2048,512]{1,0:T(8,128)(2,1)S(1)} collective-permute-done((bf16[2048,512]{1,0:T(8,128)(2,1)S(1)}, bf16[2048,512]{1,0:T(8,128)(2,1)S(1)}, u32[]{:S(2)}, u32[]{:S(2)}) %collective-permute-start.12) | collective-permute-done | bytes 2097184 | tf_op jit(solution)/shard_map/ppermute | solution.py:27
  57.2 0.7 add_convert_fusion.1
  57.9 8.0 %collective-permute-start.13 = (bf16[1024,512]{1,0:T(8,128)(2,1)S(1)}, bf16[1024,512]{1,0:T(8,128)(2,1)S(1)}, u32[]{:S(2)}, u32[]{:S(2)}) collective-permute-start(bf16[1024,512]{1,0:T(8,128)(2,1)S(1)} %get-tuple-element.149), channel_id=1, source_target_pairs={{0,2},{1,5},{2,0},{3,7},{4,6},{5,1},{6,4},{7,3},{8,10},{9,13},{10,... | collective-permute-start | bytes 3145736 | tf_op jit(solution)/shard_map/ppermute | solution.py:37
  65.9 5.0 %shard_map.267 = (f32[512,512]{1,0:T(8,128)S(1)}, bf16[2,512,128]{2,1,0:T(8,128)(2,1)S(1)}, bf16[2,512,128]{2,1,0:T(8,128)(2,1)S(1)}, bf16[768,512]{1,0:T(8,128)...) custom-call(s32[28]{0:T(128)S(1)} %concatenate.34.refs_0_.meta, ...), custom_call_target="tpu_custom_call" | custom-call | flops 9900000256 | tf_op jit(solution)/shard_map/pallas_call | solution.py:562
  70.9 7.7 %collective-permute-done.13 = bf16[1024,512]{1,0:T(8,128)(2,1)S(1)} collective-permute-done((bf16[1024,512]{1,0:T(8,128)(2,1)S(1)}, bf16[1024,512]{1,0:T(8,128)(2,1)S(1)}, u32[]{:S(2)}, u32[]{:S(2)}) %collective-permute-start.13) | collective-permute-done | bytes 1048608 | tf_op jit(solution)/shard_map/ppermute | solution.py:37
  78.9 2.5 %collective-permute-start.14 = (bf16[512,512]{1,0:T(8,128)(2,1)S(1)}, bf16[512,512]{1,0:T(8,128)(2,1)S(1)}, u32[]{:S(2)}, u32[]{:S(2)}) collective-permute-start(bf16[512,512]{1,0:T(8,128)(2,1)S(1)} %get-tuple-element.151), channel_id=1, source_target_pairs={{0,4},{1,9},{2,6},{3,11},{4,0},{5,13},{6,2},{7,15},{8,12},{9,1},{1... | collective-permute-start | bytes 1572872 | tf_op jit(solution)/shard_map/ppermute | solution.py:37
  81.5 5.0 %shard_map.268 = (f32[512,512]{1,0:T(8,128)S(1)}, bf16[2,512,128]{2,1,0:T(8,128)(2,1)S(1)}, bf16[2,512,128]{2,1,0:T(8,128)(2,1)S(1)}, bf16[768,512]{1,0:T(8,128)...) custom-call(s32[28]{0:T(128)S(1)} %concatenate.34.refs_0_.meta, ...), custom_call_target="tpu_custom_call" | custom-call | flops 9900000256 | tf_op jit(solution)/shard_map/pallas_call | solution.py:562
  86.5 2.2 %collective-permute-done.14.refs_1_ = bf16[512,512]{1,0:T(8,128)(2,1)S(1)} collective-permute-done((bf16[512,512]{1,0:T(8,128)(2,1)S(1)}, bf16[512,512]{1,0:T(8,128)(2,1)S(1)}, u32[]{:S(2)}, u32[]{:S(2)}) %collective-permute-start.14) | collective-permute-done | bytes 524320 | tf_op jit(solution)/shard_map/ppermute | solution.py:37
  88.8 2.1 %collective-permute-start.15 = (bf16[256,512]{1,0:T(8,128)(2,1)S(1)}, bf16[256,512]{1,0:T(8,128)(2,1)S(1)}, u32[]{:S(2)}, u32[]{:S(2)}) collective-permute-start(bf16[256,512]{1,0:T(8,128)(2,1)S(1)} %get-tuple-element.155), channel_id=1, source_target_pairs={{0,8},{1,3},{2,10},{3,1},{4,12},{5,7},{6,14},{7,5},{8,0},{9,11},{1... | collective-permute-start | bytes 786440 | tf_op jit(solution)/shard_map/ppermute | solution.py:37
  91.0 0.6 collective-permute-start.18
  91.7 2.4 %shard_map.270 = (bf16[768,512]{1,0:T(8,128)(2,1)S(1)}, bf16[768,512]{1,0:T(8,128)(2,1)S(1)}) custom-call(s32[4,8]{1,0:T(4,128)S(1)} %select_select_fusion.refs_0_, bf16[512,512]{1,0:T(8,128)(2,1)} %copy-done.22, f32[1024,512]{1,0:T(8,128)S(1)} %get-tuple-element.95.refs_1_.refs_3_.refs_2_, bf16[768,512]{1,0:T(8,128)(2,1)S(1)} %get-tuple-element.120.refs_3_, ...), custom_call_target="tpu_custom_call" | custom-call | flops 1650000000 | tf_op jit(solution)/shard_map/pallas_call | solution.py:562
  94.6 0.7 collective-permute-done.15
  95.3 3.3 %collective-permute-start.16 = (bf16[128,512]{1,0:T(8,128)(2,1)S(1)}, bf16[128,512]{1,0:T(8,128)(2,1)S(1)}, u32[]{:S(2)}, u32[]{:S(2)}) collective-permute-start(bf16[128,512]{1,0:T(8,128)(2,1)S(1)} %add_convert_fusion.16), channel_id=1, source_target_pairs={{0,16},{1,17},{2,18},{3,19},{4,20},{5,21},{6,22},{7,23},{8,24},{9,... | collective-permute-start | bytes 393224 | tf_op jit(solution)/shard_map/ppermute | solution.py:37
  98.8 2.7 %collective-permute-start.20 = (bf16[1,512,128]{2,1,0:T(8,128)(2,1)S(1)}, bf16[1,512,128]{2,1,0:T(8,128)(2,1)S(1)}, u32[]{:S(2)}, u32[]{:S(2)}) collective-permute-start(bf16[1,512,128]{2,1,0:T(8,128)(2,1)S(1)} %get-tuple-element.158), channel_id=1, source_target_pairs={{0,2},{1,3},{2,0},{3,1},{4,6},{5,7},{6,4},{7,5},{8,10},{9,11},{10,... | collective-permute-start | bytes 393224 | tf_op jit(solution)/shard_map/ppermute | solution.py:27
  101.5 4.3 %collective-permute-done.16.refs_1_ = bf16[128,512]{1,0:T(8,128)(2,1)S(1)} collective-permute-done((bf16[128,512]{1,0:T(8,128)(2,1)S(1)}, bf16[128,512]{1,0:T(8,128)(2,1)S(1)}, u32[]{:S(2)}, u32[]{:S(2)}) %collective-permute-start.16) | collective-permute-done | bytes 131104 | tf_op jit(solution)/shard_map/ppermute | solution.py:37
  106.0 2.1 %collective-permute-start.19 = (bf16[1,512,128]{2,1,0:T(8,128)(2,1)S(1)}, bf16[1,512,128]{2,1,0:T(8,128)(2,1)S(1)}, u32[]{:S(2)}, u32[]{:S(2)}) collective-permute-start(bf16[1,512,128]{2,1,0:T(8,128)(2,1)S(1)} %get-tuple-element.160), channel_id=1, source_target_pairs={{0,2},{1,3},{2,0},{3,1},{4,6},{5,7},{6,4},{7,5},{8,10},{9,11},{10,... | collective-permute-start | bytes 393224 | tf_op jit(solution)/shard_map/ppermute | solution.py:27
  108.2 4.8 %collective-permute-done.26 = bf16[128,512]{1,0:T(8,128)(2,1)S(1)} collective-permute-done((bf16[128,512]{1,0:T(8,128)(2,1)S(1)}, bf16[128,512]{1,0:T(8,128)(2,1)S(1)}, u32[]{:S(2)}, u32[]{:S(2)}) %collective-permute-start.26) | collective-permute-done | bytes 131104 | tf_op jit(solution)/shard_map/ppermute | solution.py:37
  113.3 2.4 %collective-permute-start.22 = (bf16[384,512]{1,0:T(8,128)(2,1)S(1)}, bf16[384,512]{1,0:T(8,128)(2,1)S(1)}, u32[]{:S(2)}, u32[]{:S(2)}) collective-permute-start(bf16[384,512]{1,0:T(8,128)(2,1)S(1)} %get-tuple-element.153), channel_id=1, source_target_pairs={{0,2},{1,5},{2,0},{3,7},{4,6},{5,1},{6,4},{7,3},{8,10},{9,13},{10,... | collective-permute-start | bytes 1179656 | tf_op jit(solution)/shard_map/ppermute | solution.py:37
  115.7 3.9 %shard_map.269 = (f32[2,512,512]{2,1,0:T(8,128)}, bf16[80,512]{1,0:T(8,128)(2,1)S(1)}, bf16[80,512]{1,0:T(8,128)(2,1)S(1)}) custom-call(s32[28]{0:T(128)S(1)} %concatenate.34.refs_0_.meta, bf16[128,512]{1,0:T(8,128)(2,1)} %copy-done.25, bf16[2,512,512]{2,1,0:T(8,128)(2,1)S(1)} %copy-done.3, f32[1024,512]{1,0:T(8,128)S(1)} %get-tuple-element.95.refs_1_.refs_3_.refs_2_, ...), custom_call_target="tpu_custom_call" | custom-call | flops 4180000000 | tf_op jit(solution)/shard_map/pallas_call | solution.py:562
  119.6 2.4 %collective-permute-start.23 = (bf16[80,512]{1,0:T(8,128)(2,1)S(1)}, bf16[80,512]{1,0:T(8,128)(2,1)S(1)}, u32[]{:S(2)}, u32[]{:S(2)}) collective-permute-start(bf16[80,512]{1,0:T(8,128)(2,1)S(1)} %get-tuple-element.125), channel_id=1, source_target_pairs={{0,1},{1,0},{2,3},{3,2},{4,5},{5,4},{6,7},{7,6},{8,9},{9,8},{10,11... | collective-permute-start | bytes 245768 | tf_op jit(solution)/shard_map/ppermute | solution.py:27
  122.1 1.1 collective-permute-start.28
  123.3 3.2 %collective-permute-start.24 = (bf16[272,512]{1,0:T(8,128)(2,1)S(1)}, bf16[272,512]{1,0:T(8,128)(2,1)S(1)}, u32[]{:S(2)}, u32[]{:S(2)}) collective-permute-start(bf16[272,512]{1,0:T(8,128)(2,1)S(1)} %pad_maximum_fusion.3), channel_id=1, source_target_pairs={{0,4},{1,9},{2,6},{3,11},{4,0},{5,13},{6,2},{7,15},{8,12},{9,1},{1... | collective-permute-start | bytes 835592 | tf_op jit(solution)/shard_map/ppermute | solution.py:37
  126.5 4.8 %collective-permute-done.28 = bf16[512,512]{1,0:T(8,128)(2,1)S(1)} collective-permute-done((bf16[512,512]{1,0:T(8,128)(2,1)S(1)}, bf16[512,512]{1,0:T(8,128)(2,1)S(1)}, u32[]{:S(2)}, u32[]{:S(2)}) %collective-permute-start.28) | collective-permute-done | bytes 524320 | tf_op jit(solution)/shard_map/ppermute | solution.py:37
  131.4 0.7 collective-permute-start.29
  132.1 3.2 %collective-permute-done.24 = bf16[272,512]{1,0:T(8,128)(2,1)S(1)} collective-permute-done((bf16[272,512]{1,0:T(8,128)(2,1)S(1)}, bf16[272,512]{1,0:T(8,128)(2,1)S(1)}, u32[]{:S(2)}, u32[]{:S(2)}) %collective-permute-start.24) | collective-permute-done | bytes 278560 | tf_op jit(solution)/shard_map/ppermute | solution.py:37
  135.6 5.4 %collective-permute-done.25 = bf16[176,512]{1,0:T(8,128)(2,1)S(1)} collective-permute-done((bf16[176,512]{1,0:T(8,128)(2,1)S(1)}, bf16[176,512]{1,0:T(8,128)(2,1)S(1)}, u32[]{:S(2)}, u32[]{:S(2)}) %collective-permute-start.25) | collective-permute-done | bytes 180256 | tf_op jit(solution)/shard_map/ppermute | solution.py:37
  141.2 8.0 %collective-permute-done.30 = bf16[128,512]{1,0:T(8,128)(2,1)S(1)} collective-permute-done((bf16[128,512]{1,0:T(8,128)(2,1)S(1)}, bf16[128,512]{1,0:T(8,128)(2,1)S(1)}, u32[]{:S(2)}, u32[]{:S(2)}) %collective-permute-start.30) | collective-permute-done | bytes 131104 | tf_op jit(solution)/shard_map/ppermute | solution.py:37
  149.2 0.7 copy-done.23
  149.8 0.9 add_convert_fusion.24
  150.8 3.3 %shard_map.271 = (f32[2048,512]{1,0:T(8,128)}, f32[512,2048]{1,0:T(8,128)}) custom-call(s32[28]{0:T(128)S(1)} %concatenate.34.refs_0_.meta, bf16[1024,512]{1,0:T(8,128)(2,1)S(1)} %pad_maximum_fusion.own, bf16[1024,512]{1,0:T(8,128)(2,1)S(1)} %collective-permute-done.32.got), custom_call_target="tpu_custom_call" | custom-call | bytes 6291456 | tf_op jit(solution)/shard_map/pallas_call | solution.py:713
  154.1 1.9 %collective-permute-done.31 = bf16[48,512]{1,0:T(8,128)(2,1)S(1)} collective-permute-done((bf16[48,512]{1,0:T(8,128)(2,1)S(1)}, bf16[48,512]{1,0:T(8,128)(2,1)S(1)}, u32[]{:S(2)}, u32[]{:S(2)}) %collective-permute-start.31) | collective-permute-done | bytes 49184 | tf_op jit(solution)/shard_map/ppermute | solution.py:27
  156.9 4.5 %shard_map.272 = (f32[2048,512]{1,0:T(8,128)}, f32[512,2048]{1,0:T(8,128)}) custom-call(s32[28]{0:T(128)S(1)} %concatenate.34.refs_0_.meta, bf16[1024,512]{1,0:T(8,128)(2,1)S(1)} %collective-permute-done.29.own, bf16[1024,512]{1,0:T(8,128)(2,1)} %collective-permute-done.34.got, ...), custom_call_target="tpu_custom_call", output_to_operand_aliasing={{0}: (3, {}), {1}: (4, {})} | custom-call | bytes 6291456 | tf_op jit(solution)/shard_map/pallas_call | solution.py:713
  161.4 2.9 %collective-permute-start.35 = (bf16[192,512]{1,0:T(8,128)(2,1)S(1)}, bf16[192,512]{1,0:T(8,128)(2,1)S(1)}, u32[]{:S(2)}, u32[]{:S(2)}) collective-permute-start(bf16[192,512]{1,0:T(8,128)(2,1)S(1)} %pad_maximum_fusion.5), channel_id=1, source_target_pairs={{0,4},{4,0},{8,12},{12,8},{16,20},{20,16},{24,28},{28,24},{1,5},{5... | collective-permute-start | bytes 589832 | tf_op jit(solution)/shard_map/ppermute | solution.py:27
  164.5 4.8 %collective-permute-done.35 = bf16[192,512]{1,0:T(8,128)(2,1)S(1)} collective-permute-done((bf16[192,512]{1,0:T(8,128)(2,1)S(1)}, bf16[192,512]{1,0:T(8,128)(2,1)S(1)}, u32[]{:S(2)}, u32[]{:S(2)}) %collective-permute-start.35) | collective-permute-done | bytes 196640 | tf_op jit(solution)/shard_map/ppermute | solution.py:27
  169.3 1.6 shard_map.273
  (145 shorter events, 7.2 us)
Async XLA Ops:
  0.6 8.6 %collective-permute-start.3 = (bf16[192,512]{1,0:T(8,128)(2,1)}, bf16[192,512]{1,0:T(8,128)(2,1)S(1)}, u32[]{:S(2)}, u32[]{:S(2)}) collective-permute-start(bf16[192,512]{1,0:T(8,128)(2,1)} %bitcast.18), channel_id=1, source_target_pairs={{0,2},{1,3},{2,0},{3,1},{4,6},{5,7},{6,4},{7,5},{8,10},{9,11},{10,... | collective-permute-start | bytes 589832 | tf_op jit(solution)/shard_map/ppermute | solution.py:27
  3.7 10.2 %copy-start.27 = (s32[2,1,8]{2,1,0:T(1,128)S(1)}, s32[2,1,8]{2,1,0:T(1,128)}, u32[]{:S(2)}) copy-start(s32[2,1,8]{2,1,0:T(1,128)} %param.18) | copy-start | bytes 196
  6.1 9.0 %copy-start.15 = (bf16[512,128]{1,0:T(8,128)(2,1)}, bf16[512,128]{1,0:T(8,128)(2,1)S(1)}, u32[]{:S(2)}) copy-start(bf16[512,128]{1,0:T(8,128)(2,1)S(1)} %get-tuple-element.83.refs_4_) | copy-start | bytes 393220
  6.1 15.6 %copy-start.14 = (bf16[512,128]{1,0:T(8,128)(2,1)}, bf16[512,128]{1,0:T(8,128)(2,1)S(1)}, u32[]{:S(2)}) copy-start(bf16[512,128]{1,0:T(8,128)(2,1)S(1)} %get-tuple-element.89.refs_4_) | copy-start | bytes 393220
  6.2 5.4 %collective-permute-start = (bf16[512,128]{1,0:T(8,128)(2,1)S(1)}, bf16[512,128]{1,0:T(8,128)(2,1)S(1)}, u32[]{:S(2)}, u32[]{:S(2)}) collective-permute-start(bf16[512,128]{1,0:T(8,128)(2,1)S(1)} %get-tuple-element.83.refs_4_), channel_id=1, source_target_pairs={{0,2},{1,3},{2,0},{3,1},{4,6},{5,7},{6,4},{7,5},{8,10},{9,11},{10,... | collective-permute-start | bytes 393224 | tf_op jit(solution)/shard_map/ppermute | solution.py:27
  6.3 8.8 %collective-permute-start.4 = (bf16[192,512]{1,0:T(8,128)(2,1)S(1)}, bf16[192,512]{1,0:T(8,128)(2,1)S(1)}, u32[]{:S(2)}, u32[]{:S(2)}) collective-permute-start(bf16[192,512]{1,0:T(8,128)(2,1)S(1)} %bitcast.21), channel_id=1, source_target_pairs={{0,1},{1,0},{2,3},{3,2},{4,5},{5,4},{6,7},{7,6},{8,9},{9,8},{10,11... | collective-permute-start | bytes 589832 | tf_op jit(solution)/shard_map/ppermute | solution.py:27
  9.3 5.9 %collective-permute-start.5 = (bf16[192,512]{1,0:T(8,128)(2,1)S(1)}, bf16[192,512]{1,0:T(8,128)(2,1)S(1)}, u32[]{:S(2)}, u32[]{:S(2)}) collective-permute-start(bf16[192,512]{1,0:T(8,128)(2,1)S(1)} %collective-permute-done.3.refs_9_.refs_11_), channel_id=1, source_target_pairs={{0,1},{1,0},{2,3},{3,2},{4,5},{5,4},{6,7},{7,6},{8,9},{9,8},{10,11... | collective-permute-start | bytes 589832 | tf_op jit(solution)/shard_map/ppermute | solution.py:27
  9.3 5.5 %collective-permute-start.1 = (bf16[512,128]{1,0:T(8,128)(2,1)S(1)}, bf16[512,128]{1,0:T(8,128)(2,1)S(1)}, u32[]{:S(2)}, u32[]{:S(2)}) collective-permute-start(bf16[512,128]{1,0:T(8,128)(2,1)S(1)} %get-tuple-element.83.refs_4_), channel_id=1, source_target_pairs={{0,1},{1,0},{2,3},{3,2},{4,5},{5,4},{6,7},{7,6},{8,9},{9,8},{10,11... | collective-permute-start | bytes 393224 | tf_op jit(solution)/shard_map/ppermute | solution.py:27
  11.6 3.5 %collective-permute-start.2 = (bf16[512,128]{1,0:T(8,128)(2,1)S(1)}, bf16[512,128]{1,0:T(8,128)(2,1)S(1)}, u32[]{:S(2)}, u32[]{:S(2)}) collective-permute-start(bf16[512,128]{1,0:T(8,128)(2,1)S(1)} %collective-permute-done.refs_5_), channel_id=1, source_target_pairs={{0,1},{1,0},{2,3},{3,2},{4,5},{5,4},{6,7},{7,6},{8,9},{9,8},{10,11... | collective-permute-start | bytes 393224 | tf_op jit(solution)/shard_map/ppermute | solution.py:27
  11.6 10.8 %collective-permute-start.9 = (bf16[192,512]{1,0:T(8,128)(2,1)S(1)}, bf16[192,512]{1,0:T(8,128)(2,1)S(1)}, u32[]{:S(2)}, u32[]{:S(2)}) collective-permute-start(bf16[192,512]{1,0:T(8,128)(2,1)S(1)} %bitcast.24), channel_id=1, source_target_pairs={{0,2},{1,3},{2,0},{3,1},{4,6},{5,7},{6,4},{7,5},{8,10},{9,11},{10,... | collective-permute-start | bytes 589832 | tf_op jit(solution)/shard_map/ppermute | solution.py:27
  14.8 7.0 %collective-permute-start.6 = (bf16[512,128]{1,0:T(8,128)(2,1)S(1)}, bf16[512,128]{1,0:T(8,128)(2,1)S(1)}, u32[]{:S(2)}, u32[]{:S(2)}) collective-permute-start(bf16[512,128]{1,0:T(8,128)(2,1)S(1)} %get-tuple-element.89.refs_4_), channel_id=1, source_target_pairs={{0,2},{1,3},{2,0},{3,1},{4,6},{5,7},{6,4},{7,5},{8,10},{9,11},{10,... | collective-permute-start | bytes 393224 | tf_op jit(solution)/shard_map/ppermute | solution.py:27
  21.7 1.3 collective-permute-start.7
  21.9 1.4 collective-permute-start.8
  22.2 7.1 %collective-permute-start.10 = (bf16[192,512]{1,0:T(8,128)(2,1)S(1)}, bf16[192,512]{1,0:T(8,128)(2,1)S(1)}, u32[]{:S(2)}, u32[]{:S(2)}) collective-permute-start(bf16[192,512]{1,0:T(8,128)(2,1)S(1)} %bitcast.25), channel_id=1, source_target_pairs={{0,1},{1,0},{2,3},{3,2},{4,5},{5,4},{6,7},{7,6},{8,9},{9,8},{10,11... | collective-permute-start | bytes 589832 | tf_op jit(solution)/shard_map/ppermute | solution.py:27
  22.4 7.0 %collective-permute-start.11 = (bf16[192,512]{1,0:T(8,128)(2,1)S(1)}, bf16[192,512]{1,0:T(8,128)(2,1)S(1)}, u32[]{:S(2)}, u32[]{:S(2)}) collective-permute-start(bf16[192,512]{1,0:T(8,128)(2,1)S(1)} %collective-permute-done.9.refs_12_.refs_15_), channel_id=1, source_target_pairs={{0,1},{1,0},{2,3},{3,2},{4,5},{5,4},{6,7},{7,6},{8,9},{9,8},{10,11... | collective-permute-start | bytes 589832 | tf_op jit(solution)/shard_map/ppermute | solution.py:27
  51.0 6.2 %collective-permute-start.12 = (bf16[2048,512]{1,0:T(8,128)(2,1)S(1)}, bf16[2048,512]{1,0:T(8,128)(2,1)S(1)}, u32[]{:S(2)}, u32[]{:S(2)}) collective-permute-start(bf16[2048,512]{1,0:T(8,128)(2,1)S(1)} %get-tuple-element.94), channel_id=1, source_target_pairs={{0,1},{1,0},{2,3},{3,2},{4,5},{5,4},{6,7},{7,6},{8,9},{9,8},{10,11... | collective-permute-start | bytes 6291464 | tf_op jit(solution)/shard_map/ppermute | solution.py:27
  57.2 8.7 %copy-start.8 = (bf16[192,512]{1,0:T(8,128)(2,1)S(1)}, bf16[192,512]{1,0:T(8,128)(2,1)}, u32[]{:S(2)}) copy-start(bf16[192,512]{1,0:T(8,128)(2,1)} %copy-done.7) | copy-start | bytes 589828
  57.2 8.7 %copy-start.10 = (bf16[192,512]{1,0:T(8,128)(2,1)S(1)}, bf16[192,512]{1,0:T(8,128)(2,1)}, u32[]{:S(2)}) copy-start(bf16[192,512]{1,0:T(8,128)(2,1)} %copy-done.9) | copy-start | bytes 589828
  57.2 8.7 %copy-start.12 = (bf16[192,512]{1,0:T(8,128)(2,1)S(1)}, bf16[192,512]{1,0:T(8,128)(2,1)}, u32[]{:S(2)}) copy-start(bf16[192,512]{1,0:T(8,128)(2,1)} %copy-done.11) | copy-start | bytes 589828
  57.2 8.8 %copy-start.16 = (bf16[512,12]{0,1:T(8,128)(2,1)S(1)}, bf16[512,12]{0,1:T(8,128)(2,1)}, u32[]{:S(2)}) copy-start(bf16[512,12]{0,1:T(8,128)(2,1)} %param.21) | copy-start | bytes 36868
  57.2 8.8 %copy-start.17 = (s32[2,512,3]{1,0,2:T(2,128)S(1)}, s32[2,512,3]{1,0,2:T(2,128)}, u32[]{:S(2)}) copy-start(s32[2,512,3]{1,0,2:T(2,128)} %param.17) | copy-start | bytes 36868
  57.9 20.8 %collective-permute-start.13 = (bf16[1024,512]{1,0:T(8,128)(2,1)S(1)}, bf16[1024,512]{1,0:T(8,128)(2,1)S(1)}, u32[]{:S(2)}, u32[]{:S(2)}) collective-permute-start(bf16[1024,512]{1,0:T(8,128)(2,1)S(1)} %get-tuple-element.149), channel_id=1, source_target_pairs={{0,2},{1,5},{2,0},{3,7},{4,6},{5,1},{6,4},{7,3},{8,10},{9,13},{10,... | collective-permute-start | bytes 3145736 | tf_op jit(solution)/shard_map/ppermute | solution.py:37
  78.9 9.7 %collective-permute-start.14 = (bf16[512,512]{1,0:T(8,128)(2,1)S(1)}, bf16[512,512]{1,0:T(8,128)(2,1)S(1)}, u32[]{:S(2)}, u32[]{:S(2)}) collective-permute-start(bf16[512,512]{1,0:T(8,128)(2,1)S(1)} %get-tuple-element.151), channel_id=1, source_target_pairs={{0,4},{1,9},{2,6},{3,11},{4,0},{5,13},{6,2},{7,15},{8,12},{9,1},{1... | collective-permute-start | bytes 1572872 | tf_op jit(solution)/shard_map/ppermute | solution.py:37
  88.8 6.5 %collective-permute-start.15 = (bf16[256,512]{1,0:T(8,128)(2,1)S(1)}, bf16[256,512]{1,0:T(8,128)(2,1)S(1)}, u32[]{:S(2)}, u32[]{:S(2)}) collective-permute-start(bf16[256,512]{1,0:T(8,128)(2,1)S(1)} %get-tuple-element.155), channel_id=1, source_target_pairs={{0,8},{1,3},{2,10},{3,1},{4,12},{5,7},{6,14},{7,5},{8,0},{9,11},{1... | collective-permute-start | bytes 786440 | tf_op jit(solution)/shard_map/ppermute | solution.py:37
  91.0 7.7 %collective-permute-start.18 = (bf16[2,512,128]{2,1,0:T(8,128)(2,1)S(1)}, bf16[2,512,128]{2,1,0:T(8,128)(2,1)S(1)}, u32[]{:S(2)}, u32[]{:S(2)}) collective-permute-start(bf16[2,512,128]{2,1,0:T(8,128)(2,1)S(1)} %get-tuple-element.116), channel_id=1, source_target_pairs={{0,1},{1,0},{2,3},{3,2},{4,5},{5,4},{6,7},{7,6},{8,9},{9,8},{10,11... | collective-permute-start | bytes 786440 | tf_op jit(solution)/shard_map/ppermute | solution.py:27
  91.6 14.4 %collective-permute-start.17 = (bf16[2,512,128]{2,1,0:T(8,128)(2,1)S(1)}, bf16[2,512,128]{2,1,0:T(8,128)(2,1)S(1)}, u32[]{:S(2)}, u32[]{:S(2)}) collective-permute-start(bf16[2,512,128]{2,1,0:T(8,128)(2,1)S(1)} %get-tuple-element.114), channel_id=1, source_target_pairs={{0,1},{1,0},{2,3},{3,2},{4,5},{5,4},{6,7},{7,6},{8,9},{9,8},{10,11... | collective-permute-start | bytes 786440 | tf_op jit(solution)/shard_map/ppermute | solution.py:27
  94.0 19.0 %collective-permute-start.21 = (bf16[768,512]{1,0:T(8,128)(2,1)S(1)}, bf16[768,512]{1,0:T(8,128)(2,1)S(1)}, u32[]{:S(2)}, u32[]{:S(2)}) collective-permute-start(bf16[768,512]{1,0:T(8,128)(2,1)S(1)} %get-tuple-element.123), channel_id=1, source_target_pairs={{0,1},{1,0},{2,3},{3,2},{4,5},{5,4},{6,7},{7,6},{8,9},{9,8},{10,11... | collective-permute-start | bytes 2359304 | tf_op jit(solution)/shard_map/ppermute | solution.py:27
  95.3 10.5 %collective-permute-start.16 = (bf16[128,512]{1,0:T(8,128)(2,1)S(1)}, bf16[128,512]{1,0:T(8,128)(2,1)S(1)}, u32[]{:S(2)}, u32[]{:S(2)}) collective-permute-start(bf16[128,512]{1,0:T(8,128)(2,1)S(1)} %add_convert_fusion.16), channel_id=1, source_target_pairs={{0,16},{1,17},{2,18},{3,19},{4,20},{5,21},{6,22},{7,23},{8,24},{9,... | collective-permute-start | bytes 393224 | tf_op jit(solution)/shard_map/ppermute | solution.py:37
  98.7 16.9 %copy-start.13 = (bf16[512,128]{1,0:T(8,128)(2,1)S(1)}, bf16[512,128]{1,0:T(8,128)(2,1)}, u32[]{:S(2)}) copy-start(bf16[512,128]{1,0:T(8,128)(2,1)} %refs_5_.5) | copy-start | bytes 393220
  98.8 16.9 %copy-start.21 = (bf16[512]{0:T(512)(128)(2,1)S(1)}, bf16[512]{0:T(512)(128)(2,1)}, u32[]{:S(2)}) copy-start(bf16[512]{0:T(512)(128)(2,1)} %refs_4_.5) | copy-start | bytes 3076
  98.8 16.9 %collective-permute-start.20 = (bf16[1,512,128]{2,1,0:T(8,128)(2,1)S(1)}, bf16[1,512,128]{2,1,0:T(8,128)(2,1)S(1)}, u32[]{:S(2)}, u32[]{:S(2)}) collective-permute-start(bf16[1,512,128]{2,1,0:T(8,128)(2,1)S(1)} %get-tuple-element.158), channel_id=1, source_target_pairs={{0,2},{1,3},{2,0},{3,1},{4,6},{5,7},{6,4},{7,5},{8,10},{9,11},{10,... | collective-permute-start | bytes 393224 | tf_op jit(solution)/shard_map/ppermute | solution.py:27
  105.9 7.1 %collective-permute-start.26 = (bf16[128,512]{1,0:T(8,128)(2,1)S(1)}, bf16[128,512]{1,0:T(8,128)(2,1)S(1)}, u32[]{:S(2)}, u32[]{:S(2)}) collective-permute-start(bf16[128,512]{1,0:T(8,128)(2,1)S(1)} %add_convert_fusion.10), channel_id=1, source_target_pairs={{0,16},{1,17},{2,18},{3,19},{4,20},{5,21},{6,22},{7,23},{8,24},{9,... | collective-permute-start | bytes 393224 | tf_op jit(solution)/shard_map/ppermute | solution.py:37
  106.0 9.6 %collective-permute-start.19 = (bf16[1,512,128]{2,1,0:T(8,128)(2,1)S(1)}, bf16[1,512,128]{2,1,0:T(8,128)(2,1)S(1)}, u32[]{:S(2)}, u32[]{:S(2)}) collective-permute-start(bf16[1,512,128]{2,1,0:T(8,128)(2,1)S(1)} %get-tuple-element.160), channel_id=1, source_target_pairs={{0,2},{1,3},{2,0},{3,1},{4,6},{5,7},{6,4},{7,5},{8,10},{9,11},{10,... | collective-permute-start | bytes 393224 | tf_op jit(solution)/shard_map/ppermute | solution.py:27
  113.0 9.1 %collective-permute-start.27 = (bf16[256,512]{1,0:T(8,128)(2,1)S(1)}, bf16[256,512]{1,0:T(8,128)(2,1)S(1)}, u32[]{:S(2)}, u32[]{:S(2)}) collective-permute-start(bf16[256,512]{1,0:T(8,128)(2,1)S(1)} %pad_maximum_fusion.4), channel_id=1, source_target_pairs={{0,8},{1,3},{2,10},{3,1},{4,12},{5,7},{6,14},{7,5},{8,0},{9,11},{1... | collective-permute-start | bytes 786440 | tf_op jit(solution)/shard_map/ppermute | solution.py:37
  113.3 9.9 %collective-permute-start.22 = (bf16[384,512]{1,0:T(8,128)(2,1)S(1)}, bf16[384,512]{1,0:T(8,128)(2,1)S(1)}, u32[]{:S(2)}, u32[]{:S(2)}) collective-permute-start(bf16[384,512]{1,0:T(8,128)(2,1)S(1)} %get-tuple-element.153), channel_id=1, source_target_pairs={{0,2},{1,5},{2,0},{3,7},{4,6},{5,1},{6,4},{7,3},{8,10},{9,13},{10,... | collective-permute-start | bytes 1179656 | tf_op jit(solution)/shard_map/ppermute | solution.py:37
  119.6 3.5 %collective-permute-start.23 = (bf16[80,512]{1,0:T(8,128)(2,1)S(1)}, bf16[80,512]{1,0:T(8,128)(2,1)S(1)}, u32[]{:S(2)}, u32[]{:S(2)}) collective-permute-start(bf16[80,512]{1,0:T(8,128)(2,1)S(1)} %get-tuple-element.125), channel_id=1, source_target_pairs={{0,1},{1,0},{2,3},{3,2},{4,5},{5,4},{6,7},{7,6},{8,9},{9,8},{10,11... | collective-permute-start | bytes 245768 | tf_op jit(solution)/shard_map/ppermute | solution.py:27
  122.1 9.2 %collective-permute-start.28 = (bf16[512,512]{1,0:T(8,128)(2,1)S(1)}, bf16[512,512]{1,0:T(8,128)(2,1)S(1)}, u32[]{:S(2)}, u32[]{:S(2)}) collective-permute-start(bf16[512,512]{1,0:T(8,128)(2,1)S(1)} %pad_maximum_fusion.1), channel_id=1, source_target_pairs={{0,4},{1,9},{2,6},{3,11},{4,0},{5,13},{6,2},{7,15},{8,12},{9,1},{1... | collective-permute-start | bytes 1572872 | tf_op jit(solution)/shard_map/ppermute | solution.py:37
  123.3 12.0 %collective-permute-start.24 = (bf16[272,512]{1,0:T(8,128)(2,1)S(1)}, bf16[272,512]{1,0:T(8,128)(2,1)S(1)}, u32[]{:S(2)}, u32[]{:S(2)}) collective-permute-start(bf16[272,512]{1,0:T(8,128)(2,1)S(1)} %pad_maximum_fusion.3), channel_id=1, source_target_pairs={{0,4},{1,9},{2,6},{3,11},{4,0},{5,13},{6,2},{7,15},{8,12},{9,1},{1... | collective-permute-start | bytes 835592 | tf_op jit(solution)/shard_map/ppermute | solution.py:37
  131.4 17.8 %collective-permute-start.29 = (bf16[1024,512]{1,0:T(8,128)(2,1)S(1)}, bf16[1024,512]{1,0:T(8,128)(2,1)S(1)}, u32[]{:S(2)}, u32[]{:S(2)}) collective-permute-start(bf16[1024,512]{1,0:T(8,128)(2,1)S(1)} %pad_maximum_fusion.own), channel_id=1, source_target_pairs={{0,2},{1,5},{2,0},{3,7},{4,6},{5,1},{6,4},{7,3},{8,10},{9,13},{10,... | collective-permute-start | bytes 3145736 | tf_op jit(solution)/shard_map/ppermute | solution.py:37
  135.5 5.6 %collective-permute-start.25 = (bf16[176,512]{1,0:T(8,128)(2,1)S(1)}, bf16[176,512]{1,0:T(8,128)(2,1)S(1)}, u32[]{:S(2)}, u32[]{:S(2)}) collective-permute-start(bf16[176,512]{1,0:T(8,128)(2,1)S(1)} %pad_maximum_fusion.6), channel_id=1, source_target_pairs={{0,8},{1,3},{2,10},{3,1},{4,12},{5,7},{6,14},{7,5},{8,0},{9,11},{1... | collective-permute-start | bytes 540680 | tf_op jit(solution)/shard_map/ppermute | solution.py:37
  135.5 15.3 %collective-permute-start.32 = (bf16[1024,512]{1,0:T(8,128)(2,1)S(1)}, bf16[1024,512]{1,0:T(8,128)(2,1)S(1)}, u32[]{:S(2)}, u32[]{:S(2)}) collective-permute-start(bf16[1024,512]{1,0:T(8,128)(2,1)S(1)} %pad_maximum_fusion.own), channel_id=1, source_target_pairs={{0,1},{1,0},{2,3},{3,2},{4,5},{5,4},{6,7},{7,6},{8,9},{9,8},{10,11... | collective-permute-start | bytes 3145736 | tf_op jit(solution)/shard_map/ppermute | solution.py:27
  141.1 8.1 %collective-permute-start.30 = (bf16[128,512]{1,0:T(8,128)(2,1)S(1)}, bf16[128,512]{1,0:T(8,128)(2,1)S(1)}, u32[]{:S(2)}, u32[]{:S(2)}) collective-permute-start(bf16[128,512]{1,0:T(8,128)(2,1)S(1)} %pad_maximum_fusion.7), channel_id=1, source_target_pairs={{0,16},{1,17},{2,18},{3,19},{4,20},{5,21},{6,22},{7,23},{8,24},{9,... | collective-permute-start | bytes 393224 | tf_op jit(solution)/shard_map/ppermute | solution.py:37
  149.8 7.1 %collective-permute-start.34 = (bf16[1024,512]{1,0:T(8,128)(2,1)S(1)}, bf16[1024,512]{1,0:T(8,128)(2,1)}, u32[]{:S(2)}, u32[]{:S(2)}) collective-permute-start(bf16[1024,512]{1,0:T(8,128)(2,1)S(1)} %collective-permute-done.29.own), channel_id=1, source_target_pairs={{0,1},{1,0},{2,3},{3,2},{4,5},{5,4},{6,7},{7,6},{8,9},{9,8},{10,11... | collective-permute-start | bytes 3145736 | tf_op jit(solution)/shard_map/ppermute | solution.py:27
  150.7 5.3 %collective-permute-start.31 = (bf16[48,512]{1,0:T(8,128)(2,1)S(1)}, bf16[48,512]{1,0:T(8,128)(2,1)S(1)}, u32[]{:S(2)}, u32[]{:S(2)}) collective-permute-start(bf16[48,512]{1,0:T(8,128)(2,1)S(1)} %add_convert_fusion.24), channel_id=1, source_target_pairs={{0,16},{4,20},{8,24},{12,28},{16,0},{20,4},{24,8},{28,12},{1,17},{... | collective-permute-start | bytes 147464 | tf_op jit(solution)/shard_map/ppermute | solution.py:27
  156.0 5.4 %collective-permute-start.33 = (bf16[96,512]{1,0:T(8,128)(2,1)S(1)}, bf16[96,512]{1,0:T(8,128)(2,1)S(1)}, u32[]{:S(2)}, u32[]{:S(2)}) collective-permute-start(bf16[96,512]{1,0:T(8,128)(2,1)S(1)} %pad_maximum_fusion.8), channel_id=1, source_target_pairs={{0,8},{4,12},{8,0},{12,4},{16,24},{20,28},{24,16},{28,20},{1,9},{5... | collective-permute-start | bytes 294920 | tf_op jit(solution)/shard_map/ppermute | solution.py:27
  156.5 7.8 %collective-permute-start.36 = (bf16[80,512]{1,0:T(8,128)(2,1)S(1)}, bf16[80,512]{1,0:T(8,128)(2,1)S(1)}, u32[]{:S(2)}, u32[]{:S(2)}) collective-permute-start(bf16[80,512]{1,0:T(8,128)(2,1)S(1)} %add_convert_fusion.20), channel_id=1, source_target_pairs={{0,2},{1,5},{2,0},{3,7},{4,6},{5,1},{6,4},{7,3},{8,10},{9,13},{10,... | collective-permute-start | bytes 245768 | tf_op jit(solution)/shard_map/ppermute | solution.py:37
  161.4 7.9 %collective-permute-start.35 = (bf16[192,512]{1,0:T(8,128)(2,1)S(1)}, bf16[192,512]{1,0:T(8,128)(2,1)S(1)}, u32[]{:S(2)}, u32[]{:S(2)}) collective-permute-start(bf16[192,512]{1,0:T(8,128)(2,1)S(1)} %pad_maximum_fusion.5), channel_id=1, source_target_pairs={{0,4},{4,0},{8,12},{12,8},{16,20},{20,16},{24,28},{28,24},{1,5},{5... | collective-permute-start | bytes 589832 | tf_op jit(solution)/shard_map/ppermute | solution.py:27
  164.4 4.9 %collective-permute-start.37 = (bf16[80,512]{1,0:T(8,128)(2,1)S(1)}, bf16[80,512]{1,0:T(8,128)(2,1)S(1)}, u32[]{:S(2)}, u32[]{:S(2)}) collective-permute-start(bf16[80,512]{1,0:T(8,128)(2,1)S(1)} %add_convert_fusion.19.own), channel_id=1, source_target_pairs={{0,1},{1,0},{2,3},{3,2},{4,5},{5,4},{6,7},{7,6},{8,9},{9,8},{10,11... | collective-permute-start | bytes 245768 | tf_op jit(solution)/shard_map/ppermute | solution.py:27
  (24 other events, 97.0 us)

commit v5 on v4

--- a/solution.py
+++ b/solution.py
@@ -311,8 +311,8 @@
     meta, tokens, cotan, gain, shift, down_bias, w_up, up_bias, w_down = refs[:9]
     mixt = refs[9 : 9 + micros]
     wo = refs[9 + micros : 9 + micros + groups]
-    block_out, gh, own, sent, up_row, rows = refs[9 + micros + groups : 15 + micros + groups]
-    hidden, second, acc, grad_acc, act_s, gu_s = refs[15 + micros + groups :]
+    own, sent, up_row, hidden, acc, grad_acc = refs[9 + micros + groups : 15 + micros + groups]
+    second, act_s, gu_s = refs[15 + micros + groups :]
     total, width = hidden.shape
     tok = tokens.shape[1]
     size = wo[0].shape[0]
@@ -374,6 +374,10 @@
         return carry
 
     lax.fori_loop(0, w_up.shape[1] // tile, one_tile, 0)
+
+
+def second_norm_kernel(sub, cotan, gain, down_bias, hidden, acc, grad_acc, block_out, gh, rows):
+    total, width = hidden.shape
     sums = [jnp.zeros((1, width), f32) for _ in range(3)]
     for i in range(total // sub):
         at = slice(i * sub, (i + 1) * sub)
@@ -616,7 +620,7 @@
             target.append(value)
 
     f_tile = 512
-    block_out, gh, ffn_own, ffn_sent, up_row, ffn_rows = call(
+    ffn_own, ffn_sent, up_row, hidden, acc, grad_acc = call(
         functools.partial(ffn_kernel, (chunk, f_tile, min(512, tok), micros, groups)),
         [meta],
         [
@@ -625,15 +629,22 @@
         ]
         + mixt + wo,
         [
-            ((total, width), b16), ((total, width), f32), ((hidden_units, width), b16),
-            ((hidden_units, width), b16), ((1, hidden_units), f32), ((8, width), f32),
+            ((hidden_units, width), b16), ((hidden_units, width), b16), ((1, hidden_units), f32),
+            ((total, width), f32), ((total, width), f32), ((total, width), f32),
         ],
         [
-            ((total, width), f32), ((total, width), b16), ((total, width), f32),
-            ((total, width), f32), ((total, f_tile), b16), ((total, f_tile), b16),
+            ((total, width), b16), ((total, f_tile), b16), ((total, f_tile), b16),
         ],
-        limit=32,
+        limit=26,
         cost=11,
+    )
+
+    block_out, gh, ffn_rows = call(
+        functools.partial(second_norm_kernel, min(512, tok)),
+        [],
+        [cotangent.reshape(total, width), gain_two, down_bias, hidden, acc, grad_acc],
+        [((total, width), b16), ((total, width), f32), ((8, width), f32)],
+        cost=1.5,
     )
 
     part, gq, chosen, kept, arrived, tokens_back = [], [], [], [], [], []
@@ -759,7 +770,7 @@
         if i == len(ways_up) - 3:
             filled = ordered(0, own_low, got_low, ())
             came, *filled = lax.optimization_barrier((came, *filled))
-        if i == len(ways_up) - 2:
+        if i == len(ways_up) - 1:
             filled = ordered(1, own_high, got_high, filled)
             came, *filled = lax.optimization_barrier((came, *filled))
         weights = jnp.concatenate([weights, came], axis=0)

time: 171 us -> 166 us (0.971)
  waiting for transfers between devices: 57.8 us -> 51.6 us
    ppermute x13, waiting for transfers between devices: 41.2 us -> 33.8 us  [hop(): return lax.ppermute(values, ('batch', 'expert'), pairs)]
    pallas_call x9 -> x10, Pallas kernels: 52.2 us -> 52.2 us  [call(): pl.pallas_call(kernel, in_specs=[smem] * len(scalars) + [far_spec if i in...]
  transfers between devices with their start and end apart: 38 -> 38, of which waited for: 17 -> 19; matrix products, arithmetic and copies ran while one was open for 2% -> 2% of each run, Pallas kernels for 22% -> 24%
where the time goes in v5:
time: 166 us
  Pallas kernels  60 us (36%)
  waiting for transfers between devices  51.6 us (31%)
  starting transfers between devices  46.7 us (28%)
  other arithmetic  3.66 us (2%)
  local copies, waits for them, and re-layouts  2.85 us (2%)
    pallas_call x10, Pallas kernels, call(): pl.pallas_call(kernel, in_specs=[smem] * len(scalars) + [far_spec if i in...  52.2 us
    ppermute x13, waiting for transfers between devices, hop(): return lax.ppermute(values, ('batch', 'expert'), pairs)  33.8 us
    ppermute x13, starting transfers between devices, hop(): return lax.ppermute(values, ('batch', 'expert'), pairs)  25.3 us
    ppermute x25, starting transfers between devices, flip(): return lax.ppermute(values, axis, [(i, i ^ 1 << bit) for i in range(size)])  21.4 us
    ppermute x25, waiting for transfers between devices, flip(): return lax.ppermute(values, axis, [(i, i ^ 1 << bit) for i in range(size)])  17.8 us
    pallas_call x2, Pallas kernels, ordered(): pl.pallas_call(functools.partial(order_kernel, chunk, top_bit, side), gri...  7.79 us
  transfers between devices with their start and end apart: 38, of which 19 were waited for; matrix products, arithmetic and copies ran while one was open for 2% of the time, Pallas kernels for 24%

profile of v5, /device:TPU:0, one launch (start us, length us, event | category | flops | bytes accessed | tf_op | source)
XLA Modules:
  0.0 166.3 jit_solution(5326055357197690594)
XLA Ops:
  0.6 3.0 %collective-permute-start.3 = (bf16[192,512]{1,0:T(8,128)(2,1)}, bf16[192,512]{1,0:T(8,128)(2,1)S(1)}, u32[]{:S(2)}, u32[]{:S(2)}) collective-permute-start(bf16[192,512]{1,0:T(8,128)(2,1)} %bitcast.19), channel_id=1, source_target_pairs={{0,2},{1,3},{2,0},{3,1},{4,6},{5,7},{6,4},{7,5},{8,10},{9,11},{10,... | collective-permute-start | bytes 589832 | tf_op jit(solution)/shard_map/ppermute | solution.py:27
  3.7 2.5 %shard_map.263 = (bf16[512,512]{1,0:T(8,128)(2,1)S(1)}, bf16[512,512]{1,0:T(8,128)(2,1)S(1)}, bf16[512,128]{1,0:T(8,128)(2,1)S(1)}, bf16[512,128]{1,0:T(8,128)(2...) custom-call(bf16[2,512,512]{2,1,0:T(8,128)(2,1)} %refs_2_.1, bf16[512,128]{1,0:T(8,128)(2,1)} %refs_5_.5, ...), custom_call_target="tpu_custom_call" | custom-call | flops 2640000000 | tf_op jit(solution)/shard_map/pallas_call | solution.py:566
  6.3 2.9 %collective-permute-done.3.refs_9_.refs_11_ = bf16[192,512]{1,0:T(8,128)(2,1)S(1)} collective-permute-done((bf16[192,512]{1,0:T(8,128)(2,1)}, bf16[192,512]{1,0:T(8,128)(2,1)S(1)}, u32[]{:S(2)}, u32[]{:S(2)}) %collective-permute-start.3) | collective-permute-done | bytes 196640 | tf_op jit(solution)/shard_map/ppermute | solution.py:27
  9.8 1.8 %collective-permute-done.refs_5_ = bf16[512,128]{1,0:T(8,128)(2,1)S(1)} collective-permute-done((bf16[512,128]{1,0:T(8,128)(2,1)S(1)}, bf16[512,128]{1,0:T(8,128)(2,1)S(1)}, u32[]{:S(2)}, u32[]{:S(2)}) %collective-permute-start) | collective-permute-done | bytes 131104 | tf_op jit(solution)/shard_map/ppermute | solution.py:27
  11.6 1.8 %collective-permute-start.9 = (bf16[192,512]{1,0:T(8,128)(2,1)S(1)}, bf16[192,512]{1,0:T(8,128)(2,1)S(1)}, u32[]{:S(2)}, u32[]{:S(2)}) collective-permute-start(bf16[192,512]{1,0:T(8,128)(2,1)S(1)} %bitcast.25), channel_id=1, source_target_pairs={{0,2},{1,3},{2,0},{3,1},{4,6},{5,7},{6,4},{7,5},{8,10},{9,11},{10,... | collective-permute-start | bytes 589832 | tf_op jit(solution)/shard_map/ppermute | solution.py:27
  13.9 0.7 reduce.3
  15.9 4.9 %shard_map.264 = (bf16[2048,128]{1,0:T(8,128)(2,1)S(1)}, bf16[128,2048]{1,0:T(8,128)(2,1)S(1)}, bf16[2,64,768]{2,1,0:T(8,128)(2,1)S(1)}, f32[2,64,768]{2,1,0:T(8...) custom-call(s32[28]{0:T(128)S(1)} %concatenate.34.refs_0_.meta, ...), custom_call_target="tpu_custom_call" | custom-call | flops 5500000256 | tf_op jit(solution)/shard_map/pallas_call | solution.py:566
  20.8 0.9 collective-permute-done.6.refs_5_
  21.7 1.2 collective-permute-start.7
  24.9 5.4 %shard_map.265 = (bf16[2048,128]{1,0:T(8,128)(2,1)S(1)}, bf16[128,2048]{1,0:T(8,128)(2,1)S(1)}, bf16[2,64,768]{2,1,0:T(8,128)(2,1)S(1)}, f32[2,64,768]{2,1,0:T(8...) custom-call(s32[28]{0:T(128)S(1)} %concatenate.34.refs_0_.meta, ...), custom_call_target="tpu_custom_call" | custom-call | flops 5500000256 | tf_op jit(solution)/shard_map/pallas_call | solution.py:566
  30.4 19.2 %shard_map.266 = (bf16[2048,512]{1,0:T(8,128)(2,1)S(1)}, bf16[2048,512]{1,0:T(8,128)(2,1)S(1)}, f32[1,2048]{1,0:T(1,128)S(1)}, f32[1024,512]{1,0:T(8,128)S(1)}, ...) custom-call(s32[28]{0:T(128)S(1)} %concatenate.34.refs_0_.meta, bf16[2,512,512]{2,1,0:T(8,128)(2,1)S(1)} %copy-done.5, ...), custom_call_target="tpu_custom_call" | custom-call | flops 12099999744 | tf_op jit(solution)/shard_map/pallas_call | solution.py:566
  49.6 1.3 collective-permute-start.12
  51.0 3.7 %collective-permute-done.12 = bf16[2048,512]{1,0:T(8,128)(2,1)S(1)} collective-permute-done((bf16[2048,512]{1,0:T(8,128)(2,1)S(1)}, bf16[2048,512]{1,0:T(8,128)(2,1)S(1)}, u32[]{:S(2)}, u32[]{:S(2)}) %collective-permute-start.12) | collective-permute-done | bytes 2097184 | tf_op jit(solution)/shard_map/ppermute | solution.py:27
  55.3 8.5 %collective-permute-start.13 = (bf16[1024,512]{1,0:T(8,128)(2,1)S(1)}, bf16[1024,512]{1,0:T(8,128)(2,1)S(1)}, u32[]{:S(2)}, u32[]{:S(2)}) collective-permute-start(bf16[1024,512]{1,0:T(8,128)(2,1)S(1)} %get-tuple-element.155), channel_id=1, source_target_pairs={{0,2},{1,5},{2,0},{3,7},{4,6},{5,1},{6,4},{7,3},{8,10},{9,13},{10,... | collective-permute-start | bytes 3145736 | tf_op jit(solution)/shard_map/ppermute | solution.py:37
  63.9 2.4 %shard_map.267 = (bf16[1024,512]{1,0:T(8,128)(2,1)}, f32[1024,512]{1,0:T(8,128)S(1)}, f32[8,512]{1,0:T(8,128)S(1)}) custom-call(bf16[1024,512]{1,0:T(8,128)(2,1)S(1)} %bitcast.18, bf16[512]{0:T(512)(128)(2,1)S(1)} %copy-done.1, bf16[512]{0:T(512)(128)(2,1)S(1)} %copy-done.2, f32[1024,512]{1,0:T(8,128)S(1)} %get-tuple-element.95.hidden, ...), custom_call_target="tpu_custom_call" | custom-call | flops 1650000000 | tf_op jit(solution)/shard_map/pallas_call | solution.py:566
  66.3 5.0 %shard_map.268 = (f32[512,512]{1,0:T(8,128)S(1)}, bf16[2,512,128]{2,1,0:T(8,128)(2,1)S(1)}, bf16[2,512,128]{2,1,0:T(8,128)(2,1)S(1)}, bf16[768,512]{1,0:T(8,128)...) custom-call(s32[28]{0:T(128)S(1)} %concatenate.34.refs_0_.meta, ...), custom_call_target="tpu_custom_call" | custom-call | flops 9900000256 | tf_op jit(solution)/shard_map/pallas_call | solution.py:566
  71.3 5.3 %collective-permute-done.13 = bf16[1024,512]{1,0:T(8,128)(2,1)S(1)} collective-permute-done((bf16[1024,512]{1,0:T(8,128)(2,1)S(1)}, bf16[1024,512]{1,0:T(8,128)(2,1)S(1)}, u32[]{:S(2)}, u32[]{:S(2)}) %collective-permute-start.13) | collective-permute-done | bytes 1048608 | tf_op jit(solution)/shard_map/ppermute | solution.py:37
  76.9 1.6 collective-permute-start.14
  78.5 5.0 %shard_map.269 = (f32[512,512]{1,0:T(8,128)S(1)}, bf16[2,512,128]{2,1,0:T(8,128)(2,1)S(1)}, bf16[2,512,128]{2,1,0:T(8,128)(2,1)S(1)}, bf16[768,512]{1,0:T(8,128)...) custom-call(s32[28]{0:T(128)S(1)} %concatenate.34.refs_0_.meta, ...), custom_call_target="tpu_custom_call" | custom-call | flops 9900000256 | tf_op jit(solution)/shard_map/pallas_call | solution.py:566
  83.5 2.7 %collective-permute-done.14.refs_1_ = bf16[512,512]{1,0:T(8,128)(2,1)S(1)} collective-permute-done((bf16[512,512]{1,0:T(8,128)(2,1)S(1)}, bf16[512,512]{1,0:T(8,128)(2,1)S(1)}, u32[]{:S(2)}, u32[]{:S(2)}) %collective-permute-start.14) | collective-permute-done | bytes 524320 | tf_op jit(solution)/shard_map/ppermute | solution.py:37
  86.3 1.6 collective-permute-start.15
  88.0 2.9 %collective-permute-start.18 = (bf16[2,512,128]{2,1,0:T(8,128)(2,1)S(1)}, bf16[2,512,128]{2,1,0:T(8,128)(2,1)S(1)}, u32[]{:S(2)}, u32[]{:S(2)}) collective-permute-start(bf16[2,512,128]{2,1,0:T(8,128)(2,1)S(1)} %get-tuple-element.122), channel_id=1, source_target_pairs={{0,1},{1,0},{2,3},{3,2},{4,5},{5,4},{6,7},{7,6},{8,9},{9,8},{10,11... | collective-permute-start | bytes 786440 | tf_op jit(solution)/shard_map/ppermute | solution.py:27
  91.0 2.4 %shard_map.271 = (bf16[768,512]{1,0:T(8,128)(2,1)S(1)}, bf16[768,512]{1,0:T(8,128)(2,1)S(1)}) custom-call(s32[4,8]{1,0:T(4,128)S(1)} %select_select_fusion.refs_0_, bf16[512,512]{1,0:T(8,128)(2,1)} %copy-done.26, f32[1024,512]{1,0:T(8,128)S(1)} %get-tuple-element.101.refs_1_.refs_3_.refs_2_, bf16[768,512]{1,0:T(8,128)(2,1)S(1)} %get-tuple-element.126.refs_3_, ...), custom_call_target="tpu_custom_call" | custom-call | flops 1650000000 | tf_op jit(solution)/shard_map/pallas_call | solution.py:566
  93.9 0.7 collective-permute-start.16
  94.7 4.7 %collective-permute-start.20 = (bf16[1,512,128]{2,1,0:T(8,128)(2,1)S(1)}, bf16[1,512,128]{2,1,0:T(8,128)(2,1)S(1)}, u32[]{:S(2)}, u32[]{:S(2)}) collective-permute-start(bf16[1,512,128]{2,1,0:T(8,128)(2,1)S(1)} %get-tuple-element.164), channel_id=1, source_target_pairs={{0,2},{1,3},{2,0},{3,1},{4,6},{5,7},{6,4},{7,5},{8,10},{9,11},{10,... | collective-permute-start | bytes 393224 | tf_op jit(solution)/shard_map/ppermute | solution.py:27
  99.4 4.3 %collective-permute-done.16.refs_1_ = bf16[128,512]{1,0:T(8,128)(2,1)S(1)} collective-permute-done((bf16[128,512]{1,0:T(8,128)(2,1)S(1)}, bf16[128,512]{1,0:T(8,128)(2,1)S(1)}, u32[]{:S(2)}, u32[]{:S(2)}) %collective-permute-start.16) | collective-permute-done | bytes 131104 | tf_op jit(solution)/shard_map/ppermute | solution.py:37
  104.0 3.3 %collective-permute-start.19 = (bf16[1,512,128]{2,1,0:T(8,128)(2,1)S(1)}, bf16[1,512,128]{2,1,0:T(8,128)(2,1)S(1)}, u32[]{:S(2)}, u32[]{:S(2)}) collective-permute-start(bf16[1,512,128]{2,1,0:T(8,128)(2,1)S(1)} %get-tuple-element.166), channel_id=1, source_target_pairs={{0,2},{1,3},{2,0},{3,1},{4,6},{5,7},{6,4},{7,5},{8,10},{9,11},{10,... | collective-permute-start | bytes 393224 | tf_op jit(solution)/shard_map/ppermute | solution.py:27
  107.2 3.0 %collective-permute-done.26 = bf16[128,512]{1,0:T(8,128)(2,1)S(1)} collective-permute-done((bf16[128,512]{1,0:T(8,128)(2,1)S(1)}, bf16[128,512]{1,0:T(8,128)(2,1)S(1)}, u32[]{:S(2)}, u32[]{:S(2)}) %collective-permute-start.26) | collective-permute-done | bytes 131104 | tf_op jit(solution)/shard_map/ppermute | solution.py:37
  110.6 3.1 %collective-permute-start.22 = (bf16[384,512]{1,0:T(8,128)(2,1)S(1)}, bf16[384,512]{1,0:T(8,128)(2,1)S(1)}, u32[]{:S(2)}, u32[]{:S(2)}) collective-permute-start(bf16[384,512]{1,0:T(8,128)(2,1)S(1)} %get-tuple-element.159), channel_id=1, source_target_pairs={{0,2},{1,5},{2,0},{3,7},{4,6},{5,1},{6,4},{7,3},{8,10},{9,13},{10,... | collective-permute-start | bytes 1179656 | tf_op jit(solution)/shard_map/ppermute | solution.py:37
  113.7 4.0 %shard_map.270 = (f32[2,512,512]{2,1,0:T(8,128)}, bf16[80,512]{1,0:T(8,128)(2,1)S(1)}, bf16[80,512]{1,0:T(8,128)(2,1)S(1)}) custom-call(s32[28]{0:T(128)S(1)} %concatenate.34.refs_0_.meta, bf16[128,512]{1,0:T(8,128)(2,1)} %copy-done.29, bf16[2,512,512]{2,1,0:T(8,128)(2,1)S(1)} %copy-done.5, f32[1024,512]{1,0:T(8,128)S(1)} %get-tuple-element.101.refs_1_.refs_3_.refs_2_, ...), custom_call_target="tpu_custom_call" | custom-call | flops 4180000000 | tf_op jit(solution)/shard_map/pallas_call | solution.py:566
  118.2 0.7 collective-permute-done.23
  119.0 1.3 collective-permute-done.22
  120.4 0.7 collective-permute-start.24
  121.0 5.9 %collective-permute-done.28 = bf16[512,512]{1,0:T(8,128)(2,1)S(1)} collective-permute-done((bf16[512,512]{1,0:T(8,128)(2,1)S(1)}, bf16[512,512]{1,0:T(8,128)(2,1)S(1)}, u32[]{:S(2)}, u32[]{:S(2)}) %collective-permute-start.28) | collective-permute-done | bytes 524320 | tf_op jit(solution)/shard_map/ppermute | solution.py:37
  127.0 2.1 %collective-permute-start.29 = (bf16[1024,512]{1,0:T(8,128)(2,1)S(1)}, bf16[1024,512]{1,0:T(8,128)(2,1)S(1)}, u32[]{:S(2)}, u32[]{:S(2)}) collective-permute-start(bf16[1024,512]{1,0:T(8,128)(2,1)S(1)} %pad_maximum_fusion.own), channel_id=1, source_target_pairs={{0,2},{1,5},{2,0},{3,7},{4,6},{5,1},{6,4},{7,3},{8,10},{9,13},{10,... | collective-permute-start | bytes 3145736 | tf_op jit(solution)/shard_map/ppermute | solution.py:37
  129.1 1.0 collective-permute-done.24
  130.3 2.3 %collective-permute-start.25 = (bf16[176,512]{1,0:T(8,128)(2,1)S(1)}, bf16[176,512]{1,0:T(8,128)(2,1)S(1)}, u32[]{:S(2)}, u32[]{:S(2)}) collective-permute-start(bf16[176,512]{1,0:T(8,128)(2,1)S(1)} %pad_maximum_fusion.6), channel_id=1, source_target_pairs={{0,8},{1,3},{2,10},{3,1},{4,12},{5,7},{6,14},{7,5},{8,0},{9,11},{1... | collective-permute-start | bytes 540680 | tf_op jit(solution)/shard_map/ppermute | solution.py:37
  132.6 3.5 %collective-permute-done.25 = bf16[176,512]{1,0:T(8,128)(2,1)S(1)} collective-permute-done((bf16[176,512]{1,0:T(8,128)(2,1)S(1)}, bf16[176,512]{1,0:T(8,128)(2,1)S(1)}, u32[]{:S(2)}, u32[]{:S(2)}) %collective-permute-start.25) | collective-permute-done | bytes 180256 | tf_op jit(solution)/shard_map/ppermute | solution.py:37
  136.2 3.1 %collective-permute-start.30 = (bf16[128,512]{1,0:T(8,128)(2,1)S(1)}, bf16[128,512]{1,0:T(8,128)(2,1)S(1)}, u32[]{:S(2)}, u32[]{:S(2)}) collective-permute-start(bf16[128,512]{1,0:T(8,128)(2,1)S(1)} %pad_maximum_fusion.7), channel_id=1, source_target_pairs={{0,16},{1,17},{2,18},{3,19},{4,20},{5,21},{6,22},{7,23},{8,24},{9,... | collective-permute-start | bytes 393224 | tf_op jit(solution)/shard_map/ppermute | solution.py:37
  139.3 6.7 %collective-permute-done.30 = bf16[128,512]{1,0:T(8,128)(2,1)S(1)} collective-permute-done((bf16[128,512]{1,0:T(8,128)(2,1)S(1)}, bf16[128,512]{1,0:T(8,128)(2,1)S(1)}, u32[]{:S(2)}, u32[]{:S(2)}) %collective-permute-start.30) | collective-permute-done | bytes 131104 | tf_op jit(solution)/shard_map/ppermute | solution.py:37
  146.7 0.9 add_convert_fusion.24
  147.8 3.3 %shard_map.272 = (f32[2048,512]{1,0:T(8,128)}, f32[512,2048]{1,0:T(8,128)}) custom-call(s32[28]{0:T(128)S(1)} %concatenate.34.refs_0_.meta, bf16[1024,512]{1,0:T(8,128)(2,1)S(1)} %pad_maximum_fusion.own, bf16[1024,512]{1,0:T(8,128)(2,1)S(1)} %collective-permute-done.32.got), custom_call_target="tpu_custom_call" | custom-call | bytes 6291456 | tf_op jit(solution)/shard_map/pallas_call | solution.py:724
  151.1 2.4 %collective-permute-done.31 = bf16[48,512]{1,0:T(8,128)(2,1)S(1)} collective-permute-done((bf16[48,512]{1,0:T(8,128)(2,1)S(1)}, bf16[48,512]{1,0:T(8,128)(2,1)S(1)}, u32[]{:S(2)}, u32[]{:S(2)}) %collective-permute-start.31) | collective-permute-done | bytes 49184 | tf_op jit(solution)/shard_map/ppermute | solution.py:27
  154.0 1.0 collective-permute-start.36
  155.0 3.4 %collective-permute-done.33 = bf16[96,512]{1,0:T(8,128)(2,1)S(1)} collective-permute-done((bf16[96,512]{1,0:T(8,128)(2,1)S(1)}, bf16[96,512]{1,0:T(8,128)(2,1)S(1)}, u32[]{:S(2)}, u32[]{:S(2)}) %collective-permute-start.33) | collective-permute-done | bytes 98336 | tf_op jit(solution)/shard_map/ppermute | solution.py:27
  158.7 4.5 %shard_map.273 = (f32[2048,512]{1,0:T(8,128)}, f32[512,2048]{1,0:T(8,128)}) custom-call(s32[28]{0:T(128)S(1)} %concatenate.34.refs_0_.meta, bf16[1024,512]{1,0:T(8,128)(2,1)S(1)} %collective-permute-done.29.own, bf16[1024,512]{1,0:T(8,128)(2,1)} %collective-permute-done.35.got, ...), custom_call_target="tpu_custom_call", output_to_operand_aliasing={{0}: (3, {}), {1}: (4, {})} | custom-call | bytes 6291456 | tf_op jit(solution)/shard_map/pallas_call | solution.py:724
  163.2 1.3 collective-permute-done.34
  164.5 1.6 shard_map.274
  (154 shorter events, 9.5 us)
Async XLA Ops:
  0.6 8.6 %collective-permute-start.3 = (bf16[192,512]{1,0:T(8,128)(2,1)}, bf16[192,512]{1,0:T(8,128)(2,1)S(1)}, u32[]{:S(2)}, u32[]{:S(2)}) collective-permute-start(bf16[192,512]{1,0:T(8,128)(2,1)} %bitcast.19), channel_id=1, source_target_pairs={{0,2},{1,3},{2,0},{3,1},{4,6},{5,7},{6,4},{7,5},{8,10},{9,11},{10,... | collective-permute-start | bytes 589832 | tf_op jit(solution)/shard_map/ppermute | solution.py:27
  3.7 7.9 %copy-start.8 = (bf16[3,64,512]{2,1,0:T(8,128)(2,1)S(1)}, bf16[3,64,512]{2,1,0:T(8,128)(2,1)}, u32[]{:S(2)}) copy-start(bf16[3,64,512]{2,1,0:T(8,128)(2,1)} %param.24) | copy-start | bytes 589828
  3.7 10.2 %copy-start.31 = (s32[2,1,8]{2,1,0:T(1,128)S(1)}, s32[2,1,8]{2,1,0:T(1,128)}, u32[]{:S(2)}) copy-start(s32[2,1,8]{2,1,0:T(1,128)} %param.18) | copy-start | bytes 196
  6.1 9.0 %copy-start.19 = (bf16[512,128]{1,0:T(8,128)(2,1)}, bf16[512,128]{1,0:T(8,128)(2,1)S(1)}, u32[]{:S(2)}) copy-start(bf16[512,128]{1,0:T(8,128)(2,1)S(1)} %get-tuple-element.86.refs_4_) | copy-start | bytes 393220
  6.1 15.6 %copy-start.18 = (bf16[512,128]{1,0:T(8,128)(2,1)}, bf16[512,128]{1,0:T(8,128)(2,1)S(1)}, u32[]{:S(2)}) copy-start(bf16[512,128]{1,0:T(8,128)(2,1)S(1)} %get-tuple-element.92.refs_4_) | copy-start | bytes 393220
  6.2 18.1 %copy-start.24 = (f32[8,512]{1,0:T(8,128)}, f32[8,512]{1,0:T(8,128)S(1)}, u32[]{:S(2)}) copy-start(f32[8,512]{1,0:T(8,128)S(1)} %get-tuple-element.89.refs_3_) | copy-start | bytes 49156
  6.2 5.4 %collective-permute-start = (bf16[512,128]{1,0:T(8,128)(2,1)S(1)}, bf16[512,128]{1,0:T(8,128)(2,1)S(1)}, u32[]{:S(2)}, u32[]{:S(2)}) collective-permute-start(bf16[512,128]{1,0:T(8,128)(2,1)S(1)} %get-tuple-element.86.refs_4_), channel_id=1, source_target_pairs={{0,2},{1,3},{2,0},{3,1},{4,6},{5,7},{6,4},{7,5},{8,10},{9,11},{10,... | collective-permute-start | bytes 393224 | tf_op jit(solution)/shard_map/ppermute | solution.py:27
  6.3 8.8 %collective-permute-start.4 = (bf16[192,512]{1,0:T(8,128)(2,1)S(1)}, bf16[192,512]{1,0:T(8,128)(2,1)S(1)}, u32[]{:S(2)}, u32[]{:S(2)}) collective-permute-start(bf16[192,512]{1,0:T(8,128)(2,1)S(1)} %bitcast.22), channel_id=1, source_target_pairs={{0,1},{1,0},{2,3},{3,2},{4,5},{5,4},{6,7},{7,6},{8,9},{9,8},{10,11... | collective-permute-start | bytes 589832 | tf_op jit(solution)/shard_map/ppermute | solution.py:27
  9.3 5.9 %collective-permute-start.5 = (bf16[192,512]{1,0:T(8,128)(2,1)S(1)}, bf16[192,512]{1,0:T(8,128)(2,1)S(1)}, u32[]{:S(2)}, u32[]{:S(2)}) collective-permute-start(bf16[192,512]{1,0:T(8,128)(2,1)S(1)} %collective-permute-done.3.refs_9_.refs_11_), channel_id=1, source_target_pairs={{0,1},{1,0},{2,3},{3,2},{4,5},{5,4},{6,7},{7,6},{8,9},{9,8},{10,11... | collective-permute-start | bytes 589832 | tf_op jit(solution)/shard_map/ppermute | solution.py:27
  9.3 5.5 %collective-permute-start.1 = (bf16[512,128]{1,0:T(8,128)(2,1)S(1)}, bf16[512,128]{1,0:T(8,128)(2,1)S(1)}, u32[]{:S(2)}, u32[]{:S(2)}) collective-permute-start(bf16[512,128]{1,0:T(8,128)(2,1)S(1)} %get-tuple-element.86.refs_4_), channel_id=1, source_target_pairs={{0,1},{1,0},{2,3},{3,2},{4,5},{5,4},{6,7},{7,6},{8,9},{9,8},{10,11... | collective-permute-start | bytes 393224 | tf_op jit(solution)/shard_map/ppermute | solution.py:27
  11.6 3.5 %collective-permute-start.2 = (bf16[512,128]{1,0:T(8,128)(2,1)S(1)}, bf16[512,128]{1,0:T(8,128)(2,1)S(1)}, u32[]{:S(2)}, u32[]{:S(2)}) collective-permute-start(bf16[512,128]{1,0:T(8,128)(2,1)S(1)} %collective-permute-done.refs_5_), channel_id=1, source_target_pairs={{0,1},{1,0},{2,3},{3,2},{4,5},{5,4},{6,7},{7,6},{8,9},{9,8},{10,11... | collective-permute-start | bytes 393224 | tf_op jit(solution)/shard_map/ppermute | solution.py:27
  11.6 11.8 %collective-permute-start.9 = (bf16[192,512]{1,0:T(8,128)(2,1)S(1)}, bf16[192,512]{1,0:T(8,128)(2,1)S(1)}, u32[]{:S(2)}, u32[]{:S(2)}) collective-permute-start(bf16[192,512]{1,0:T(8,128)(2,1)S(1)} %bitcast.25), channel_id=1, source_target_pairs={{0,2},{1,3},{2,0},{3,1},{4,6},{5,7},{6,4},{7,5},{8,10},{9,11},{10,... | collective-permute-start | bytes 589832 | tf_op jit(solution)/shard_map/ppermute | solution.py:27
  14.8 7.0 %collective-permute-start.6 = (bf16[512,128]{1,0:T(8,128)(2,1)S(1)}, bf16[512,128]{1,0:T(8,128)(2,1)S(1)}, u32[]{:S(2)}, u32[]{:S(2)}) collective-permute-start(bf16[512,128]{1,0:T(8,128)(2,1)S(1)} %get-tuple-element.92.refs_4_), channel_id=1, source_target_pairs={{0,2},{1,3},{2,0},{3,1},{4,6},{5,7},{6,4},{7,5},{8,10},{9,11},{10,... | collective-permute-start | bytes 393224 | tf_op jit(solution)/shard_map/ppermute | solution.py:27
  15.9 7.5 %copy-start.30 = (bf16[2048]{0:T(1024)(128)(2,1)S(1)}, bf16[2048]{0:T(1024)(128)(2,1)}, u32[]{:S(2)}) copy-start(bf16[2048]{0:T(1024)(128)(2,1)} %param.28) | copy-start | bytes 12292
  21.7 2.2 %collective-permute-start.7 = (bf16[512,128]{1,0:T(8,128)(2,1)S(1)}, bf16[512,128]{1,0:T(8,128)(2,1)S(1)}, u32[]{:S(2)}, u32[]{:S(2)}) collective-permute-start(bf16[512,128]{1,0:T(8,128)(2,1)S(1)} %get-tuple-element.92.refs_4_), channel_id=1, source_target_pairs={{0,1},{1,0},{2,3},{3,2},{4,5},{5,4},{6,7},{7,6},{8,9},{9,8},{10,11... | collective-permute-start | bytes 393224 | tf_op jit(solution)/shard_map/ppermute | solution.py:27
  22.9 1.3 collective-permute-start.8
  23.0 7.4 %collective-permute-start.10 = (bf16[192,512]{1,0:T(8,128)(2,1)S(1)}, bf16[192,512]{1,0:T(8,128)(2,1)S(1)}, u32[]{:S(2)}, u32[]{:S(2)}) collective-permute-start(bf16[192,512]{1,0:T(8,128)(2,1)S(1)} %bitcast.26), channel_id=1, source_target_pairs={{0,1},{1,0},{2,3},{3,2},{4,5},{5,4},{6,7},{7,6},{8,9},{9,8},{10,11... | collective-permute-start | bytes 589832 | tf_op jit(solution)/shard_map/ppermute | solution.py:27
  23.4 6.9 %collective-permute-start.11 = (bf16[192,512]{1,0:T(8,128)(2,1)S(1)}, bf16[192,512]{1,0:T(8,128)(2,1)S(1)}, u32[]{:S(2)}, u32[]{:S(2)}) collective-permute-start(bf16[192,512]{1,0:T(8,128)(2,1)S(1)} %collective-permute-done.9.refs_12_.refs_15_), channel_id=1, source_target_pairs={{0,1},{1,0},{2,3},{3,2},{4,5},{5,4},{6,7},{7,6},{8,9},{9,8},{10,11... | collective-permute-start | bytes 589832 | tf_op jit(solution)/shard_map/ppermute | solution.py:27
  49.6 5.1 %collective-permute-start.12 = (bf16[2048,512]{1,0:T(8,128)(2,1)S(1)}, bf16[2048,512]{1,0:T(8,128)(2,1)S(1)}, u32[]{:S(2)}, u32[]{:S(2)}) collective-permute-start(bf16[2048,512]{1,0:T(8,128)(2,1)S(1)} %get-tuple-element.100), channel_id=1, source_target_pairs={{0,1},{1,0},{2,3},{3,2},{4,5},{5,4},{6,7},{7,6},{8,9},{9,8},{10,11... | collective-permute-start | bytes 6291464 | tf_op jit(solution)/shard_map/ppermute | solution.py:27
  55.3 21.2 %collective-permute-start.13 = (bf16[1024,512]{1,0:T(8,128)(2,1)S(1)}, bf16[1024,512]{1,0:T(8,128)(2,1)S(1)}, u32[]{:S(2)}, u32[]{:S(2)}) collective-permute-start(bf16[1024,512]{1,0:T(8,128)(2,1)S(1)} %get-tuple-element.155), channel_id=1, source_target_pairs={{0,2},{1,5},{2,0},{3,7},{4,6},{5,1},{6,4},{7,3},{8,10},{9,13},{10,... | collective-permute-start | bytes 3145736 | tf_op jit(solution)/shard_map/ppermute | solution.py:37
  71.2 7.3 %copy-start.25 = (f32[8,512]{1,0:T(8,128)S(1)}, f32[8,512]{1,0:T(8,128)}, u32[]{:S(2)}) copy-start(f32[8,512]{1,0:T(8,128)} %copy-done.24) | copy-start | bytes 49156
  76.9 9.2 %collective-permute-start.14 = (bf16[512,512]{1,0:T(8,128)(2,1)S(1)}, bf16[512,512]{1,0:T(8,128)(2,1)S(1)}, u32[]{:S(2)}, u32[]{:S(2)}) collective-permute-start(bf16[512,512]{1,0:T(8,128)(2,1)S(1)} %get-tuple-element.157), channel_id=1, source_target_pairs={{0,4},{1,9},{2,6},{3,11},{4,0},{5,13},{6,2},{7,15},{8,12},{9,1},{1... | collective-permute-start | bytes 1572872 | tf_op jit(solution)/shard_map/ppermute | solution.py:37
  86.3 7.6 %collective-permute-start.15 = (bf16[256,512]{1,0:T(8,128)(2,1)S(1)}, bf16[256,512]{1,0:T(8,128)(2,1)S(1)}, u32[]{:S(2)}, u32[]{:S(2)}) collective-permute-start(bf16[256,512]{1,0:T(8,128)(2,1)S(1)} %get-tuple-element.161), channel_id=1, source_target_pairs={{0,8},{1,3},{2,10},{3,1},{4,12},{5,7},{6,14},{7,5},{8,0},{9,11},{1... | collective-permute-start | bytes 786440 | tf_op jit(solution)/shard_map/ppermute | solution.py:37
  88.0 6.6 %collective-permute-start.18 = (bf16[2,512,128]{2,1,0:T(8,128)(2,1)S(1)}, bf16[2,512,128]{2,1,0:T(8,128)(2,1)S(1)}, u32[]{:S(2)}, u32[]{:S(2)}) collective-permute-start(bf16[2,512,128]{2,1,0:T(8,128)(2,1)S(1)} %get-tuple-element.122), channel_id=1, source_target_pairs={{0,1},{1,0},{2,3},{3,2},{4,5},{5,4},{6,7},{7,6},{8,9},{9,8},{10,11... | collective-permute-start | bytes 786440 | tf_op jit(solution)/shard_map/ppermute | solution.py:27
  90.9 13.0 %collective-permute-start.17 = (bf16[2,512,128]{2,1,0:T(8,128)(2,1)S(1)}, bf16[2,512,128]{2,1,0:T(8,128)(2,1)S(1)}, u32[]{:S(2)}, u32[]{:S(2)}) collective-permute-start(bf16[2,512,128]{2,1,0:T(8,128)(2,1)S(1)} %get-tuple-element.120), channel_id=1, source_target_pairs={{0,1},{1,0},{2,3},{3,2},{4,5},{5,4},{6,7},{7,6},{8,9},{9,8},{10,11... | collective-permute-start | bytes 786440 | tf_op jit(solution)/shard_map/ppermute | solution.py:27
  93.4 17.0 %collective-permute-start.21 = (bf16[768,512]{1,0:T(8,128)(2,1)S(1)}, bf16[768,512]{1,0:T(8,128)(2,1)S(1)}, u32[]{:S(2)}, u32[]{:S(2)}) collective-permute-start(bf16[768,512]{1,0:T(8,128)(2,1)S(1)} %get-tuple-element.129), channel_id=1, source_target_pairs={{0,1},{1,0},{2,3},{3,2},{4,5},{5,4},{6,7},{7,6},{8,9},{9,8},{10,11... | collective-permute-start | bytes 2359304 | tf_op jit(solution)/shard_map/ppermute | solution.py:27
  93.9 9.8 %collective-permute-start.16 = (bf16[128,512]{1,0:T(8,128)(2,1)S(1)}, bf16[128,512]{1,0:T(8,128)(2,1)S(1)}, u32[]{:S(2)}, u32[]{:S(2)}) collective-permute-start(bf16[128,512]{1,0:T(8,128)(2,1)S(1)} %add_convert_fusion.16), channel_id=1, source_target_pairs={{0,16},{1,17},{2,18},{3,19},{4,20},{5,21},{6,22},{7,23},{8,24},{9,... | collective-permute-start | bytes 393224 | tf_op jit(solution)/shard_map/ppermute | solution.py:37
  94.7 19.0 %copy-start.17 = (bf16[512,128]{1,0:T(8,128)(2,1)S(1)}, bf16[512,128]{1,0:T(8,128)(2,1)}, u32[]{:S(2)}) copy-start(bf16[512,128]{1,0:T(8,128)(2,1)} %refs_5_.5) | copy-start | bytes 393220
  94.7 19.0 %copy-start.23 = (bf16[512]{0:T(512)(128)(2,1)S(1)}, bf16[512]{0:T(512)(128)(2,1)}, u32[]{:S(2)}) copy-start(bf16[512]{0:T(512)(128)(2,1)} %refs_4_.5) | copy-start | bytes 3076
  94.7 19.0 %collective-permute-start.20 = (bf16[1,512,128]{2,1,0:T(8,128)(2,1)S(1)}, bf16[1,512,128]{2,1,0:T(8,128)(2,1)S(1)}, u32[]{:S(2)}, u32[]{:S(2)}) collective-permute-start(bf16[1,512,128]{2,1,0:T(8,128)(2,1)S(1)} %get-tuple-element.164), channel_id=1, source_target_pairs={{0,2},{1,3},{2,0},{3,1},{4,6},{5,7},{6,4},{7,5},{8,10},{9,11},{10,... | collective-permute-start | bytes 393224 | tf_op jit(solution)/shard_map/ppermute | solution.py:27
  103.8 6.5 %collective-permute-start.26 = (bf16[128,512]{1,0:T(8,128)(2,1)S(1)}, bf16[128,512]{1,0:T(8,128)(2,1)S(1)}, u32[]{:S(2)}, u32[]{:S(2)}) collective-permute-start(bf16[128,512]{1,0:T(8,128)(2,1)S(1)} %add_convert_fusion.10), channel_id=1, source_target_pairs={{0,16},{1,17},{2,18},{3,19},{4,20},{5,21},{6,22},{7,23},{8,24},{9,... | collective-permute-start | bytes 393224 | tf_op jit(solution)/shard_map/ppermute | solution.py:37
  104.0 9.7 %collective-permute-start.19 = (bf16[1,512,128]{2,1,0:T(8,128)(2,1)S(1)}, bf16[1,512,128]{2,1,0:T(8,128)(2,1)S(1)}, u32[]{:S(2)}, u32[]{:S(2)}) collective-permute-start(bf16[1,512,128]{2,1,0:T(8,128)(2,1)S(1)} %get-tuple-element.166), channel_id=1, source_target_pairs={{0,2},{1,3},{2,0},{3,1},{4,6},{5,7},{6,4},{7,5},{8,10},{9,11},{10,... | collective-permute-start | bytes 393224 | tf_op jit(solution)/shard_map/ppermute | solution.py:27
  110.3 7.4 %collective-permute-start.27 = (bf16[256,512]{1,0:T(8,128)(2,1)S(1)}, bf16[256,512]{1,0:T(8,128)(2,1)S(1)}, u32[]{:S(2)}, u32[]{:S(2)}) collective-permute-start(bf16[256,512]{1,0:T(8,128)(2,1)S(1)} %pad_maximum_fusion.4), channel_id=1, source_target_pairs={{0,8},{1,3},{2,10},{3,1},{4,12},{5,7},{6,14},{7,5},{8,0},{9,11},{1... | collective-permute-start | bytes 786440 | tf_op jit(solution)/shard_map/ppermute | solution.py:37
  110.6 9.6 %collective-permute-start.22 = (bf16[384,512]{1,0:T(8,128)(2,1)S(1)}, bf16[384,512]{1,0:T(8,128)(2,1)S(1)}, u32[]{:S(2)}, u32[]{:S(2)}) collective-permute-start(bf16[384,512]{1,0:T(8,128)(2,1)S(1)} %get-tuple-element.159), channel_id=1, source_target_pairs={{0,2},{1,5},{2,0},{3,7},{4,6},{5,1},{6,4},{7,3},{8,10},{9,13},{10,... | collective-permute-start | bytes 1179656 | tf_op jit(solution)/shard_map/ppermute | solution.py:37
  117.7 1.3 collective-permute-start.23
  117.7 9.2 %collective-permute-start.28 = (bf16[512,512]{1,0:T(8,128)(2,1)S(1)}, bf16[512,512]{1,0:T(8,128)(2,1)S(1)}, u32[]{:S(2)}, u32[]{:S(2)}) collective-permute-start(bf16[512,512]{1,0:T(8,128)(2,1)S(1)} %pad_maximum_fusion.1), channel_id=1, source_target_pairs={{0,4},{1,9},{2,6},{3,11},{4,0},{5,13},{6,2},{7,15},{8,12},{9,1},{1... | collective-permute-start | bytes 1572872 | tf_op jit(solution)/shard_map/ppermute | solution.py:37
  120.4 9.8 %collective-permute-start.24 = (bf16[272,512]{1,0:T(8,128)(2,1)S(1)}, bf16[272,512]{1,0:T(8,128)(2,1)S(1)}, u32[]{:S(2)}, u32[]{:S(2)}) collective-permute-start(bf16[272,512]{1,0:T(8,128)(2,1)S(1)} %pad_maximum_fusion.3), channel_id=1, source_target_pairs={{0,4},{1,9},{2,6},{3,11},{4,0},{5,13},{6,2},{7,15},{8,12},{9,1},{1... | collective-permute-start | bytes 835592 | tf_op jit(solution)/shard_map/ppermute | solution.py:37
  127.0 19.0 %collective-permute-start.29 = (bf16[1024,512]{1,0:T(8,128)(2,1)S(1)}, bf16[1024,512]{1,0:T(8,128)(2,1)S(1)}, u32[]{:S(2)}, u32[]{:S(2)}) collective-permute-start(bf16[1024,512]{1,0:T(8,128)(2,1)S(1)} %pad_maximum_fusion.own), channel_id=1, source_target_pairs={{0,2},{1,5},{2,0},{3,7},{4,6},{5,1},{6,4},{7,3},{8,10},{9,13},{10,... | collective-permute-start | bytes 3145736 | tf_op jit(solution)/shard_map/ppermute | solution.py:37
  130.3 5.8 %collective-permute-start.25 = (bf16[176,512]{1,0:T(8,128)(2,1)S(1)}, bf16[176,512]{1,0:T(8,128)(2,1)S(1)}, u32[]{:S(2)}, u32[]{:S(2)}) collective-permute-start(bf16[176,512]{1,0:T(8,128)(2,1)S(1)} %pad_maximum_fusion.6), channel_id=1, source_target_pairs={{0,8},{1,3},{2,10},{3,1},{4,12},{5,7},{6,14},{7,5},{8,0},{9,11},{1... | collective-permute-start | bytes 540680 | tf_op jit(solution)/shard_map/ppermute | solution.py:37
  132.6 15.2 %collective-permute-start.32 = (bf16[1024,512]{1,0:T(8,128)(2,1)S(1)}, bf16[1024,512]{1,0:T(8,128)(2,1)S(1)}, u32[]{:S(2)}, u32[]{:S(2)}) collective-permute-start(bf16[1024,512]{1,0:T(8,128)(2,1)S(1)} %pad_maximum_fusion.own), channel_id=1, source_target_pairs={{0,1},{1,0},{2,3},{3,2},{4,5},{5,4},{6,7},{7,6},{8,9},{9,8},{10,11... | collective-permute-start | bytes 3145736 | tf_op jit(solution)/shard_map/ppermute | solution.py:27
  136.2 9.9 %collective-permute-start.30 = (bf16[128,512]{1,0:T(8,128)(2,1)S(1)}, bf16[128,512]{1,0:T(8,128)(2,1)S(1)}, u32[]{:S(2)}, u32[]{:S(2)}) collective-permute-start(bf16[128,512]{1,0:T(8,128)(2,1)S(1)} %pad_maximum_fusion.7), channel_id=1, source_target_pairs={{0,16},{1,17},{2,18},{3,19},{4,20},{5,21},{6,22},{7,23},{8,24},{9,... | collective-permute-start | bytes 393224 | tf_op jit(solution)/shard_map/ppermute | solution.py:37
  146.7 12.0 %collective-permute-start.35 = (bf16[1024,512]{1,0:T(8,128)(2,1)S(1)}, bf16[1024,512]{1,0:T(8,128)(2,1)}, u32[]{:S(2)}, u32[]{:S(2)}) collective-permute-start(bf16[1024,512]{1,0:T(8,128)(2,1)S(1)} %collective-permute-done.29.own), channel_id=1, source_target_pairs={{0,1},{1,0},{2,3},{3,2},{4,5},{5,4},{6,7},{7,6},{8,9},{9,8},{10,11... | collective-permute-start | bytes 3145736 | tf_op jit(solution)/shard_map/ppermute | solution.py:27
  146.7 7.3 %copy-start.28 = (bf16[128,512]{1,0:T(8,128)(2,1)S(1)}, bf16[128,512]{1,0:T(8,128)(2,1)}, u32[]{:S(2)}) copy-start(bf16[128,512]{1,0:T(8,128)(2,1)} %copy-done.27) | copy-start | bytes 393220
  147.6 5.9 %collective-permute-start.31 = (bf16[48,512]{1,0:T(8,128)(2,1)S(1)}, bf16[48,512]{1,0:T(8,128)(2,1)S(1)}, u32[]{:S(2)}, u32[]{:S(2)}) collective-permute-start(bf16[48,512]{1,0:T(8,128)(2,1)S(1)} %add_convert_fusion.24), channel_id=1, source_target_pairs={{0,16},{4,20},{8,24},{12,28},{16,0},{20,4},{24,8},{28,12},{1,17},{... | collective-permute-start | bytes 147464 | tf_op jit(solution)/shard_map/ppermute | solution.py:27
  153.5 4.8 %collective-permute-start.33 = (bf16[96,512]{1,0:T(8,128)(2,1)S(1)}, bf16[96,512]{1,0:T(8,128)(2,1)S(1)}, u32[]{:S(2)}, u32[]{:S(2)}) collective-permute-start(bf16[96,512]{1,0:T(8,128)(2,1)S(1)} %pad_maximum_fusion.8), channel_id=1, source_target_pairs={{0,8},{4,12},{8,0},{12,4},{16,24},{20,28},{24,16},{28,20},{1,9},{5... | collective-permute-start | bytes 294920 | tf_op jit(solution)/shard_map/ppermute | solution.py:27
  154.0 4.5 %collective-permute-start.36 = (bf16[80,512]{1,0:T(8,128)(2,1)S(1)}, bf16[80,512]{1,0:T(8,128)(2,1)S(1)}, u32[]{:S(2)}, u32[]{:S(2)}) collective-permute-start(bf16[80,512]{1,0:T(8,128)(2,1)S(1)} %add_convert_fusion.20), channel_id=1, source_target_pairs={{0,2},{1,5},{2,0},{3,7},{4,6},{5,1},{6,4},{7,3},{8,10},{9,13},{10,... | collective-permute-start | bytes 245768 | tf_op jit(solution)/shard_map/ppermute | solution.py:37
  158.4 6.1 %collective-permute-start.34 = (bf16[192,512]{1,0:T(8,128)(2,1)S(1)}, bf16[192,512]{1,0:T(8,128)(2,1)S(1)}, u32[]{:S(2)}, u32[]{:S(2)}) collective-permute-start(bf16[192,512]{1,0:T(8,128)(2,1)S(1)} %pad_maximum_fusion.5), channel_id=1, source_target_pairs={{0,4},{4,0},{8,12},{12,8},{16,20},{20,16},{24,28},{28,24},{1,5},{5... | collective-permute-start | bytes 589832 | tf_op jit(solution)/shard_map/ppermute | solution.py:27
  158.6 5.9 %collective-permute-start.37 = (bf16[80,512]{1,0:T(8,128)(2,1)S(1)}, bf16[80,512]{1,0:T(8,128)(2,1)S(1)}, u32[]{:S(2)}, u32[]{:S(2)}) collective-permute-start(bf16[80,512]{1,0:T(8,128)(2,1)S(1)} %add_convert_fusion.19.own), channel_id=1, source_target_pairs={{0,1},{1,0},{2,3},{3,2},{4,5},{5,4},{6,7},{7,6},{8,9},{9,8},{10,11... | collective-permute-start | bytes 245768 | tf_op jit(solution)/shard_map/ppermute | solution.py:27
  (28 other events, 93.5 us)
